TPU v7x, 32 devices: a whole 2x2x4 slice. The times are simulated.
32 devices in a mesh: tm: 4 (over y, x), sx: 2 (over core), sy: 4 (over z).
Axes of the slice: x: 2, y: 2, z: 4, core: 2. Of those that a mesh axis runs over, the one named last changes fastest.
Arguments:
- initial: float32 [512, 2048], P('sx', 'sy'), may hold values from 0.5 to 1.5
- kappa: float32 [512, 2048], P('sx', 'sy'), may hold values from 0.0016 to 0.016
- c_guess: float32 [4, 512, 2048], P('tm', 'sx', 'sy'), may hold values from 0.5 to 1.5
Outputs:
- c_values: float32 [4, 512, 2048], P('tm', 'sx', 'sy')
- f_values: float32 [4, 512, 2048], P('tm', 'sx', 'sy')
All inputs are finite; a program needn't handle non-finite values.
Results may differ from a plain program's by a relative error of at most 0.00002.
Values sent between devices are 32-bit elements; how exact they have to be, the bound alone decides.
No kernel may reach another device: no remote copies, remote signals or barrier semaphores. Data moves between devices by JAX's collectives and lax.ppermute only.
A program may use at most 64 MiB of HBM per device.

v0:
```python
import jax
import jax.numpy as jnp
from jax import lax
from jax.sharding import PartitionSpec as P


def with_halo(x, sides, width):
    for axis, dim in sides:
        size, length = (lax.axis_size(axis), x.shape[dim])
        up = [(i, (i + 1) % size) for i in range(size - 1)]
        down = [(j, i) for i, j in up]
        last = lax.slice_in_dim(x, length - width, length, axis=dim)
        leading = lax.slice_in_dim(x, 0, width, axis=dim)
        before = lax.ppermute(last, axis, up)
        after = lax.ppermute(leading, axis, down)
        x = jnp.concatenate([before, x, after], axis=dim)
    return x


def shifted(x, axis, by):
    length = lax.axis_size(axis)
    pairs = [(i, i + by) for i in range(length) if 0 <= i + by < length]
    return lax.ppermute(x, axis, pairs)


def on_device(initial, kappa, c_guess):
    index = lax.axis_index("tm")
    count = lax.axis_size("tm")
    first = index == 0
    is_odd = index % 2 == 1

    def spread(field):
        flux = kappa * field * field
        padded = with_halo(flux, (("sx", 0), ("sy", 1)), 1)
        return (
            padded[2:, 1:-1] + padded[:-2, 1:-1] + padded[1:-1, 2:] + padded[1:-1, :-2] - 4.0 * flux
        )

    def earlier(stack, keep):
        moved = shifted(stack, "tm", 1)
        head = moved[0]
        if keep:
            head = jnp.where(first, initial, head)
        head_lap = spread(head)
        others = moved[1:]
        return (head, head_lap, others)

    guess = c_guess[0]
    prev_w, lap_w, unused = earlier(guess[None], True)
    fine = prev_w + lap_w
    lap_f = spread(fine)
    value = fine + lap_f
    first_rhs = value - prev_w - 2.0 * lap_w
    quarter = prev_w + 4.0 * lap_w
    value_prev, lap_v, others = earlier(jnp.stack([value, quarter]), False)
    second_rhs = jnp.where(is_odd, value_prev + 2.0 * lap_v + first_rhs - others[0], 0.0)
    steps = count // 2
    every = lax.all_gather(second_rhs[None], "tm", axis=0, tiled=True)
    target = (index + 1) // 2
    state = initial
    chosen = initial
    chosen_lap = jnp.zeros_like(initial)
    for level_index in range(steps):
        state_lap = spread(state)
        chosen = jnp.where(target == level_index, state, chosen)
        chosen_lap = jnp.where(target == level_index, state_lap, chosen_lap)
        state = state + 4.0 * state_lap + every[2 * level_index + 1]
    chosen = jnp.where(target == steps, state, chosen)
    new_c = jnp.where(is_odd, chosen, chosen + 2.0 * chosen_lap + first_rhs)
    prev_n, lap_n, unused = earlier(new_c[None], True)
    f_out = prev_n + lap_n
    return (new_c[None], f_out[None])


def solution(mesh):
    return jax.shard_map(
        on_device,
        mesh=mesh,
        in_specs=(P("sx", "sy"), P("sx", "sy"), P("tm", "sx", "sy")),
        out_specs=(P("tm", "sx", "sy"), P("tm", "sx", "sy")),
        check_vma=False,
    )
```

profile of v0, /device:TPU:14, one launch (start us, length us, event | category | flops | bytes accessed | tf_op | source)
XLA Modules:
  0.0 199.9 jit_solution(12286385694902027704)
XLA Ops:
  8.7 14.5 %collective-permute-done.4 = f32[1,256,512]{2,1,0:T(8,128)S(1)} collective-permute-done((f32[1,256,512]{2,1,0:T(8,128)}, f32[1,256,512]{2,1,0:T(8,128)S(1)}, u32[]{:S(2)}, u32[]{:S(2)}) %collective-permute-start.4) | collective-permute-done | bytes 524320 | tf_op jit(solution)/shard_map/ppermute | solution.py:23
  25.8 3.0 %collective-permute-start.6 = (f32[1,512]{1,0:T(1,128)S(1)}, f32[1,512]{1,0:T(1,128)S(1)}, u32[]{:S(2)}, u32[]{:S(2)}) collective-permute-start(f32[1,512]{1,0:T(1,128)S(1)} %get-tuple-element.27), channel_id=1, source_target_pairs={{0,4},{1,5},{2,6},{3,7},{8,12},{9,13},{10,14},{11,15},{16,20},{17,... | collective-permute-start | bytes 6152 | tf_op jit(solution)/shard_map/ppermute | solution.py:14
  29.8 2.4 %collective-permute-start.7 = (f32[258,1]{1,0:T(8,128)S(1)}, f32[258,1]{1,0:T(8,128)S(1)}, u32[]{:S(2)}, u32[]{:S(2)}) collective-permute-start(f32[258,1]{1,0:T(8,128)S(1)} %get-tuple-element.15), channel_id=1, source_target_pairs={{1,0},{2,1},{3,2},{5,4},{6,5},{7,6},{9,8},{10,9},{11,10},{13,12},{... | collective-permute-start | bytes 3104 | tf_op jit(solution)/shard_map/ppermute | solution.py:15
  32.2 3.5 %collective-permute-start.8 = (f32[258,1]{1,0:T(8,128)S(1)}, f32[258,1]{1,0:T(8,128)S(1)}, u32[]{:S(2)}, u32[]{:S(2)}) collective-permute-start(f32[258,1]{1,0:T(8,128)S(1)} %get-tuple-element.16), channel_id=1, source_target_pairs={{0,1},{1,2},{2,3},{4,5},{5,6},{6,7},{8,9},{9,10},{10,11},{12,13},{... | collective-permute-start | bytes 3104 | tf_op jit(solution)/shard_map/ppermute | solution.py:14
  37.5 2.1 %collective-permute-done.8 = f32[258,1]{1,0:T(8,128)S(1)} collective-permute-done((f32[258,1]{1,0:T(8,128)S(1)}, f32[258,1]{1,0:T(8,128)S(1)}, u32[]{:S(2)}, u32[]{:S(2)}) %collective-permute-start.8) | collective-permute-done | bytes 1064 | tf_op jit(solution)/shard_map/ppermute | solution.py:14
  46.4 3.9 %collective-permute-start.12 = (f32[258,1]{1,0:T(8,128)S(1)}, f32[258,1]{1,0:T(8,128)S(1)}, u32[]{:S(2)}, u32[]{:S(2)}) collective-permute-start(f32[258,1]{1,0:T(8,128)S(1)} %get-tuple-element.14), channel_id=1, source_target_pairs={{0,1},{1,2},{2,3},{4,5},{5,6},{6,7},{8,9},{9,10},{10,11},{12,13},{... | collective-permute-start | bytes 3104 | tf_op jit(solution)/shard_map/ppermute | solution.py:14
  56.1 25.0 %collective-permute-done.13 = f32[2,256,512]{2,1,0:T(8,128)S(1)} collective-permute-done((f32[2,256,512]{2,1,0:T(8,128)S(1)}, f32[2,256,512]{2,1,0:T(8,128)S(1)}, u32[]{:S(2)}, u32[]{:S(2)}) %collective-permute-start.13) | collective-permute-done | bytes 1048608 | tf_op jit(solution)/shard_map/ppermute | solution.py:23
  83.6 3.0 %collective-permute-start.15 = (f32[1,512]{1,0:T(1,128)S(1)}, f32[1,512]{1,0:T(1,128)S(1)}, u32[]{:S(2)}, u32[]{:S(2)}) collective-permute-start(f32[1,512]{1,0:T(1,128)S(1)} %get-tuple-element.23), channel_id=1, source_target_pairs={{0,4},{1,5},{2,6},{3,7},{8,12},{9,13},{10,14},{11,15},{16,20},{17,... | collective-permute-start | bytes 6152 | tf_op jit(solution)/shard_map/ppermute | solution.py:14
  90.0 3.9 %collective-permute-start.17 = (f32[258,1]{1,0:T(8,128)S(1)}, f32[258,1]{1,0:T(8,128)}, u32[]{:S(2)}, u32[]{:S(2)}) collective-permute-start(f32[258,1]{1,0:T(8,128)S(1)} %get-tuple-element.12), channel_id=1, source_target_pairs={{0,1},{1,2},{2,3},{4,5},{5,6},{6,7},{8,9},{9,10},{10,11},{12,13},{... | collective-permute-start | bytes 3104 | tf_op jit(solution)/shard_map/ppermute | solution.py:14
  94.0 2.1 %collective-permute-done.16 = f32[258,1]{1,0:T(8,128)} collective-permute-done((f32[258,1]{1,0:T(8,128)}, f32[258,1]{1,0:T(8,128)}, u32[]{:S(2)}, u32[]{:S(2)}) %collective-permute-start.16) | collective-permute-done | bytes 1064 | tf_op jit(solution)/shard_map/ppermute | solution.py:15
  97.9 4.0 %fusion.12 = f32[256,512]{1,0:T(8,128)} fusion(f32[2,256,512]{2,1,0:T(8,128)} %copy-done.4, f32[258,1]{1,0:T(8,128)} %collective-permute-done.17, f32[1,512]{1,0:T(1,128)} %copy-done.11, f32[256,512]{1,0:T(8,128)} %copy-done.2, f32[1,512]{1,0:T(1,128)} %copy-done.12, f32[258,1]{1,0:T(8,128)} %collective-permute-done.16, pred[]{:T(512)S(6)} %eq.19, ...), kind=kLoop, calls=%fused_computation.38 | loop fusion | flops 4456448 | bytes 3682337 | tf_op jit(solution)/shard_map/jit(_where)/select_n | solution.py:56
  103.2 3.0 %collective-permute-start.1 = (f32[1,512]{1,0:T(1,128)S(1)}, f32[1,512]{1,0:T(1,128)S(1)}, u32[]{:S(2)}, u32[]{:S(2)}) collective-permute-start(f32[1,512]{1,0:T(1,128)S(1)} %get-tuple-element.21), channel_id=1, source_target_pairs={{0,4},{1,5},{2,6},{3,7},{8,12},{9,13},{10,14},{11,15},{16,20},{17,... | collective-permute-start | bytes 6152 | tf_op jit(solution)/shard_map/ppermute | solution.py:14
  109.1 3.9 %collective-permute-start.3 = (f32[258,1]{1,0:T(8,128)S(1)}, f32[258,1]{1,0:T(8,128)}, u32[]{:S(2)}, u32[]{:S(2)}) collective-permute-start(f32[258,1]{1,0:T(8,128)S(1)} %get-tuple-element.10), channel_id=1, source_target_pairs={{0,1},{1,2},{2,3},{4,5},{5,6},{6,7},{8,9},{9,10},{10,11},{12,13},{... | collective-permute-start | bytes 3104 | tf_op jit(solution)/shard_map/ppermute | solution.py:14
  114.9 2.0 %collective-permute-done.3 = f32[258,1]{1,0:T(8,128)} collective-permute-done((f32[258,1]{1,0:T(8,128)S(1)}, f32[258,1]{1,0:T(8,128)}, u32[]{:S(2)}, u32[]{:S(2)}) %collective-permute-start.3) | collective-permute-done | bytes 1064 | tf_op jit(solution)/shard_map/ppermute | solution.py:14
  116.9 22.1 %all-gather.3.cloned.1.call-done = f32[1024,512]{1,0:T(8,128)} async-done(((f32[256,512]{1,0:T(8,128)}), f32[1024,512]{1,0:T(8,128)}) %all-gather.3.cloned.1.call-update) | async-done | bytes 2097168 | tf_op jit(solution)/shard_map/all_gather | solution.py:58
  141.9 3.0 %collective-permute-start.19 = (f32[1,512]{1,0:T(1,128)S(1)}, f32[1,512]{1,0:T(1,128)S(1)}, u32[]{:S(2)}, u32[]{:S(2)}) collective-permute-start(f32[1,512]{1,0:T(1,128)S(1)} %get-tuple-element.19), channel_id=1, source_target_pairs={{0,4},{1,5},{2,6},{3,7},{8,12},{9,13},{10,14},{11,15},{16,20},{17,... | collective-permute-start | bytes 6152 | tf_op jit(solution)/shard_map/ppermute | solution.py:14
  146.5 2.4 %collective-permute-start.20 = (f32[258,1]{1,0:T(8,128)}, f32[258,1]{1,0:T(8,128)}, u32[]{:S(2)}, u32[]{:S(2)}) collective-permute-start(f32[258,1]{1,0:T(8,128)} %get-tuple-element.7), channel_id=1, source_target_pairs={{1,0},{2,1},{3,2},{5,4},{6,5},{7,6},{9,8},{10,9},{11,10},{13,12},{... | collective-permute-start | bytes 3104 | tf_op jit(solution)/shard_map/ppermute | solution.py:15
  149.0 3.4 %collective-permute-start.21 = (f32[258,1]{1,0:T(8,128)}, f32[258,1]{1,0:T(8,128)}, u32[]{:S(2)}, u32[]{:S(2)}) collective-permute-start(f32[258,1]{1,0:T(8,128)} %get-tuple-element.8), channel_id=1, source_target_pairs={{0,1},{1,2},{2,3},{4,5},{5,6},{6,7},{8,9},{9,10},{10,11},{12,13},{... | collective-permute-start | bytes 3104 | tf_op jit(solution)/shard_map/ppermute | solution.py:14
  152.4 2.2 %collective-permute-done.20 = f32[258,1]{1,0:T(8,128)} collective-permute-done((f32[258,1]{1,0:T(8,128)}, f32[258,1]{1,0:T(8,128)}, u32[]{:S(2)}, u32[]{:S(2)}) %collective-permute-start.20) | collective-permute-done | bytes 1064 | tf_op jit(solution)/shard_map/ppermute | solution.py:15
  154.6 2.2 %collective-permute-done.21 = f32[258,1]{1,0:T(8,128)} collective-permute-done((f32[258,1]{1,0:T(8,128)}, f32[258,1]{1,0:T(8,128)}, u32[]{:S(2)}, u32[]{:S(2)}) %collective-permute-start.21) | collective-permute-done | bytes 1064 | tf_op jit(solution)/shard_map/ppermute | solution.py:14
  156.7 5.1 %select_bitcast_fusion = f32[1,256,512]{2,1,0:T(8,128)S(1)} fusion(f32[1024,512]{1,0:T(8,128)} %all-gather.3.cloned.1.call-done, f32[256,512]{1,0:T(8,128)S(1)} %copy-done.1, f32[1,512]{1,0:T(1,128)} %copy-done.9, f32[256,512]{1,0:T(8,128)} %copy-done.3, f32[1,512]{1,0:T(1,128)} %copy-done.10, f32[258,1]{1,0:T(8,128)} %collective-permute-done.21, ...), kind=kLoop, calls=%fused_computation.94 | loop fusion | flops 7340032 | bytes 4737076 | tf_op jit(solution)/shard_map/broadcast_in_dim | solution.py:72
  163.1 13.6 %collective-permute-done.22 = f32[1,256,512]{2,1,0:T(8,128)S(1)} collective-permute-done((f32[1,256,512]{2,1,0:T(8,128)S(1)}, f32[1,256,512]{2,1,0:T(8,128)S(1)}, u32[]{:S(2)}, u32[]{:S(2)}) %collective-permute-start.22) | collective-permute-done | bytes 524320 | tf_op jit(solution)/shard_map/ppermute | solution.py:23
  178.2 3.0 %collective-permute-start.24 = (f32[1,512]{1,0:T(1,128)S(1)}, f32[1,512]{1,0:T(1,128)S(1)}, u32[]{:S(2)}, u32[]{:S(2)}) collective-permute-start(f32[1,512]{1,0:T(1,128)S(1)} %get-tuple-element.17), channel_id=1, source_target_pairs={{0,4},{1,5},{2,6},{3,7},{8,12},{9,13},{10,14},{11,15},{16,20},{17,... | collective-permute-start | bytes 6152 | tf_op jit(solution)/shard_map/ppermute | solution.py:14
  184.1 3.9 %collective-permute-start.26 = (f32[258,1]{1,0:T(8,128)S(1)}, f32[258,1]{1,0:T(8,128)S(1)}, u32[]{:S(2)}, u32[]{:S(2)}) collective-permute-start(f32[258,1]{1,0:T(8,128)S(1)} %get-tuple-element.6), channel_id=1, source_target_pairs={{0,1},{1,2},{2,3},{4,5},{5,6},{6,7},{8,9},{9,10},{10,11},{12,13},{... | collective-permute-start | bytes 3104 | tf_op jit(solution)/shard_map/ppermute | solution.py:14
  (82 shorter events, 47.9 us)
Async XLA Ops:
  7.2 131.9 %all-gather.3.cloned.1.call-start = ((), (), s32[]{:S(2)}) async-start(), calls=%async_computation | async-start | bytes 2621440 | tf_op jit(solution)/shard_map/all_gather | solution.py:58
  7.2 15.9 %collective-permute-start.4 = (f32[1,256,512]{2,1,0:T(8,128)}, f32[1,256,512]{2,1,0:T(8,128)S(1)}, u32[]{:S(2)}, u32[]{:S(2)}) collective-permute-start(f32[1,256,512]{2,1,0:T(8,128)} %param.5), channel_id=1, source_target_pairs={{0,8},{8,16},{16,24},{1,9},{9,17},{17,25},{2,10},{10,18},{18,26},{... | collective-permute-start | bytes 1572872 | tf_op jit(solution)/shard_map/ppermute | solution.py:23
  24.5 4.3 %collective-permute-start.5 = (f32[1,512]{1,0:T(1,128)S(1)}, f32[1,512]{1,0:T(1,128)S(1)}, u32[]{:S(2)}, u32[]{:S(2)}) collective-permute-start(f32[1,512]{1,0:T(1,128)S(1)} %get-tuple-element.28), channel_id=1, source_target_pairs={{4,0},{5,1},{6,2},{7,3},{12,8},{13,9},{14,10},{15,11},{20,16},{21,... | collective-permute-start | bytes 6152 | tf_op jit(solution)/shard_map/ppermute | solution.py:15
  25.8 3.8 %collective-permute-start.6 = (f32[1,512]{1,0:T(1,128)S(1)}, f32[1,512]{1,0:T(1,128)S(1)}, u32[]{:S(2)}, u32[]{:S(2)}) collective-permute-start(f32[1,512]{1,0:T(1,128)S(1)} %get-tuple-element.27), channel_id=1, source_target_pairs={{0,4},{1,5},{2,6},{3,7},{8,12},{9,13},{10,14},{11,15},{16,20},{17,... | collective-permute-start | bytes 6152 | tf_op jit(solution)/shard_map/ppermute | solution.py:14
  29.8 7.7 %collective-permute-start.7 = (f32[258,1]{1,0:T(8,128)S(1)}, f32[258,1]{1,0:T(8,128)S(1)}, u32[]{:S(2)}, u32[]{:S(2)}) collective-permute-start(f32[258,1]{1,0:T(8,128)S(1)} %get-tuple-element.15), channel_id=1, source_target_pairs={{1,0},{2,1},{3,2},{5,4},{6,5},{7,6},{9,8},{10,9},{11,10},{13,12},{... | collective-permute-start | bytes 3104 | tf_op jit(solution)/shard_map/ppermute | solution.py:15
  32.2 7.4 %collective-permute-start.8 = (f32[258,1]{1,0:T(8,128)S(1)}, f32[258,1]{1,0:T(8,128)S(1)}, u32[]{:S(2)}, u32[]{:S(2)}) collective-permute-start(f32[258,1]{1,0:T(8,128)S(1)} %get-tuple-element.16), channel_id=1, source_target_pairs={{0,1},{1,2},{2,3},{4,5},{5,6},{6,7},{8,9},{9,10},{10,11},{12,13},{... | collective-permute-start | bytes 3104 | tf_op jit(solution)/shard_map/ppermute | solution.py:14
  44.5 7.6 %collective-permute-start.11 = (f32[258,1]{1,0:T(8,128)S(1)}, f32[258,1]{1,0:T(8,128)S(1)}, u32[]{:S(2)}, u32[]{:S(2)}) collective-permute-start(f32[258,1]{1,0:T(8,128)S(1)} %get-tuple-element.13), channel_id=1, source_target_pairs={{1,0},{2,1},{3,2},{5,4},{6,5},{7,6},{9,8},{10,9},{11,10},{13,12},{... | collective-permute-start | bytes 3104 | tf_op jit(solution)/shard_map/ppermute | solution.py:15
  46.4 7.6 %collective-permute-start.12 = (f32[258,1]{1,0:T(8,128)S(1)}, f32[258,1]{1,0:T(8,128)S(1)}, u32[]{:S(2)}, u32[]{:S(2)}) collective-permute-start(f32[258,1]{1,0:T(8,128)S(1)} %get-tuple-element.14), channel_id=1, source_target_pairs={{0,1},{1,2},{2,3},{4,5},{5,6},{6,7},{8,9},{9,10},{10,11},{12,13},{... | collective-permute-start | bytes 3104 | tf_op jit(solution)/shard_map/ppermute | solution.py:14
  54.8 26.3 %collective-permute-start.13 = (f32[2,256,512]{2,1,0:T(8,128)S(1)}, f32[2,256,512]{2,1,0:T(8,128)S(1)}, u32[]{:S(2)}, u32[]{:S(2)}) collective-permute-start(f32[2,256,512]{2,1,0:T(8,128)S(1)} %pad_maximum_fusion), channel_id=1, source_target_pairs={{0,8},{8,16},{16,24},{1,9},{9,17},{17,25},{2,10},{10,18},{18,26},{... | collective-permute-start | bytes 3145736 | tf_op jit(solution)/shard_map/ppermute | solution.py:23
  82.3 4.3 %collective-permute-start.14 = (f32[1,512]{1,0:T(1,128)S(1)}, f32[1,512]{1,0:T(1,128)S(1)}, u32[]{:S(2)}, u32[]{:S(2)}) collective-permute-start(f32[1,512]{1,0:T(1,128)S(1)} %get-tuple-element.24), channel_id=1, source_target_pairs={{4,0},{5,1},{6,2},{7,3},{12,8},{13,9},{14,10},{15,11},{20,16},{21,... | collective-permute-start | bytes 6152 | tf_op jit(solution)/shard_map/ppermute | solution.py:15
  83.6 3.8 %collective-permute-start.15 = (f32[1,512]{1,0:T(1,128)S(1)}, f32[1,512]{1,0:T(1,128)S(1)}, u32[]{:S(2)}, u32[]{:S(2)}) collective-permute-start(f32[1,512]{1,0:T(1,128)S(1)} %get-tuple-element.23), channel_id=1, source_target_pairs={{0,4},{1,5},{2,6},{3,7},{8,12},{9,13},{10,14},{11,15},{16,20},{17,... | collective-permute-start | bytes 6152 | tf_op jit(solution)/shard_map/ppermute | solution.py:14
  88.1 8.0 %collective-permute-start.16 = (f32[258,1]{1,0:T(8,128)}, f32[258,1]{1,0:T(8,128)}, u32[]{:S(2)}, u32[]{:S(2)}) collective-permute-start(f32[258,1]{1,0:T(8,128)} %get-tuple-element.11), channel_id=1, source_target_pairs={{1,0},{2,1},{3,2},{5,4},{6,5},{7,6},{9,8},{10,9},{11,10},{13,12},{... | collective-permute-start | bytes 3104 | tf_op jit(solution)/shard_map/ppermute | solution.py:15
  90.0 7.8 %collective-permute-start.17 = (f32[258,1]{1,0:T(8,128)S(1)}, f32[258,1]{1,0:T(8,128)}, u32[]{:S(2)}, u32[]{:S(2)}) collective-permute-start(f32[258,1]{1,0:T(8,128)S(1)} %get-tuple-element.12), channel_id=1, source_target_pairs={{0,1},{1,2},{2,3},{4,5},{5,6},{6,7},{8,9},{9,10},{10,11},{12,13},{... | collective-permute-start | bytes 3104 | tf_op jit(solution)/shard_map/ppermute | solution.py:14
  101.9 4.3 %collective-permute-start = (f32[1,512]{1,0:T(1,128)S(1)}, f32[1,512]{1,0:T(1,128)S(1)}, u32[]{:S(2)}, u32[]{:S(2)}) collective-permute-start(f32[1,512]{1,0:T(1,128)S(1)} %get-tuple-element.22), channel_id=1, source_target_pairs={{4,0},{5,1},{6,2},{7,3},{12,8},{13,9},{14,10},{15,11},{20,16},{21,... | collective-permute-start | bytes 6152 | tf_op jit(solution)/shard_map/ppermute | solution.py:15
  103.2 3.8 %collective-permute-start.1 = (f32[1,512]{1,0:T(1,128)S(1)}, f32[1,512]{1,0:T(1,128)S(1)}, u32[]{:S(2)}, u32[]{:S(2)}) collective-permute-start(f32[1,512]{1,0:T(1,128)S(1)} %get-tuple-element.21), channel_id=1, source_target_pairs={{0,4},{1,5},{2,6},{3,7},{8,12},{9,13},{10,14},{11,15},{16,20},{17,... | collective-permute-start | bytes 6152 | tf_op jit(solution)/shard_map/ppermute | solution.py:14
  107.2 7.7 %collective-permute-start.2 = (f32[258,1]{1,0:T(8,128)S(1)}, f32[258,1]{1,0:T(8,128)S(1)}, u32[]{:S(2)}, u32[]{:S(2)}) collective-permute-start(f32[258,1]{1,0:T(8,128)S(1)} %get-tuple-element.9), channel_id=1, source_target_pairs={{1,0},{2,1},{3,2},{5,4},{6,5},{7,6},{9,8},{10,9},{11,10},{13,12},{... | collective-permute-start | bytes 3104 | tf_op jit(solution)/shard_map/ppermute | solution.py:15
  109.1 7.8 %collective-permute-start.3 = (f32[258,1]{1,0:T(8,128)S(1)}, f32[258,1]{1,0:T(8,128)}, u32[]{:S(2)}, u32[]{:S(2)}) collective-permute-start(f32[258,1]{1,0:T(8,128)S(1)} %get-tuple-element.10), channel_id=1, source_target_pairs={{0,1},{1,2},{2,3},{4,5},{5,6},{6,7},{8,9},{9,10},{10,11},{12,13},{... | collective-permute-start | bytes 3104 | tf_op jit(solution)/shard_map/ppermute | solution.py:14
  140.6 4.3 %collective-permute-start.18 = (f32[1,512]{1,0:T(1,128)S(1)}, f32[1,512]{1,0:T(1,128)S(1)}, u32[]{:S(2)}, u32[]{:S(2)}) collective-permute-start(f32[1,512]{1,0:T(1,128)S(1)} %get-tuple-element.20), channel_id=1, source_target_pairs={{4,0},{5,1},{6,2},{7,3},{12,8},{13,9},{14,10},{15,11},{20,16},{21,... | collective-permute-start | bytes 6152 | tf_op jit(solution)/shard_map/ppermute | solution.py:15
  146.5 8.0 %collective-permute-start.20 = (f32[258,1]{1,0:T(8,128)}, f32[258,1]{1,0:T(8,128)}, u32[]{:S(2)}, u32[]{:S(2)}) collective-permute-start(f32[258,1]{1,0:T(8,128)} %get-tuple-element.7), channel_id=1, source_target_pairs={{1,0},{2,1},{3,2},{5,4},{6,5},{7,6},{9,8},{10,9},{11,10},{13,12},{... | collective-permute-start | bytes 3104 | tf_op jit(solution)/shard_map/ppermute | solution.py:15
  149.0 7.8 %collective-permute-start.21 = (f32[258,1]{1,0:T(8,128)}, f32[258,1]{1,0:T(8,128)}, u32[]{:S(2)}, u32[]{:S(2)}) collective-permute-start(f32[258,1]{1,0:T(8,128)} %get-tuple-element.8), channel_id=1, source_target_pairs={{0,1},{1,2},{2,3},{4,5},{5,6},{6,7},{8,9},{9,10},{10,11},{12,13},{... | collective-permute-start | bytes 3104 | tf_op jit(solution)/shard_map/ppermute | solution.py:14
  161.8 14.9 %collective-permute-start.22 = (f32[1,256,512]{2,1,0:T(8,128)S(1)}, f32[1,256,512]{2,1,0:T(8,128)S(1)}, u32[]{:S(2)}, u32[]{:S(2)}) collective-permute-start(f32[1,256,512]{2,1,0:T(8,128)S(1)} %select_bitcast_fusion), channel_id=1, source_target_pairs={{0,8},{8,16},{16,24},{1,9},{9,17},{17,25},{2,10},{10,18},{18,26},{... | collective-permute-start | bytes 1572872 | tf_op jit(solution)/shard_map/ppermute | solution.py:23
  176.9 4.3 %collective-permute-start.23 = (f32[1,512]{1,0:T(1,128)S(1)}, f32[1,512]{1,0:T(1,128)S(1)}, u32[]{:S(2)}, u32[]{:S(2)}) collective-permute-start(f32[1,512]{1,0:T(1,128)S(1)} %get-tuple-element.18), channel_id=1, source_target_pairs={{4,0},{5,1},{6,2},{7,3},{12,8},{13,9},{14,10},{15,11},{20,16},{21,... | collective-permute-start | bytes 6152 | tf_op jit(solution)/shard_map/ppermute | solution.py:15
  182.2 7.7 %collective-permute-start.25 = (f32[258,1]{1,0:T(8,128)S(1)}, f32[258,1]{1,0:T(8,128)S(1)}, u32[]{:S(2)}, u32[]{:S(2)}) collective-permute-start(f32[258,1]{1,0:T(8,128)S(1)} %get-tuple-element.5), channel_id=1, source_target_pairs={{1,0},{2,1},{3,2},{5,4},{6,5},{7,6},{9,8},{10,9},{11,10},{13,12},{... | collective-permute-start | bytes 3104 | tf_op jit(solution)/shard_map/ppermute | solution.py:15
  184.1 7.7 %collective-permute-start.26 = (f32[258,1]{1,0:T(8,128)S(1)}, f32[258,1]{1,0:T(8,128)S(1)}, u32[]{:S(2)}, u32[]{:S(2)}) collective-permute-start(f32[258,1]{1,0:T(8,128)S(1)} %get-tuple-element.6), channel_id=1, source_target_pairs={{0,1},{1,2},{2,3},{4,5},{5,6},{6,7},{8,9},{9,10},{10,11},{12,13},{... | collective-permute-start | bytes 3104 | tf_op jit(solution)/shard_map/ppermute | solution.py:14
  (17 other events, 189.2 us)
Sparse Core Ops, SparseCore 0:
  102.0 36.9 all-gather.2
where the time goes:
time: 203 us; the launch traced here: 200 us
  waiting for transfers between devices  104 us (51%)
  starting transfers between devices  63.3 us (31%)
  other arithmetic  17 us (8%)
  between operations  14.5 us (7%)
    ppermute x3, waiting for transfers between devices, shifted(): return lax.ppermute(x, axis, pairs)  53.1 us
    ppermute x12, starting transfers between devices, with_halo(): before = lax.ppermute(last, axis, up)  39 us
    all_gather x1, waiting for transfers between devices, on_device(): every = lax.all_gather(second_rhs[None], 'tm', axis=0, tiled=True)  22.1 us
    ppermute x12, starting transfers between devices, with_halo(): after = lax.ppermute(leading, axis, down)  20.2 us
    ppermute x12, waiting for transfers between devices, with_halo(): before = lax.ppermute(last, axis, up)  15.8 us
    ppermute x12, waiting for transfers between devices, with_halo(): after = lax.ppermute(leading, axis, down)  12.9 us
    broadcast_in_dim x2, other arithmetic, on_device(): return (new_c[None], f_out[None])  6.27 us
  transfers between devices with their start and end apart: 28, of which 22 were waited for; matrix products, arithmetic and copies ran while one was open for 0% of the time, Pallas kernels for 0%

commit v1 on v0

v1 whole, which is shorter than its diff:
```python
import functools
import jax
import jax.numpy as jnp
from jax import lax
from jax.experimental import pallas as pl
from jax.experimental.pallas import tpu as pltpu
from jax.sharding import PartitionSpec as P

LANES = 128
SUBLANES = 8
VMEM = pltpu.VMEM


def round_up(value, step):
    return -(-value // step) * step


def ring_pairs(order):
    size = len(order)
    return [(order[i], order[(i + 1) % size]) for i in range(size)]


def both_ways(axis, gray=False):
    size = lax.axis_size(axis)
    order = list(range(size))
    if gray and size & (size - 1) == 0:
        order = [i ^ (i >> 1) for i in order]
    ahead = ring_pairs(order)
    return ahead, [(j, i) for i, j in ahead], order


def edge_kernel(halo, rows, rows_before, rows_after, *refs):
    fields = len(refs) // 2 - 1
    lefts, rights = refs[:fields], refs[fields : 2 * fields]
    first_out, last_out = refs[2 * fields :]
    ix, last_ix = lax.axis_index("sx"), lax.axis_size("sx") - 1
    length = first_out.shape[-1]
    width = rows_before.shape[-1]
    for k in range(fields):
        for block, out, col, lo in (
            (lefts[k], first_out, 0, 0),
            (rights[k], last_out, width - LANES, LANES - halo),
        ):
            after = rows_after[k, :, col : col + LANES]
            before = rows_before[k, :, col : col + LANES]
            if k == 0:
                after = jnp.where(ix == last_ix, 0.0, after)
                before = jnp.where(ix == 0, 0.0, before)
            rest = jnp.zeros((length - rows - 2 * halo, LANES), jnp.float32)
            whole = jnp.concatenate([block[...], after, before, rest], axis=0)
            out[k] = whole.T[lo : lo + halo]


def solve_kernel(plan, *refs):
    rows, width, halo, count, position = (
        plan["rows"], plan["width"], plan["halo"], plan["count"], plan["position"],
    )
    names = plan["names"]
    ref = dict(zip(names, refs))
    kap, state, mid, lap_w, wk, first, second, fa, fb = refs[len(names) + 2 :]
    c_out, f_out = refs[len(names) : len(names) + 2]
    total, wide = rows + 2 * halo, width + LANES
    here = lax.axis_index("tm")
    ix, last_ix = lax.axis_index("sx"), lax.axis_size("sx") - 1
    iy, last_iy = lax.axis_index("sy"), lax.axis_size("sy") - 1
    blocks = total // SUBLANES

    def fill(dst, tile, before, after, left, right, mask=False):
        dst[0:rows, 0:width] = tile
        if mask:
            after = jnp.where(ix == last_ix, 0.0, after)
            before = jnp.where(ix == 0, 0.0, before)
            right = jnp.where(iy == last_iy, 0.0, right)
            left = jnp.where(iy == 0, 0.0, left)
        dst[rows : rows + halo, 0:width] = after
        dst[rows + halo : total, 0:width] = before
        gap = jnp.zeros((LANES - 2 * halo, left.shape[-1]), jnp.float32)
        sides = jnp.concatenate([right, gap, left], axis=0).T
        dst[:, width:wide] = sides[:total]

    def at(i):
        return pl.ds(pl.multiple_of(i * SUBLANES, SUBLANES), SUBLANES)

    def flux_at(dst, i, value):
        dst[at(i + 1), :] = value

        @pl.when(i == 0)
        def _():
            dst[at(blocks + 1), :] = value

        @pl.when(i == blocks - 1)
        def _():
            dst[at(0), :] = value

    def over(body):
        def step(i, carry):
            body(i)
            return carry

        lax.fori_loop(0, blocks, step, 0)

    row = lax.broadcasted_iota(jnp.int32, (SUBLANES, wide), 0)

    def lap(src, i):
        low, cur, high = src[at(i), :], src[at(i + 1), :], src[at(i + 2), :]
        up = jnp.where(row == 0, pltpu.roll(low, 1, 0), pltpu.roll(cur, 1, 0))
        down = jnp.where(row == SUBLANES - 1, pltpu.roll(high, SUBLANES - 1, 0), pltpu.roll(cur, SUBLANES - 1, 0))
        return down + up + pltpu.roll(cur, wide - 1, 1) + pltpu.roll(cur, 1, 1) - 4.0 * cur

    def flux(dst, src):
        def body(i):
            v = src[at(i), :]
            flux_at(dst, i, kap[at(i), :] * v * v)

        over(body)

    def first_part(w, g):
        flux(fa, w)

        def one(i):
            lw = lap(fa, i)
            lap_w[at(i), :] = lw
            f = w[at(i), :] + lw
            mid[at(i), :] = f
            flux_at(fb, i, kap[at(i), :] * f * f)

        over(one)

        def two(i):
            v = mid[at(i), :] + lap(fb, i)
            mid[at(i), :] = v
            g[at(i), :] = (v - w[at(i), :]) - 2.0 * lap_w[at(i), :]
            flux_at(fa, i, kap[at(i), :] * v * v)

        over(two)

    def second_part(w, g):
        def one(i):
            v = mid[at(i), :]
            q = w[at(i), :] + 4.0 * lap_w[at(i), :]
            g[at(i), :] = v + 2.0 * lap(fa, i) - q

        over(one)

    def load(point):
        if point < 0:
            fill(wk, ref["initial"][...], ref["before"][1], ref["after"][1], ref["left"][1], ref["right"][1])
            return
        mine = jnp.int32(0)
        theirs = position[point]
        for t in range(count):
            mine = jnp.where(here == t, position[t], mine)
        away = lax.rem(mine - theirs + count, count)
        for s in range(1, count):

            @pl.when(away == s)
            def _():
                if 2 * s == count:
                    tile = jnp.concatenate([ref["half_back"][0], ref["half_ahead"][0]], axis=0)
                else:
                    tile = ref[f"tile_{s}"][0]
                strips = ref[f"strip_{s}"]
                side = strips.shape[-1] - width
                fill(
                    wk, tile,
                    strips[:halo, :width], strips[halo:, :width],
                    strips[:halo, width:], strips[halo:, width:],
                )

    fill(kap, ref["kappa"][...], ref["before"][0], ref["after"][0], ref["left"][0], ref["right"][0], True)
    fill(state, ref["initial"][...], ref["before"][1], ref["after"][1], ref["left"][1], ref["right"][1])

    inner = rows // SUBLANES

    def tail(j):
        load(2 * j - 1)
        first_part(wk, first)

        @pl.when(lax.rem(here, 2) == 1)
        def _():
            second_part(wk, second)

        flux(fb, state)

        @pl.when(lax.rem(here, 2) == 0)
        def _():
            def body(i):
                x, lx = state[at(i), :], lap(fb, i)
                c = x + 2.0 * lx + first[at(i), :]

                @pl.when(i < inner)
                def _():
                    c_out[0, at(i), :] = c[:, :width]
                    f_out[0, at(i), :] = (x + lx)[:, :width]

            over(body)

        @pl.when(lax.rem(here, 2) == 1)
        def _():
            def body(i):
                x, lx = state[at(i), :], lap(fb, i)
                c = x + 2.0 * lx + first[at(i), :]
                mid[at(i), :] = c
                flux_at(fa, i, kap[at(i), :] * c * c)
                second[at(i), :] = x + 4.0 * lx + second[at(i), :]

            over(body)

            def last(i):
                @pl.when(i < inner)
                def _():
                    f_out[0, at(i), :] = (mid[at(i), :] + lap(fa, i))[:, :width]

            over(last)
            load(2 * j)
            first_part(wk, first)

            def add(i):
                @pl.when(i < inner)
                def _():
                    c_out[0, at(i), :] = (second[at(i), :] + first[at(i), :])[:, :width]

            over(add)

    for j in range((count + 1) // 2):

        @pl.when(lax.div(here, 2) == j)
        def _():
            tail(j)

        if 2 * j + 2 < count:

            @pl.when(lax.div(here, 2) > j)
            def _():
                load(2 * j - 1)
                first_part(wk, first)
                second_part(wk, second)
                load(2 * j)
                first_part(wk, first)
                flux(fb, state)

                def body(i):
                    state[at(i), :] = state[at(i), :] + 4.0 * lap(fb, i) + (second[at(i), :] + first[at(i), :])

                over(body)


def on_device(initial, kappa, c_guess):
    count = lax.axis_size("tm")
    rows, width = initial.shape
    halo = round_up(count // 2 + 3, SUBLANES)
    total, wide = rows + 2 * halo, width + LANES
    ahead, back, order = both_ways("tm", gray=True)
    position = [order.index(t) for t in range(count)]
    middle = rows // 2

    def kernel(body, outs, scratch=()):
        return pl.pallas_call(
            body,
            out_shape=[jax.ShapeDtypeStruct(s, jnp.float32) for s in outs],
            scratch_shapes=[VMEM(s, jnp.float32) for s in scratch],
            compiler_params=pltpu.CompilerParams(vmem_limit_bytes=48 * 2**20),
        )

    tiles = {}
    onward, backward = c_guess, c_guess
    for s in range(1, count // 2):
        onward = lax.ppermute(onward, "tm", ahead)
        backward = lax.ppermute(backward, "tm", back)
        tiles[s], tiles[count - s] = onward, backward
    half_ahead = lax.ppermute(onward[:, middle:], "tm", ahead)
    half_back = lax.ppermute(backward[:, :middle], "tm", back)

    sx_up, sx_down, _ = both_ways("sx")
    sy_up, sy_down, _ = both_ways("sy")
    fields = (kappa, initial, c_guess[0])
    before = lax.ppermute(jnp.stack([x[rows - halo :] for x in fields]), "sx", sx_up)
    after = lax.ppermute(jnp.stack([x[:halo] for x in fields]), "sx", sx_down)
    length = round_up(total, LANES)
    packed = (len(fields), halo, length)
    first_cols, last_cols = kernel(functools.partial(edge_kernel, halo, rows), [packed] * 2)(
        before, after, *[x[:, :LANES] for x in fields], *[x[:, width - LANES :] for x in fields]
    )
    left = lax.ppermute(last_cols, "sy", sy_up)
    right = lax.ppermute(first_cols, "sy", sy_down)

    strip = jnp.concatenate(
        [jnp.concatenate([before[2], after[2]], axis=0), jnp.concatenate([left[2], right[2]], axis=0)], axis=1
    )
    strips = {}
    onward, backward = strip, strip
    for s in range(1, count // 2 + 1):
        onward = lax.ppermute(onward, "tm", ahead)
        strips[s] = onward
        if 2 * s < count:
            backward = lax.ppermute(backward, "tm", back)
            strips[count - s] = backward

    given = dict(
        kappa=kappa, initial=initial, before=before, after=after, left=left, right=right,
        half_ahead=half_ahead, half_back=half_back,
    )
    given |= {f"tile_{s}": x for s, x in tiles.items()}
    given |= {f"strip_{s}": x for s, x in strips.items()}
    plan = dict(rows=rows, width=width, halo=halo, count=count, position=position, names=list(given))
    ext = (total, wide)
    padded = (total + 2 * SUBLANES, wide)
    c_new, f_new = kernel(
        functools.partial(solve_kernel, plan), [c_guess.shape] * 2, [ext] * 7 + [padded] * 2
    )(*given.values())
    return c_new, f_new


def solution(mesh):
    return jax.shard_map(
        on_device,
        mesh=mesh,
        in_specs=(P("sx", "sy"), P("sx", "sy"), P("tm", "sx", "sy")),
        out_specs=(P("tm", "sx", "sy"), P("tm", "sx", "sy")),
        check_vma=False,
    )
```

time: 203 us -> 73.5 us (0.36); the launches traced: 200 us -> 73 us
  waiting for transfers between devices: 104 us -> 13.3 us
  starting transfers between devices: 63.3 us -> 10.4 us
  Pallas kernels: 0 us -> 45.8 us
  other arithmetic: 17 us -> 0.02 us
  between operations: 14.5 us -> 0.73 us
    ppermute x27 -> x11, waiting for transfers between devices: 81.9 us -> 13.3 us  [the longest x3 7.17 us: on_device(): onward = lax.ppermute(onward, 'tm', ahead)]
    ppermute x27 -> x11, starting transfers between devices: 63.2 us -> 10.4 us  [the longest x3 3.63 us: on_device(): onward = lax.ppermute(onward, 'tm', ahead)]
    pallas_call x0 -> x2, Pallas kernels: none -> 45.8 us  [the longest x1 45.5 us: on_device(): kernel(functools.partial(solve_kernel, plan), [c_guess.shape] * 2, [ext]...]
    all_gather x1 -> x0, waiting for transfers between devices: 22.1 us -> none  [on_device(): every = lax.all_gather(second_rhs[None], 'tm', axis=0, tiled=True)]
    broadcast_in_dim x2 -> x0, other arithmetic: 6.27 us -> none  [on_device(): return (new_c[None], f_out[None])]
    select_n x1 -> x0, other arithmetic: 4 us -> none  [on_device(): jnp.where(is_odd, value_prev + 2.0 * lap_v + first_rhs - others[0], 0.0)]
    mul x5 -> x0, other arithmetic: 3.57 us -> none  [spread(): flux = kappa * field * field]
  transfers between devices with their start and end apart: 28 -> 11, of which waited for: 22 -> 4; matrix products, arithmetic and copies ran while one was open for 0% -> 4% of each run, Pallas kernels for 0% -> 0%
where the time goes in v1:
time: 73.5 us; the launch traced here: 73 us
  Pallas kernels  45.8 us (62%)
  waiting for transfers between devices  13.3 us (18%)
  starting transfers between devices  10.4 us (14%)
  local copies, waits for them, and re-layouts  2.74 us (4%)
    pallas_call x1, Pallas kernels, on_device(): kernel(functools.partial(solve_kernel, plan), [c_guess.shape] * 2, [ext]...  45.5 us
    ppermute x3, waiting for transfers between devices, on_device(): onward = lax.ppermute(onward, 'tm', ahead)  7.17 us
    ppermute x2, waiting for transfers between devices, on_device(): backward = lax.ppermute(backward, 'tm', back)  4.19 us
    ppermute x3, starting transfers between devices, on_device(): onward = lax.ppermute(onward, 'tm', ahead)  3.63 us
    ppermute x2, starting transfers between devices, on_device(): backward = lax.ppermute(backward, 'tm', back)  2.05 us
    ppermute x1, waiting for transfers between devices, on_device(): left = lax.ppermute(last_cols, 'sy', sy_up)  1.93 us
    ppermute x1, starting transfers between devices, on_device(): left = lax.ppermute(last_cols, 'sy', sy_up)  1.63 us
    ppermute x1, starting transfers between devices, on_device(): half_ahead = lax.ppermute(onward[:, middle:], 'tm', ahead)  1.57 us
  transfers between devices with their start and end apart: 11, of which 4 were waited for; matrix products, arithmetic and copies ran while one was open for 4% of the time, Pallas kernels for 0%

profile of v1, /device:TPU:14, one launch (start us, length us, event | category | flops | bytes accessed | tf_op | source)
XLA Modules:
  0.0 73.0 jit_solution(6991168196080863738)
XLA Ops:
  0.6 0.6 collective-permute-start.6
  1.2 1.5 %collective-permute-start.4 = (f32[1,256,512]{2,1,0:T(8,128)}, f32[1,256,512]{2,1,0:T(8,128)S(1)}, u32[]{:S(2)}, u32[]{:S(2)}) collective-permute-start(f32[1,256,512]{2,1,0:T(8,128)} %param.5), channel_id=1, source_target_pairs={{0,8},{8,24},{24,16},{16,0},{1,9},{9,25},{25,17},{17,1},{2,10},{10... | collective-permute-start | bytes 1572872 | tf_op jit(solution)/shard_map/ppermute | solution.py:268
  2.7 0.8 %fusion.3 = (f32[1,8,512]{2,1,0:T(8,128)S(1)}, f32[1,8,512]{2,1,0:T(8,128)S(1)}) fusion(f32[1,256,512]{2,1,0:T(8,128)} %param.5), kind=kLoop, calls=%fused_computation.14 | loop fusion | bytes 65536 | tf_op jit(solution)/shard_map/slice | solution.py:278
  3.5 0.8 %slice_bitcast_fusion.2 = (f32[1,8,512]{2,1,0:T(8,128)S(1)}, f32[1,8,512]{2,1,0:T(8,128)S(1)}, f32[1,8,512]{2,1,0:T(8,128)S(1)}, f32[1,8,512]{2,1,0:T(8,128)S(1)}) fusion(f32[256,512]{1,0:T(8,128)} %refs_1_.1, f32[256,512]{1,0:T(8,128)} %refs_0_.1), kind=kLoop, calls=%fused_computation.5 | loop fusion | bytes 131072 | tf_op jit(solution)/shard_map/stack | solution.py:278
  4.2 0.1 collective-permute-start
  4.3 0.0 copy-start.2
  4.3 0.5 collective-permute-start.1
  4.8 1.1 %fusion.1 = (f32[256,128]{1,0:T(8,128)S(1)}, f32[256,128]{1,0:T(8,128)S(1)}, f32[256,128]{1,0:T(8,128)S(1)}, f32[256,128]{1,0:T(8,128)S(1)}) fusion(f32[256,512]{1,0:T(8,128)} %refs_1_.1, f32[256,512]{1,0:T(8,128)} %refs_0_.1), kind=kLoop, calls=%fused_computation.12 | loop fusion | bytes 1048576 | tf_op jit(solution)/shard_map/slice | solution.py:282
  6.0 0.0 collective-permute-done.rows_before.refs_2_
  6.0 0.0 collective-permute-done.1.rows_after.refs_3_
  6.0 0.3 shard_map.50
  6.4 1.6 %collective-permute-start.2 = (f32[3,8,384]{2,1,0:T(8,128)S(1)}, f32[3,8,384]{2,1,0:T(8,128)S(1)}, u32[]{:S(2)}, u32[]{:S(2)}) collective-permute-start(f32[3,8,384]{2,1,0:T(8,128)S(1)} %get-tuple-element.4), channel_id=1, source_target_pairs={{0,1},{1,2},{2,3},{3,0},{4,5},{5,6},{6,7},{7,4},{8,9},{9,10},{10,1... | collective-permute-start | bytes 110600 | tf_op jit(solution)/shard_map/ppermute | solution.py:284
  8.0 0.4 collective-permute-start.3
  8.4 1.9 %collective-permute-done.2.refs_4_ = f32[3,8,384]{2,1,0:T(8,128)S(1)} collective-permute-done((f32[3,8,384]{2,1,0:T(8,128)S(1)}, f32[3,8,384]{2,1,0:T(8,128)S(1)}, u32[]{:S(2)}, u32[]{:S(2)}) %collective-permute-start.2) | collective-permute-done | bytes 36896 | tf_op jit(solution)/shard_map/ppermute | solution.py:284
  10.4 4.2 %collective-permute-done.6.refs_9_ = f32[1,256,512]{2,1,0:T(8,128)S(1)} collective-permute-done((f32[1,256,512]{2,1,0:T(8,128)}, f32[1,256,512]{2,1,0:T(8,128)S(1)}, u32[]{:S(2)}, u32[]{:S(2)}) %collective-permute-start.6) | collective-permute-done | bytes 524320 | tf_op jit(solution)/shard_map/ppermute | solution.py:269
  14.6 0.6 collective-permute-start.7
  15.1 0.0 collective-permute-done.4.refs_8_
  15.2 1.6 %collective-permute-start.5 = (f32[1,128,512]{2,1,0:T(8,128)S(1)}, f32[1,128,512]{2,1,0:T(8,128)S(1)}, u32[]{:S(2)}, u32[]{:S(2)}) collective-permute-start(f32[1,128,512]{2,1,0:T(8,128)S(1)} %slice.76), channel_id=1, source_target_pairs={{0,8},{8,24},{24,16},{16,0},{1,9},{9,25},{25,17},{17,1},{2,10},{10... | collective-permute-start | bytes 786440 | tf_op jit(solution)/shard_map/ppermute | solution.py:271
  16.7 0.6 collective-permute-start.8
  17.3 1.5 %collective-permute-start.9 = (f32[16,896]{1,0:T(8,128)S(1)}, f32[16,896]{1,0:T(8,128)S(1)}, u32[]{:S(2)}, u32[]{:S(2)}) collective-permute-start(f32[16,896]{1,0:T(8,128)S(1)} %maximum_maximum_fusion), channel_id=1, source_target_pairs={{8,0},{24,8},{16,24},{0,16},{9,1},{25,9},{17,25},{1,17},{10,2},{26... | collective-permute-start | bytes 172040 | tf_op jit(solution)/shard_map/ppermute | solution.py:296
  18.8 4.5 %collective-permute-done.8.refs_10_ = f32[16,896]{1,0:T(8,128)S(1)} collective-permute-done((f32[16,896]{1,0:T(8,128)S(1)}, f32[16,896]{1,0:T(8,128)S(1)}, u32[]{:S(2)}, u32[]{:S(2)}) %collective-permute-start.8) | collective-permute-done | bytes 57376 | tf_op jit(solution)/shard_map/ppermute | solution.py:293
  23.3 1.5 %collective-permute-start.10 = (f32[16,896]{1,0:T(8,128)S(1)}, f32[16,896]{1,0:T(8,128)S(1)}, u32[]{:S(2)}, u32[]{:S(2)}) collective-permute-start(f32[16,896]{1,0:T(8,128)S(1)} %collective-permute-done.8.refs_10_), channel_id=1, source_target_pairs={{0,8},{8,24},{24,16},{16,0},{1,9},{9,25},{25,17},{17,1},{2,10},{10... | collective-permute-start | bytes 172040 | tf_op jit(solution)/shard_map/ppermute | solution.py:293
  24.9 2.7 %collective-permute-done.10.refs_12_ = f32[16,896]{1,0:T(8,128)S(1)} collective-permute-done((f32[16,896]{1,0:T(8,128)S(1)}, f32[16,896]{1,0:T(8,128)S(1)}, u32[]{:S(2)}, u32[]{:S(2)}) %collective-permute-start.10) | collective-permute-done | bytes 57376 | tf_op jit(solution)/shard_map/ppermute | solution.py:293
  27.5 45.5 %shard_map.51 = (f32[1,256,512]{2,1,0:T(8,128)}, f32[1,256,512]{2,1,0:T(8,128)}) custom-call(f32[256,512]{1,0:T(8,128)S(1)} %copy-done, f32[256,512]{1,0:T(8,128)S(1)} %copy-done.1, f32[3,8,512]{2,1,0:T(8,128)S(1)} %collective-permute-done.rows_before.refs_2_, f32[3,8,512]{2,1,0:T(8,128)S(1)} %collective-permute-done.1.rows_after.refs_3_, ...), custom_call_target="tpu_custom_call" | custom-call | tf_op jit(solution)/shard_map/pallas_call | solution.py:308
  (19 shorter events, 0.1 us)
Async XLA Ops:
  0.6 13.9 %collective-permute-start.6 = (f32[1,256,512]{2,1,0:T(8,128)}, f32[1,256,512]{2,1,0:T(8,128)S(1)}, u32[]{:S(2)}, u32[]{:S(2)}) collective-permute-start(f32[1,256,512]{2,1,0:T(8,128)} %param.5), channel_id=1, source_target_pairs={{8,0},{24,8},{16,24},{0,16},{9,1},{25,9},{17,25},{1,17},{10,2},{26... | collective-permute-start | bytes 1572872 | tf_op jit(solution)/shard_map/ppermute | solution.py:269
  1.2 14.0 %collective-permute-start.4 = (f32[1,256,512]{2,1,0:T(8,128)}, f32[1,256,512]{2,1,0:T(8,128)S(1)}, u32[]{:S(2)}, u32[]{:S(2)}) collective-permute-start(f32[1,256,512]{2,1,0:T(8,128)} %param.5), channel_id=1, source_target_pairs={{0,8},{8,24},{24,16},{16,0},{1,9},{9,25},{25,17},{17,1},{2,10},{10... | collective-permute-start | bytes 1572872 | tf_op jit(solution)/shard_map/ppermute | solution.py:268
  4.2 1.8 %collective-permute-start = (f32[3,8,512]{2,1,0:T(8,128)S(1)}, f32[3,8,512]{2,1,0:T(8,128)S(1)}, u32[]{:S(2)}, u32[]{:S(2)}) collective-permute-start(f32[3,8,512]{2,1,0:T(8,128)S(1)} %pad_maximum_fusion), channel_id=1, source_target_pairs={{0,4},{4,0},{1,5},{5,1},{2,6},{6,2},{3,7},{7,3},{8,12},{12,8},{9,1... | collective-permute-start | bytes 147464 | tf_op jit(solution)/shard_map/ppermute | solution.py:277
  4.3 1.6 %copy-start.2 = (f32[1,256,512]{2,1,0:T(8,128)S(1)}, f32[1,256,512]{2,1,0:T(8,128)}, u32[]{:S(2)}) copy-start(f32[1,256,512]{2,1,0:T(8,128)} %param.5) | copy-start | bytes 1572868
  4.3 1.7 %collective-permute-start.1 = (f32[3,8,512]{2,1,0:T(8,128)S(1)}, f32[3,8,512]{2,1,0:T(8,128)S(1)}, u32[]{:S(2)}, u32[]{:S(2)}) collective-permute-start(f32[3,8,512]{2,1,0:T(8,128)S(1)} %pad_maximum_fusion.1), channel_id=1, source_target_pairs={{4,0},{0,4},{5,1},{1,5},{6,2},{2,6},{7,3},{3,7},{12,8},{8,12},{13,... | collective-permute-start | bytes 147464 | tf_op jit(solution)/shard_map/ppermute | solution.py:278
  6.4 4.0 %collective-permute-start.2 = (f32[3,8,384]{2,1,0:T(8,128)S(1)}, f32[3,8,384]{2,1,0:T(8,128)S(1)}, u32[]{:S(2)}, u32[]{:S(2)}) collective-permute-start(f32[3,8,384]{2,1,0:T(8,128)S(1)} %get-tuple-element.4), channel_id=1, source_target_pairs={{0,1},{1,2},{2,3},{3,0},{4,5},{5,6},{6,7},{7,4},{8,9},{9,10},{10,1... | collective-permute-start | bytes 110600 | tf_op jit(solution)/shard_map/ppermute | solution.py:284
  8.0 8.8 %collective-permute-start.3 = (f32[3,8,384]{2,1,0:T(8,128)S(1)}, f32[3,8,384]{2,1,0:T(8,128)S(1)}, u32[]{:S(2)}, u32[]{:S(2)}) collective-permute-start(f32[3,8,384]{2,1,0:T(8,128)S(1)} %get-tuple-element.5), channel_id=1, source_target_pairs={{1,0},{2,1},{3,2},{0,3},{5,4},{6,5},{7,6},{4,7},{9,8},{10,9},{11,1... | collective-permute-start | bytes 110600 | tf_op jit(solution)/shard_map/ppermute | solution.py:285
  10.4 17.2 %copy-start = (f32[256,512]{1,0:T(8,128)S(1)}, f32[256,512]{1,0:T(8,128)}, u32[]{:S(2)}) copy-start(f32[256,512]{1,0:T(8,128)} %refs_0_.1) | copy-start | bytes 1572868
  10.4 17.2 %copy-start.1 = (f32[256,512]{1,0:T(8,128)S(1)}, f32[256,512]{1,0:T(8,128)}, u32[]{:S(2)}) copy-start(f32[256,512]{1,0:T(8,128)} %refs_1_.1) | copy-start | bytes 1572868
  14.6 12.9 %collective-permute-start.7 = (f32[1,128,512]{2,1,0:T(8,128)S(1)}, f32[1,128,512]{2,1,0:T(8,128)S(1)}, u32[]{:S(2)}, u32[]{:S(2)}) collective-permute-start(f32[1,128,512]{2,1,0:T(8,128)S(1)} %slice.77), channel_id=1, source_target_pairs={{8,0},{24,8},{16,24},{0,16},{9,1},{25,9},{17,25},{1,17},{10,2},{26... | collective-permute-start | bytes 786440 | tf_op jit(solution)/shard_map/ppermute | solution.py:272
  15.2 12.4 %collective-permute-start.5 = (f32[1,128,512]{2,1,0:T(8,128)S(1)}, f32[1,128,512]{2,1,0:T(8,128)S(1)}, u32[]{:S(2)}, u32[]{:S(2)}) collective-permute-start(f32[1,128,512]{2,1,0:T(8,128)S(1)} %slice.76), channel_id=1, source_target_pairs={{0,8},{8,24},{24,16},{16,0},{1,9},{9,25},{25,17},{17,1},{2,10},{10... | collective-permute-start | bytes 786440 | tf_op jit(solution)/shard_map/ppermute | solution.py:271
  16.7 6.6 %collective-permute-start.8 = (f32[16,896]{1,0:T(8,128)S(1)}, f32[16,896]{1,0:T(8,128)S(1)}, u32[]{:S(2)}, u32[]{:S(2)}) collective-permute-start(f32[16,896]{1,0:T(8,128)S(1)} %maximum_maximum_fusion), channel_id=1, source_target_pairs={{0,8},{8,24},{24,16},{16,0},{1,9},{9,25},{25,17},{17,1},{2,10},{10... | collective-permute-start | bytes 172040 | tf_op jit(solution)/shard_map/ppermute | solution.py:293
  17.3 7.5 %collective-permute-start.9 = (f32[16,896]{1,0:T(8,128)S(1)}, f32[16,896]{1,0:T(8,128)S(1)}, u32[]{:S(2)}, u32[]{:S(2)}) collective-permute-start(f32[16,896]{1,0:T(8,128)S(1)} %maximum_maximum_fusion), channel_id=1, source_target_pairs={{8,0},{24,8},{16,24},{0,16},{9,1},{25,9},{17,25},{1,17},{10,2},{26... | collective-permute-start | bytes 172040 | tf_op jit(solution)/shard_map/ppermute | solution.py:296
  23.3 4.2 %collective-permute-start.10 = (f32[16,896]{1,0:T(8,128)S(1)}, f32[16,896]{1,0:T(8,128)S(1)}, u32[]{:S(2)}, u32[]{:S(2)}) collective-permute-start(f32[16,896]{1,0:T(8,128)S(1)} %collective-permute-done.8.refs_10_), channel_id=1, source_target_pairs={{0,8},{8,24},{24,16},{16,0},{1,9},{9,25},{25,17},{17,1},{2,10},{10... | collective-permute-start | bytes 172040 | tf_op jit(solution)/shard_map/ppermute | solution.py:293

commit v2 on v0

v2 whole, which is shorter than its diff:
```python
import functools
import jax
import jax.numpy as jnp
from jax import lax
from jax.experimental import pallas as pl
from jax.experimental.pallas import tpu as pltpu
from jax.sharding import PartitionSpec as P

LANES = 128
SUBLANES = 8
BLOCK = 16


def round_up(value, step):
    return -(-value // step) * step


def ring(axis, gray=False):
    size = lax.axis_size(axis)
    order = list(range(size))
    if gray and size & (size - 1) == 0:
        order = [i ^ (i >> 1) for i in order]
    return order


def shift(x, axis, order, by):
    size = len(order)
    return lax.ppermute(x, axis, [(order[i], order[(i + by) % size]) for i in range(size)])


def call(body, outs, scratch=(), **options):
    return pl.pallas_call(
        body,
        out_shape=[jax.ShapeDtypeStruct(s, jnp.float32) for s in outs],
        scratch_shapes=[pltpu.VMEM(s, jnp.float32) for s in scratch],
        compiler_params=pltpu.CompilerParams(vmem_limit_bytes=48 * 2**20),
        **options,
    )


def edge_kernel(halo, rows, rows_before, rows_after, *refs):
    fields = len(refs) // 2 - 1
    lefts, rights = refs[:fields], refs[fields : 2 * fields]
    first_out, last_out = refs[2 * fields :]
    ix, last_ix = lax.axis_index("sx"), lax.axis_size("sx") - 1
    length = first_out.shape[-1]
    width = rows_before.shape[-1]
    for k in range(fields):
        for block, out, col, lo in (
            (lefts[k], first_out, 0, 0),
            (rights[k], last_out, width - LANES, LANES - halo),
        ):
            after = rows_after[k, :, col : col + LANES]
            before = rows_before[k, :, col : col + LANES]
            if k == 0:
                after = jnp.where(ix == last_ix, 0.0, after)
                before = jnp.where(ix == 0, 0.0, before)
            rest = jnp.zeros((length - rows - 2 * halo, LANES), jnp.float32)
            whole = jnp.concatenate([block[...], after, before, rest], axis=0)
            out[k] = whole.T[lo : lo + halo]


class Grid:
    def __init__(self, rows, width, halo):
        self.rows, self.width, self.halo = rows, width, halo
        self.total, self.wide = rows + 2 * halo, width + LANES
        self.ext = (self.total, self.wide)
        self.padded = (self.total + 2 * SUBLANES, self.wide)

    def fill(self, dst, tile, before, after, left, right):
        rows, halo, total, width = self.rows, self.halo, self.total, self.width
        at = 0
        for part in tile:
            dst[at : at + part.shape[0], 0:width] = part
            at += part.shape[0]
        dst[rows : rows + halo, 0:width] = after
        dst[rows + halo : total, 0:width] = before
        gap = jnp.zeros((LANES - 2 * halo, left.shape[-1]), jnp.float32)
        sides = jnp.concatenate([right, gap, left], axis=0).T
        dst[:, width:] = sides[:total]

    def over(self, body, dst=None):
        total = self.total
        for o in range(0, total, BLOCK):
            size = min(BLOCK, total - o)
            value = body(slice(o, o + size))
            if dst is None:
                continue
            dst[o + SUBLANES : o + SUBLANES + size, :] = value
            if o == 0:
                dst[total + SUBLANES :, :] = value[:SUBLANES]
            if o + size == total:
                dst[0:SUBLANES, :] = value[size - SUBLANES :]

    def lap(self, src, at):
        size, wide = at.stop - at.start, self.wide
        around = src[at.start : at.stop + 2 * SUBLANES, :]
        cur = around[SUBLANES : SUBLANES + size]
        up = pltpu.roll(around, 1, 0)[SUBLANES : SUBLANES + size]
        down = pltpu.roll(around, size + 2 * SUBLANES - 1, 0)[SUBLANES : SUBLANES + size]
        return down + up + pltpu.roll(cur, wide - 1, 1) + pltpu.roll(cur, 1, 1) - 4.0 * cur

    def flux(self, kap, src, dst):
        def body(at):
            v = src[at, :]
            return kap[at, :] * v * v

        self.over(body, dst)

    def first_part(self, kap, w, mid, lap_w, fa, fb, out):
        self.flux(kap, w, fa)

        def one(at):
            lw = self.lap(fa, at)
            lap_w[at, :] = lw
            f = w[at, :] + lw
            mid[at, :] = f
            return kap[at, :] * f * f

        self.over(one, fb)

        def two(at):
            v = mid[at, :] + self.lap(fb, at)
            mid[at, :] = v
            out(at, (v - w[at, :]) - 2.0 * lap_w[at, :])
            return kap[at, :] * v * v

        self.over(two, fa)

    def second_part(self, w, mid, lap_w, fa, out):
        def one(at):
            q = w[at, :] + 4.0 * lap_w[at, :]
            out(at, mid[at, :] + 2.0 * self.lap(fa, at) - q)

        self.over(one)


def absorb(grid, kap, point, here, load, even, odd, tail, work):
    wk, mid, lap_w, fa, fb = work
    load(wk)
    step = lax.div(point, 2)

    @pl.when(lax.rem(point, 2) == 1)
    def _():
        def out(at, g):
            odd[step, at, :] = g

        grid.first_part(kap, wk, mid, lap_w, fa, fb, out)

    @pl.when(lax.rem(point, 2) == 0)
    def _():
        def out(at, g):
            tail[at, :] = g

        grid.first_part(kap, wk, mid, lap_w, fa, fb, out)

        @pl.when(point < here)
        def _():
            def out(at, h):
                even[step, at, :] = h

            grid.second_part(wk, mid, lap_w, fa, out)


def start_kernel(grid, kappa, initial, before, after, left, right, kap, even, tail, low, wk, mid, lap_w, fa, fb):
    ix, last_ix = lax.axis_index("sx"), lax.axis_size("sx") - 1
    iy, last_iy = lax.axis_index("sy"), lax.axis_size("sy") - 1
    grid.fill(
        kap, [kappa[...]],
        jnp.where(ix == 0, 0.0, before[0]), jnp.where(ix == last_ix, 0.0, after[0]),
        jnp.where(iy == 0, 0.0, left[0]), jnp.where(iy == last_iy, 0.0, right[0]),
    )
    grid.fill(wk, [initial[...]], before[1], after[1], left[1], right[1])

    def out(at, g):
        x, lx = wk[at, :], lap_w[at, :]
        tail[at, :] = x + 2.0 * lx + g
        low[at, :] = x + lx

    grid.first_part(kap, wk, mid, lap_w, fa, fb, out)

    def out_even(at, h):
        even[0, at, :] = (wk[at, :] + 4.0 * lap_w[at, :]) + h

    grid.second_part(wk, mid, lap_w, fa, out_even)


def arrival(grid, index, away, tile, strip, kap, here_pos, order, even, odd, tail, work):
    count = len(order)
    here, point = lax.axis_index("tm"), jnp.int32(count)
    for p in range(count):
        point = jnp.where(here == order[p], order[(p - away) % count] + 1, point)

    def load(wk):
        halo, width = grid.halo, grid.width
        strips = strip[...]
        grid.fill(
            wk, [t[0] for t in tile],
            strips[:halo, :width], strips[halo:, :width], strips[:halo, width:], strips[halo:, width:],
        )

    @pl.when(point <= here)
    def _():
        absorb(grid, kap, point, here, load, even, odd, tail, work)


def middle_kernel(grid, order, aways, kap, even_in, odd_in, tail_in, *refs):
    pairs = [refs[2 * i : 2 * i + 2] for i in range(len(aways))]
    even, odd, tail = refs[2 * len(aways) : 2 * len(aways) + 3]
    work = refs[2 * len(aways) + 3 :]
    for away, (tile, strip) in zip(aways, pairs):
        arrival(grid, None, away, [tile], strip, kap, None, order, even, odd, tail, work)


def last_kernel(grid, order, kap, even, odd_in, tail_in, low, first, second, strip, c_out, f_out, odd, tail, *work):
    wk, mid, lap_w, fa, fb = work
    count = len(order)
    here = lax.axis_index("tm")
    rows, width = grid.rows, grid.width
    if count > 1:
        arrival(grid, None, count // 2, [first, second], strip, kap, None, order, even, odd, tail, work)
    state = wk

    def put(dst, at, value):
        stop = min(at.stop, rows)
        if at.start < stop:
            dst[0, at.start : stop, :] = value[: stop - at.start, :width]

    @pl.when(here == 0)
    def _():
        c_out[0] = tail[:rows, :width]
        f_out[0] = low[:rows, :width]

    @pl.when(here == 1)
    def _():
        grid.flux(kap, tail, fa)

        def body(at):
            put(c_out, at, even[0, at, :] + odd[0, at, :])
            put(f_out, at, tail[at, :] + grid.lap(fa, at))

        grid.over(body)

    @pl.when(here >= 2)
    def _():
        def begin(at):
            x = even[0, at, :] + odd[0, at, :]
            state[at, :] = x
            return kap[at, :] * x * x

        grid.over(begin, fb)

        if count > 4:

            def step(j, carry):
                def body(at):
                    x = state[at, :] + 4.0 * grid.lap(fb, at) + (even[j, at, :] + odd[j, at, :])
                    state[at, :] = x
                    return kap[at, :] * x * x

                grid.over(body, fa)
                fb[...] = fa[...]
                return carry

            lax.fori_loop(1, lax.div(here, 2), step, 0)

        @pl.when(lax.rem(here, 2) == 0)
        def _():
            def body(at):
                x, lx = state[at, :], grid.lap(fb, at)
                put(c_out, at, x + 2.0 * lx + tail[at, :])
                put(f_out, at, x + lx)

            grid.over(body)

        @pl.when(lax.rem(here, 2) == 1)
        def _():
            j = lax.div(here, 2)

            def body(at):
                x, lx = state[at, :], grid.lap(fb, at)
                c = x + 2.0 * lx + tail[at, :]
                mid[at, :] = c
                put(c_out, at, x + 4.0 * lx + (even[j, at, :] + odd[j, at, :]))
                return kap[at, :] * c * c

            grid.over(body, fa)

            def last(at):
                put(f_out, at, mid[at, :] + grid.lap(fa, at))

            grid.over(last)


def on_device(initial, kappa, c_guess):
    count = lax.axis_size("tm")
    rows, width = initial.shape
    halo = round_up(count // 2 + 3, SUBLANES)
    grid = Grid(rows, width, halo)
    order = ring("tm", gray=True)
    sx, sy = ring("sx"), ring("sy")
    middle = rows // 2

    tiles = {}
    onward, backward = c_guess, c_guess
    for s in range(1, count // 2):
        onward, backward = shift(onward, "tm", order, 1), shift(backward, "tm", order, -1)
        tiles[s], tiles[count - s] = onward, backward
    second = shift(onward[:, middle:], "tm", order, 1)
    first = shift(backward[:, :middle], "tm", order, -1)

    fields = (kappa, initial, c_guess[0])
    before = shift(jnp.stack([x[rows - halo :] for x in fields]), "sx", sx, 1)
    after = shift(jnp.stack([x[:halo] for x in fields]), "sx", sx, -1)
    length = round_up(grid.total, LANES)
    packed = (len(fields), halo, length)
    first_cols, last_cols = call(functools.partial(edge_kernel, halo, rows), [packed] * 2)(
        before, after, *[x[:, :LANES] for x in fields], *[x[:, width - LANES :] for x in fields]
    )
    left = shift(last_cols, "sy", sy, 1)
    right = shift(first_cols, "sy", sy, -1)

    strip = jnp.concatenate(
        [jnp.concatenate([before[2], after[2]], axis=0), jnp.concatenate([left[2], right[2]], axis=0)], axis=1
    )
    strips = {s: shift(strip, "tm", order, s) for s in range(1, count)}

    ext, padded = grid.ext, grid.padded
    work = [ext] * 3 + [padded] * 2
    sides = (count // 2, *ext)
    kap, even, tail, low = call(functools.partial(start_kernel, grid), [ext, sides, ext, ext], work)(
        kappa, initial, before, after, left, right
    )
    odd = jnp.zeros(sides, jnp.float32)
    for s in range(1, count // 2):
        aways = sorted({s, count - s})
        pairs = [x for a in aways for x in (tiles[a], strips[a])]
        even, odd, tail = call(
            functools.partial(middle_kernel, grid, order, aways), [sides, sides, ext], work,
            input_output_aliases={1: 0, 2: 1, 3: 2},
        )(kap, even, odd, tail, *pairs)
    c_new, f_new, _, _ = call(
        functools.partial(last_kernel, grid, order), [c_guess.shape] * 2 + [sides, ext], work,
        input_output_aliases={2: 2, 3: 3},
    )(kap, even, odd, tail, low, first, second, strips[count // 2])
    return c_new, f_new


def solution(mesh):
    return jax.shard_map(
        on_device,
        mesh=mesh,
        in_specs=(P("sx", "sy"), P("sx", "sy"), P("tm", "sx", "sy")),
        out_specs=(P("tm", "sx", "sy"), P("tm", "sx", "sy")),
        check_vma=False,
    )
```

time: 203 us -> 31 us (0.15); the launches traced: 200 us -> 30.6 us
  waiting for transfers between devices: 104 us -> 9.15 us
  starting transfers between devices: 63.3 us -> 10.4 us
  other arithmetic: 17 us -> 0.02 us
  between operations: 14.5 us -> 0.78 us
  Pallas kernels: 0 us -> 7.43 us
    ppermute x27 -> x11, waiting for transfers between devices: 81.9 us -> 9.15 us  [shift(): lax.ppermute(x, axis, [(order[i], order[(i + by) % size]) for i in range(...]
    ppermute x27 -> x11, starting transfers between devices: 63.2 us -> 10.4 us  [shift(): lax.ppermute(x, axis, [(order[i], order[(i + by) % size]) for i in range(...]
    all_gather x1 -> x0, waiting for transfers between devices: 22.1 us -> none  [on_device(): every = lax.all_gather(second_rhs[None], 'tm', axis=0, tiled=True)]
    pallas_call x0 -> x4, Pallas kernels: none -> 7.43 us  [the longest x1 3 us: on_device(): call(functools.partial(last_kernel, grid, order), [c_guess.shape] * 2 + [...]
    broadcast_in_dim x2 -> x0, other arithmetic: 6.27 us -> none  [on_device(): return (new_c[None], f_out[None])]
    select_n x1 -> x0, other arithmetic: 4 us -> none  [on_device(): jnp.where(is_odd, value_prev + 2.0 * lap_v + first_rhs - others[0], 0.0)]
    mul x5 -> x0, other arithmetic: 3.57 us -> none  [spread(): flux = kappa * field * field]
  transfers between devices with their start and end apart: 28 -> 11, of which waited for: 22 -> 3; matrix products, arithmetic and copies ran while one was open for 0% -> 9% of each run, Pallas kernels for 0% -> 14%
where the time goes in v2:
time: 31 us; the launch traced here: 30.6 us
  starting transfers between devices  10.4 us (34%)
  waiting for transfers between devices  9.15 us (30%)
  Pallas kernels  7.43 us (24%)
  local copies, waits for them, and re-layouts  2.84 us (9%)
  between operations  0.78 us (3%)
    ppermute x11, starting transfers between devices, shift(): lax.ppermute(x, axis, [(order[i], order[(i + by) % size]) for i in range(...  10.4 us
    ppermute x11, waiting for transfers between devices, shift(): lax.ppermute(x, axis, [(order[i], order[(i + by) % size]) for i in range(...  9.15 us
    pallas_call x1, Pallas kernels, on_device(): call(functools.partial(last_kernel, grid, order), [c_guess.shape] * 2 + [...  3 us
    pallas_call x1, Pallas kernels, on_device(): call(functools.partial(middle_kernel, grid, order, aways), [sides, sides,...  2.54 us
    pallas_call x1, Pallas kernels, on_device(): call(functools.partial(start_kernel, grid), [ext, sides, ext, ext], work)  1.57 us
    slice x2, local copies, waits for them, and re-layouts, on_device(): x[:, width - LANES:]  1.15 us
    another operation x1, local copies, waits for them, and re-layouts, on_device(): after = shift(jnp.stack([x[:halo] for x in fields]), 'sx', sx, -1)  0.77 us
    slice x1, local copies, waits for them, and re-layouts, on_device(): after = shift(jnp.stack([x[:halo] for x in fields]), 'sx', sx, -1)  0.75 us
  transfers between devices with their start and end apart: 11, of which 3 were waited for; matrix products, arithmetic and copies ran while one was open for 9% of the time, Pallas kernels for 14%

profile of v2, /device:TPU:14, one launch (start us, length us, event | category | flops | bytes accessed | tf_op | source)
XLA Modules:
  0.0 30.6 jit_solution(16995150982145849867)
XLA Ops:
  0.6 0.6 %collective-permute-start.4 = (f32[1,256,512]{2,1,0:T(8,128)}, f32[1,256,512]{2,1,0:T(8,128)S(1)}, u32[]{:S(2)}, u32[]{:S(2)}) collective-permute-start(f32[1,256,512]{2,1,0:T(8,128)} %param.5), channel_id=1, source_target_pairs={{0,8},{8,24},{24,16},{16,0},{1,9},{9,25},{25,17},{17,1},{2,10},{10... | collective-permute-start | bytes 1572872 | tf_op jit(solution)/shard_map/ppermute | solution.py:28
  1.2 1.5 %collective-permute-start.6 = (f32[1,256,512]{2,1,0:T(8,128)}, f32[1,256,512]{2,1,0:T(8,128)S(1)}, u32[]{:S(2)}, u32[]{:S(2)}) collective-permute-start(f32[1,256,512]{2,1,0:T(8,128)} %param.5), channel_id=1, source_target_pairs={{0,16},{8,0},{24,8},{16,24},{1,17},{9,1},{25,9},{17,25},{2,18},{10... | collective-permute-start | bytes 1572872 | tf_op jit(solution)/shard_map/ppermute | solution.py:28
  2.7 0.8 %fusion.3 = (f32[1,8,512]{2,1,0:T(8,128)S(1)}, f32[1,8,512]{2,1,0:T(8,128)S(1)}) fusion(f32[1,256,512]{2,1,0:T(8,128)} %param.5), kind=kLoop, calls=%fused_computation.14 | loop fusion | bytes 65536 | tf_op jit(solution)/shard_map/slice | solution.py:314
  3.5 0.8 %slice_bitcast_fusion.2 = (f32[1,8,512]{2,1,0:T(8,128)S(1)}, f32[1,8,512]{2,1,0:T(8,128)S(1)}, f32[1,8,512]{2,1,0:T(8,128)S(1)}, f32[1,8,512]{2,1,0:T(8,128)S(1)}) fusion(f32[256,512]{1,0:T(8,128)} %initial.1, f32[256,512]{1,0:T(8,128)} %kappa.1), kind=kLoop, calls=%fused_computation.5 | loop fusion | bytes 131072 | tf_op jit(solution)/shard_map/stack | solution.py:314
  4.3 0.1 collective-permute-start.1
  4.3 0.5 %collective-permute-start = (f32[3,8,512]{2,1,0:T(8,128)S(1)}, f32[3,8,512]{2,1,0:T(8,128)S(1)}, u32[]{:S(2)}, u32[]{:S(2)}) collective-permute-start(f32[3,8,512]{2,1,0:T(8,128)S(1)} %pad_maximum_fusion), channel_id=1, source_target_pairs={{0,4},{4,0},{1,5},{5,1},{2,6},{6,2},{3,7},{7,3},{8,12},{12,8},{9,1... | collective-permute-start | bytes 147464 | tf_op jit(solution)/shard_map/ppermute | solution.py:28
  4.8 1.1 %fusion.1 = (f32[256,128]{1,0:T(8,128)S(1)}, f32[256,128]{1,0:T(8,128)S(1)}, f32[256,128]{1,0:T(8,128)S(1)}, f32[256,128]{1,0:T(8,128)S(1)}) fusion(f32[256,512]{1,0:T(8,128)} %initial.1, f32[256,512]{1,0:T(8,128)} %kappa.1), kind=kLoop, calls=%fused_computation.12 | loop fusion | bytes 1048576 | tf_op jit(solution)/shard_map/slice | solution.py:318
  6.0 0.0 copy-start
  6.0 0.0 copy-start.1
  6.1 0.3 %shard_map.50 = (f32[3,8,384]{2,1,0:T(8,128)S(1)}, f32[3,8,384]{2,1,0:T(8,128)S(1)}) custom-call(f32[3,8,512]{2,1,0:T(8,128)S(1)} %collective-permute-done.rows_before.before, f32[3,8,512]{2,1,0:T(8,128)S(1)} %collective-permute-done.1.rows_after.after, f32[256,128]{1,0:T(8,128)S(1)} %get-tuple-element.38.refs_0_, f32[256,128]{1,0:T(8,128)S(1)} %get-tuple-element.27.refs_1_, ...), custom_call_target="tpu_custom_call" | custom-call | tf_op jit(solution)/shard_map/pallas_call | solution.py:317
  6.4 1.6 %collective-permute-start.2 = (f32[3,8,384]{2,1,0:T(8,128)S(1)}, f32[3,8,384]{2,1,0:T(8,128)S(1)}, u32[]{:S(2)}, u32[]{:S(2)}) collective-permute-start(f32[3,8,384]{2,1,0:T(8,128)S(1)} %get-tuple-element.13), channel_id=1, source_target_pairs={{0,1},{1,2},{2,3},{3,0},{4,5},{5,6},{6,7},{7,4},{8,9},{9,10},{10,1... | collective-permute-start | bytes 110600 | tf_op jit(solution)/shard_map/ppermute | solution.py:28
  8.0 0.4 %collective-permute-start.3 = (f32[3,8,384]{2,1,0:T(8,128)S(1)}, f32[3,8,384]{2,1,0:T(8,128)S(1)}, u32[]{:S(2)}, u32[]{:S(2)}) collective-permute-start(f32[3,8,384]{2,1,0:T(8,128)S(1)} %get-tuple-element.14), channel_id=1, source_target_pairs={{0,3},{1,0},{2,1},{3,2},{4,7},{5,4},{6,5},{7,6},{8,11},{9,8},{10,9... | collective-permute-start | bytes 110600 | tf_op jit(solution)/shard_map/ppermute | solution.py:28
  8.5 3.5 %collective-permute-done.3.right = f32[3,8,384]{2,1,0:T(8,128)S(1)} collective-permute-done((f32[3,8,384]{2,1,0:T(8,128)S(1)}, f32[3,8,384]{2,1,0:T(8,128)S(1)}, u32[]{:S(2)}, u32[]{:S(2)}) %collective-permute-start.3) | collective-permute-done | bytes 36896 | tf_op jit(solution)/shard_map/ppermute | solution.py:28
  12.0 2.8 %collective-permute-done.6.refs_2_ = f32[1,256,512]{2,1,0:T(8,128)S(1)} collective-permute-done((f32[1,256,512]{2,1,0:T(8,128)}, f32[1,256,512]{2,1,0:T(8,128)S(1)}, u32[]{:S(2)}, u32[]{:S(2)}) %collective-permute-start.6) | collective-permute-done | bytes 524320 | tf_op jit(solution)/shard_map/ppermute | solution.py:28
  14.8 1.5 %collective-permute-start.8 = (f32[1,128,512]{2,1,0:T(8,128)S(1)}, f32[1,128,512]{2,1,0:T(8,128)S(1)}, u32[]{:S(2)}, u32[]{:S(2)}) collective-permute-start(f32[1,128,512]{2,1,0:T(8,128)S(1)} %slice.80), channel_id=1, source_target_pairs={{0,16},{8,0},{24,8},{16,24},{1,17},{9,1},{25,9},{17,25},{2,18},{10... | collective-permute-start | bytes 786440 | tf_op jit(solution)/shard_map/ppermute | solution.py:28
  16.4 0.6 %collective-permute-start.9 = (f32[1,128,512]{2,1,0:T(8,128)S(1)}, f32[1,128,512]{2,1,0:T(8,128)S(1)}, u32[]{:S(2)}, u32[]{:S(2)}) collective-permute-start(f32[1,128,512]{2,1,0:T(8,128)S(1)} %slice.81), channel_id=1, source_target_pairs={{0,8},{8,24},{24,16},{16,0},{1,9},{9,25},{25,17},{17,1},{2,10},{10... | collective-permute-start | bytes 786440 | tf_op jit(solution)/shard_map/ppermute | solution.py:28
  17.0 0.6 %collective-permute-start.5 = (f32[16,896]{1,0:T(8,128)S(1)}, f32[16,896]{1,0:T(8,128)S(1)}, u32[]{:S(2)}, u32[]{:S(2)}) collective-permute-start(f32[16,896]{1,0:T(8,128)S(1)} %maximum_maximum_fusion), channel_id=1, source_target_pairs={{0,8},{8,24},{24,16},{16,0},{1,9},{9,25},{25,17},{17,1},{2,10},{10... | collective-permute-start | bytes 172040 | tf_op jit(solution)/shard_map/ppermute | solution.py:28
  17.6 1.5 %collective-permute-start.7 = (f32[16,896]{1,0:T(8,128)S(1)}, f32[16,896]{1,0:T(8,128)S(1)}, u32[]{:S(2)}, u32[]{:S(2)}) collective-permute-start(f32[16,896]{1,0:T(8,128)S(1)} %maximum_maximum_fusion), channel_id=1, source_target_pairs={{0,16},{8,0},{24,8},{16,24},{1,17},{9,1},{25,9},{17,25},{2,18},{10... | collective-permute-start | bytes 172040 | tf_op jit(solution)/shard_map/ppermute | solution.py:28
  19.1 1.4 %collective-permute-start.10 = (f32[16,896]{1,0:T(8,128)S(1)}, f32[16,896]{1,0:T(8,128)S(1)}, u32[]{:S(2)}, u32[]{:S(2)}) collective-permute-start(f32[16,896]{1,0:T(8,128)S(1)} %maximum_maximum_fusion), channel_id=1, source_target_pairs={{0,24},{8,16},{24,0},{16,8},{1,25},{9,17},{25,1},{17,9},{2,26},{10... | collective-permute-start | bytes 172040 | tf_op jit(solution)/shard_map/ppermute | solution.py:28
  20.5 1.6 %shard_map.51 = (f32[272,640]{1,0:T(8,128)S(1)}, f32[2,272,640]{2,1,0:T(8,128)S(1)}, f32[272,640]{1,0:T(8,128)S(1)}, f32[272,640]{1,0:T(8,128)S(1)}) custom-call(f32[256,512]{1,0:T(8,128)S(1)} %copy-done, f32[256,512]{1,0:T(8,128)S(1)} %copy-done.1, f32[3,8,512]{2,1,0:T(8,128)S(1)} %collective-permute-done.rows_before.before, ...), custom_call_target="tpu_custom_call" | custom-call | tf_op jit(solution)/shard_map/pallas_call | solution.py:331
  22.1 2.8 %collective-permute-done.5.refs_1_ = f32[16,896]{1,0:T(8,128)S(1)} collective-permute-done((f32[16,896]{1,0:T(8,128)S(1)}, f32[16,896]{1,0:T(8,128)S(1)}, u32[]{:S(2)}, u32[]{:S(2)}) %collective-permute-start.5) | collective-permute-done | bytes 57376 | tf_op jit(solution)/shard_map/ppermute | solution.py:28
  24.9 0.1 broadcast_in_dim.3.odd_in
  25.0 2.5 %shard_map.52 = (f32[2,272,640]{2,1,0:T(8,128)S(1)}, f32[2,272,640]{2,1,0:T(8,128)S(1)}, f32[272,640]{1,0:T(8,128)S(1)}) custom-call(f32[272,640]{1,0:T(8,128)S(1)} %get-tuple-element.15.kap, f32[2,272,640]{2,1,0:T(8,128)S(1)} %get-tuple-element.16.even_in, ...), custom_call_target="tpu_custom_call", output_to_operand_aliasing={{0}: (1, {}), {1}: (2, {}), {2}: (3, {})} | custom-call | tf_op jit(solution)/shard_map/pallas_call | solution.py:338
  27.6 3.0 %shard_map.53 = (f32[1,256,512]{2,1,0:T(8,128)}, f32[1,256,512]{2,1,0:T(8,128)}, f32[2,272,640]{2,1,0:T(8,128)S(1)}, f32[272,640]{1,0:T(8,128)S(1)}) custom-call(f32[272,640]{1,0:T(8,128)S(1)} %get-tuple-element.15.kap, f32[2,272,640]{2,1,0:T(8,128)S(1)} %get-tuple-element.18.even, ...), custom_call_target="tpu_custom_call", output_to_operand_aliasing={{2}: (2, {}), {3}: (3, {})} | custom-call | tf_op jit(solution)/shard_map/pallas_call | solution.py:342
  (22 shorter events, 0.1 us)
Async XLA Ops:
  0.6 5.4 %copy-start.2 = (f32[1,256,512]{2,1,0:T(8,128)S(1)}, f32[1,256,512]{2,1,0:T(8,128)}, u32[]{:S(2)}) copy-start(f32[1,256,512]{2,1,0:T(8,128)} %param.5) | copy-start | bytes 1572868
  0.6 15.8 %collective-permute-start.4 = (f32[1,256,512]{2,1,0:T(8,128)}, f32[1,256,512]{2,1,0:T(8,128)S(1)}, u32[]{:S(2)}, u32[]{:S(2)}) collective-permute-start(f32[1,256,512]{2,1,0:T(8,128)} %param.5), channel_id=1, source_target_pairs={{0,8},{8,24},{24,16},{16,0},{1,9},{9,25},{25,17},{17,1},{2,10},{10... | collective-permute-start | bytes 1572872 | tf_op jit(solution)/shard_map/ppermute | solution.py:28
  1.2 13.6 %collective-permute-start.6 = (f32[1,256,512]{2,1,0:T(8,128)}, f32[1,256,512]{2,1,0:T(8,128)S(1)}, u32[]{:S(2)}, u32[]{:S(2)}) collective-permute-start(f32[1,256,512]{2,1,0:T(8,128)} %param.5), channel_id=1, source_target_pairs={{0,16},{8,0},{24,8},{16,24},{1,17},{9,1},{25,9},{17,25},{2,18},{10... | collective-permute-start | bytes 1572872 | tf_op jit(solution)/shard_map/ppermute | solution.py:28
  4.3 1.8 %collective-permute-start.1 = (f32[3,8,512]{2,1,0:T(8,128)S(1)}, f32[3,8,512]{2,1,0:T(8,128)S(1)}, u32[]{:S(2)}, u32[]{:S(2)}) collective-permute-start(f32[3,8,512]{2,1,0:T(8,128)S(1)} %pad_maximum_fusion.1), channel_id=1, source_target_pairs={{0,4},{4,0},{1,5},{5,1},{2,6},{6,2},{3,7},{7,3},{8,12},{12,8},{9,1... | collective-permute-start | bytes 147464 | tf_op jit(solution)/shard_map/ppermute | solution.py:28
  4.3 1.7 %collective-permute-start = (f32[3,8,512]{2,1,0:T(8,128)S(1)}, f32[3,8,512]{2,1,0:T(8,128)S(1)}, u32[]{:S(2)}, u32[]{:S(2)}) collective-permute-start(f32[3,8,512]{2,1,0:T(8,128)S(1)} %pad_maximum_fusion), channel_id=1, source_target_pairs={{0,4},{4,0},{1,5},{5,1},{2,6},{6,2},{3,7},{7,3},{8,12},{12,8},{9,1... | collective-permute-start | bytes 147464 | tf_op jit(solution)/shard_map/ppermute | solution.py:28
  6.0 14.6 %copy-start = (f32[256,512]{1,0:T(8,128)S(1)}, f32[256,512]{1,0:T(8,128)}, u32[]{:S(2)}) copy-start(f32[256,512]{1,0:T(8,128)} %kappa.1) | copy-start | bytes 1572868
  6.0 14.5 %copy-start.1 = (f32[256,512]{1,0:T(8,128)S(1)}, f32[256,512]{1,0:T(8,128)}, u32[]{:S(2)}) copy-start(f32[256,512]{1,0:T(8,128)} %initial.1) | copy-start | bytes 1572868
  6.4 10.6 %collective-permute-start.2 = (f32[3,8,384]{2,1,0:T(8,128)S(1)}, f32[3,8,384]{2,1,0:T(8,128)S(1)}, u32[]{:S(2)}, u32[]{:S(2)}) collective-permute-start(f32[3,8,384]{2,1,0:T(8,128)S(1)} %get-tuple-element.13), channel_id=1, source_target_pairs={{0,1},{1,2},{2,3},{3,0},{4,5},{5,6},{6,7},{7,4},{8,9},{9,10},{10,1... | collective-permute-start | bytes 110600 | tf_op jit(solution)/shard_map/ppermute | solution.py:28
  8.0 4.0 %collective-permute-start.3 = (f32[3,8,384]{2,1,0:T(8,128)S(1)}, f32[3,8,384]{2,1,0:T(8,128)S(1)}, u32[]{:S(2)}, u32[]{:S(2)}) collective-permute-start(f32[3,8,384]{2,1,0:T(8,128)S(1)} %get-tuple-element.14), channel_id=1, source_target_pairs={{0,3},{1,0},{2,1},{3,2},{4,7},{5,4},{6,5},{7,6},{8,11},{9,8},{10,9... | collective-permute-start | bytes 110600 | tf_op jit(solution)/shard_map/ppermute | solution.py:28
  14.8 12.7 %collective-permute-start.8 = (f32[1,128,512]{2,1,0:T(8,128)S(1)}, f32[1,128,512]{2,1,0:T(8,128)S(1)}, u32[]{:S(2)}, u32[]{:S(2)}) collective-permute-start(f32[1,128,512]{2,1,0:T(8,128)S(1)} %slice.80), channel_id=1, source_target_pairs={{0,16},{8,0},{24,8},{16,24},{1,17},{9,1},{25,9},{17,25},{2,18},{10... | collective-permute-start | bytes 786440 | tf_op jit(solution)/shard_map/ppermute | solution.py:28
  16.4 11.2 %collective-permute-start.9 = (f32[1,128,512]{2,1,0:T(8,128)S(1)}, f32[1,128,512]{2,1,0:T(8,128)S(1)}, u32[]{:S(2)}, u32[]{:S(2)}) collective-permute-start(f32[1,128,512]{2,1,0:T(8,128)S(1)} %slice.81), channel_id=1, source_target_pairs={{0,8},{8,24},{24,16},{16,0},{1,9},{9,25},{25,17},{17,1},{2,10},{10... | collective-permute-start | bytes 786440 | tf_op jit(solution)/shard_map/ppermute | solution.py:28
  17.0 7.9 %collective-permute-start.5 = (f32[16,896]{1,0:T(8,128)S(1)}, f32[16,896]{1,0:T(8,128)S(1)}, u32[]{:S(2)}, u32[]{:S(2)}) collective-permute-start(f32[16,896]{1,0:T(8,128)S(1)} %maximum_maximum_fusion), channel_id=1, source_target_pairs={{0,8},{8,24},{24,16},{16,0},{1,9},{9,25},{25,17},{17,1},{2,10},{10... | collective-permute-start | bytes 172040 | tf_op jit(solution)/shard_map/ppermute | solution.py:28
  17.6 7.3 %collective-permute-start.7 = (f32[16,896]{1,0:T(8,128)S(1)}, f32[16,896]{1,0:T(8,128)S(1)}, u32[]{:S(2)}, u32[]{:S(2)}) collective-permute-start(f32[16,896]{1,0:T(8,128)S(1)} %maximum_maximum_fusion), channel_id=1, source_target_pairs={{0,16},{8,0},{24,8},{16,24},{1,17},{9,1},{25,9},{17,25},{2,18},{10... | collective-permute-start | bytes 172040 | tf_op jit(solution)/shard_map/ppermute | solution.py:28
  19.1 8.5 %collective-permute-start.10 = (f32[16,896]{1,0:T(8,128)S(1)}, f32[16,896]{1,0:T(8,128)S(1)}, u32[]{:S(2)}, u32[]{:S(2)}) collective-permute-start(f32[16,896]{1,0:T(8,128)S(1)} %maximum_maximum_fusion), channel_id=1, source_target_pairs={{0,24},{8,16},{24,0},{16,8},{1,25},{9,17},{25,1},{17,9},{2,26},{10... | collective-permute-start | bytes 172040 | tf_op jit(solution)/shard_map/ppermute | solution.py:28

commit v3 on v2

--- a/solution.py
+++ b/solution.py
@@ -1,4 +1,5 @@
 import functools
+import math
 import jax
 import jax.numpy as jnp
 from jax import lax
@@ -28,42 +29,68 @@
     return lax.ppermute(x, axis, [(order[i], order[(i + by) % size]) for i in range(size)])
 
 
-def call(body, outs, scratch=(), **options):
+def neighbours(axis, to_next, to_previous):
+    size, index = lax.axis_size(axis), lax.axis_index(axis)
+    even = index % 2 == 0
+    got = []
+    for start in (0, 1):
+        pairs = {i: i for i in range(size)}
+        for i in range(start, size - 1, 2):
+            pairs[i], pairs[i + 1] = i + 1, i
+        send = jnp.where(even == (start == 0), to_next, to_previous)
+        got.append(lax.ppermute(send, axis, sorted(pairs.items())))
+    from_next = jnp.where(even, got[0], got[1])
+    from_previous = jnp.where(even, got[1], got[0])
+    return from_previous, from_next
+
+
+def together(*xs):
+    return lax.optimization_barrier(xs)
+
+
+def call(body, outs, scratch=(), passes=1, semaphores=None, **options):
+    cells = sum(math.prod(s) for s in scratch[:1])
+    sems = [pltpu.SemaphoreType.DMA(semaphores)] if semaphores else []
     return pl.pallas_call(
         body,
+        cost_estimate=pl.CostEstimate(flops=16 * passes * cells, bytes_accessed=24 * passes * cells, transcendentals=0),
         out_shape=[jax.ShapeDtypeStruct(s, jnp.float32) for s in outs],
-        scratch_shapes=[pltpu.VMEM(s, jnp.float32) for s in scratch],
+        scratch_shapes=[pltpu.VMEM(s, jnp.float32) for s in scratch] + sems,
         compiler_params=pltpu.CompilerParams(vmem_limit_bytes=48 * 2**20),
         **options,
     )
 
 
-def edge_kernel(halo, rows, rows_before, rows_after, *refs):
+def cols_kernel(halo, *refs):
     fields = len(refs) // 2 - 1
-    lefts, rights = refs[:fields], refs[fields : 2 * fields]
+    firsts, lasts = refs[:fields], refs[fields : 2 * fields]
     first_out, last_out = refs[2 * fields :]
-    ix, last_ix = lax.axis_index("sx"), lax.axis_size("sx") - 1
-    length = first_out.shape[-1]
-    width = rows_before.shape[-1]
     for k in range(fields):
-        for block, out, col, lo in (
-            (lefts[k], first_out, 0, 0),
-            (rights[k], last_out, width - LANES, LANES - halo),
-        ):
-            after = rows_after[k, :, col : col + LANES]
-            before = rows_before[k, :, col : col + LANES]
+        first_out[k] = firsts[k][...].T[:halo]
+        last_out[k] = lasts[k][...].T[LANES - halo :]
+
+
+def rows_kernel(halo, first_rows, last_rows, left, right, first_out, last_out):
+    rows, width = left.shape[-1], first_rows.shape[-1]
+    iy, last_iy = lax.axis_index("sy"), lax.axis_size("sy") - 1
+    gap = jnp.zeros((LANES - 2 * halo, LANES), jnp.float32)
+    for k in range(left.shape[0]):
+        for given, out, lane, at in ((first_rows, first_out, 0, 0), (last_rows, last_out, rows - LANES, LANES - halo)):
+            after, before = right[k, :, lane : lane + LANES], left[k, :, lane : lane + LANES]
             if k == 0:
-                after = jnp.where(ix == last_ix, 0.0, after)
-                before = jnp.where(ix == 0, 0.0, before)
-            rest = jnp.zeros((length - rows - 2 * halo, LANES), jnp.float32)
-            whole = jnp.concatenate([block[...], after, before, rest], axis=0)
-            out[k] = whole.T[lo : lo + halo]
+                after, before = jnp.where(iy == last_iy, 0.0, after), jnp.where(iy == 0, 0.0, before)
+            corners = jnp.concatenate([after, gap, before], axis=0).T
+            out[k, :, :width] = given[k * halo : (k + 1) * halo]
+            out[k, :, width:] = corners[at : at + halo]
 
 
 class Grid:
-    def __init__(self, rows, width, halo):
+    def __init__(self, rows, width, halo, deep):
         self.rows, self.width, self.halo = rows, width, halo
         self.total, self.wide = rows + 2 * halo, width + LANES
+        self.deep = deep
+        self.high = round_up(2 * deep, SUBLANES)
+        self.strip = (2 * self.high, max(width, rows + LANES))
         self.ext = (self.total, self.wide)
         self.padded = (self.total + 2 * SUBLANES, self.wide)
 
@@ -71,13 +98,13 @@
         rows, halo, total, width = self.rows, self.halo, self.total, self.width
         at = 0
         for part in tile:
-            dst[at : at + part.shape[0], 0:width] = part
+            dst[at : at + part.shape[0], 0:width] = part[...]
             at += part.shape[0]
-        dst[rows : rows + halo, 0:width] = after
-        dst[rows + halo : total, 0:width] = before
-        gap = jnp.zeros((LANES - 2 * halo, left.shape[-1]), jnp.float32)
-        sides = jnp.concatenate([right, gap, left], axis=0).T
-        dst[:, width:] = sides[:total]
+        open_rows = 2 * halo - before.shape[0] - after.shape[0]
+        gap = [jnp.zeros((open_rows, self.wide), jnp.float32)] if open_rows else []
+        dst[rows:total, :] = jnp.concatenate([after, *gap, before], axis=0)
+        gap = jnp.zeros((LANES - left.shape[0] - right.shape[0], rows), jnp.float32)
+        dst[0:rows, width:] = jnp.concatenate([right, gap, left], axis=0).T
 
     def over(self, body, dst=None):
         total = self.total
@@ -166,11 +193,11 @@
     ix, last_ix = lax.axis_index("sx"), lax.axis_size("sx") - 1
     iy, last_iy = lax.axis_index("sy"), lax.axis_size("sy") - 1
     grid.fill(
-        kap, [kappa[...]],
+        kap, [kappa],
         jnp.where(ix == 0, 0.0, before[0]), jnp.where(ix == last_ix, 0.0, after[0]),
         jnp.where(iy == 0, 0.0, left[0]), jnp.where(iy == last_iy, 0.0, right[0]),
     )
-    grid.fill(wk, [initial[...]], before[1], after[1], left[1], right[1])
+    grid.fill(wk, [initial], before[1], after[1], left[1], right[1])
 
     def out(at, g):
         x, lx = wk[at, :], lap_w[at, :]
@@ -185,19 +212,17 @@
     grid.second_part(wk, mid, lap_w, fa, out_even)
 
 
-def arrival(grid, index, away, tile, strip, kap, here_pos, order, even, odd, tail, work):
+def arrival(grid, away, tile, strip, kap, order, even, odd, tail, work):
     count = len(order)
     here, point = lax.axis_index("tm"), jnp.int32(count)
     for p in range(count):
         point = jnp.where(here == order[p], order[(p - away) % count] + 1, point)
 
     def load(wk):
-        halo, width = grid.halo, grid.width
-        strips = strip[...]
-        grid.fill(
-            wk, [t[0] for t in tile],
-            strips[:halo, :width], strips[halo:, :width], strips[:halo, width:], strips[halo:, width:],
-        )
+        rows, width, deep, high = grid.rows, grid.width, grid.deep, grid.high
+        edge = jnp.concatenate([strip[: 2 * deep, :width], strip[high : high + 2 * deep, rows : rows + LANES]], axis=1)
+        cols = strip[high : high + 2 * deep, :rows]
+        grid.fill(wk, tile, edge[deep:], edge[:deep], cols[deep:], cols[:deep])
 
     @pl.when(point <= here)
     def _():
@@ -205,11 +230,10 @@
 
 
 def middle_kernel(grid, order, aways, kap, even_in, odd_in, tail_in, *refs):
-    pairs = [refs[2 * i : 2 * i + 2] for i in range(len(aways))]
-    even, odd, tail = refs[2 * len(aways) : 2 * len(aways) + 3]
-    work = refs[2 * len(aways) + 3 :]
-    for away, (tile, strip) in zip(aways, pairs):
-        arrival(grid, None, away, [tile], strip, kap, None, order, even, odd, tail, work)
+    given, refs = refs[: 2 * len(aways)], refs[2 * len(aways) :]
+    even, odd, tail = refs[:3]
+    for i, away in enumerate(aways):
+        arrival(grid, away, [given[2 * i]], given[2 * i + 1], kap, order, even, odd, tail, refs[3:])
 
 
 def last_kernel(grid, order, kap, even, odd_in, tail_in, low, first, second, strip, c_out, f_out, odd, tail, *work):
@@ -217,8 +241,7 @@
     count = len(order)
     here = lax.axis_index("tm")
     rows, width = grid.rows, grid.width
-    if count > 1:
-        arrival(grid, None, count // 2, [first, second], strip, kap, None, order, even, odd, tail, work)
+    arrival(grid, count // 2, [first, second], strip, kap, order, even, odd, tail, work)
     state = wk
 
     def put(dst, at, value):
@@ -295,54 +318,75 @@
 def on_device(initial, kappa, c_guess):
     count = lax.axis_size("tm")
     rows, width = initial.shape
-    halo = round_up(count // 2 + 3, SUBLANES)
-    grid = Grid(rows, width, halo)
+    steps = count // 2
+    halo, deep = round_up(steps + 3, SUBLANES), steps + 2
+    grid = Grid(rows, width, halo, deep)
     order = ring("tm", gray=True)
-    sx, sy = ring("sx"), ring("sy")
+    sx = ring("sx")
     middle = rows // 2
-
-    tiles = {}
-    onward, backward = c_guess, c_guess
-    for s in range(1, count // 2):
-        onward, backward = shift(onward, "tm", order, 1), shift(backward, "tm", order, -1)
-        tiles[s], tiles[count - s] = onward, backward
-    second = shift(onward[:, middle:], "tm", order, 1)
-    first = shift(backward[:, :middle], "tm", order, -1)
-
-    fields = (kappa, initial, c_guess[0])
-    before = shift(jnp.stack([x[rows - halo :] for x in fields]), "sx", sx, 1)
-    after = shift(jnp.stack([x[:halo] for x in fields]), "sx", sx, -1)
-    length = round_up(grid.total, LANES)
-    packed = (len(fields), halo, length)
-    first_cols, last_cols = call(functools.partial(edge_kernel, halo, rows), [packed] * 2)(
-        before, after, *[x[:, :LANES] for x in fields], *[x[:, width - LANES :] for x in fields]
-    )
-    left = shift(last_cols, "sy", sy, 1)
-    right = shift(first_cols, "sy", sy, -1)
-
-    strip = jnp.concatenate(
-        [jnp.concatenate([before[2], after[2]], axis=0), jnp.concatenate([left[2], right[2]], axis=0)], axis=1
-    )
-    strips = {s: shift(strip, "tm", order, s) for s in range(1, count)}
-
     ext, padded = grid.ext, grid.padded
     work = [ext] * 3 + [padded] * 2
-    sides = (count // 2, *ext)
-    kap, even, tail, low = call(functools.partial(start_kernel, grid), [ext, sides, ext, ext], work)(
+    sides = (steps, *ext)
+
+    tiles, strips = {}, {}
+    if steps > 1:
+        for s in (1, -1):
+            tiles[s] = shift(c_guess, "tm", order, s)[0]
+
+    fields = (kappa, initial, c_guess[0])
+    packed = (len(fields), halo, rows)
+    first_cols, last_cols = call(functools.partial(cols_kernel, halo), [packed] * 2)(
+        *[x[:, :LANES] for x in fields], *[x[:, width - LANES :] for x in fields]
+    )
+    left, right = neighbours("sy", last_cols, first_cols)
+    packed = (len(fields), halo, grid.wide)
+    first_rows, last_rows = call(functools.partial(rows_kernel, halo), [packed] * 2)(
+        jnp.concatenate([x[:halo] for x in fields], axis=0),
+        jnp.concatenate([x[rows - halo :] for x in fields], axis=0),
+        left, right,
+    )
+    before, after = shift(last_rows, "sx", sx, 1), shift(first_rows, "sx", sx, -1)
+
+    def padded_to(x, shape):
+        return jnp.pad(x, [(0, n - m) for m, n in zip(x.shape, shape)])
+
+    part = (grid.high, grid.strip[1])
+    edge = jnp.concatenate([after[2, :deep], before[2, halo - deep :]], axis=0)
+    cols = jnp.concatenate([right[2, :deep], left[2, halo - deep :]], axis=0)
+    strip = jnp.concatenate(
+        [padded_to(edge[:, :width], part), padded_to(jnp.concatenate([cols, edge[:, width:]], axis=1), part)], axis=0
+    )
+    if steps > 1:
+        for s in (1, -1):
+            strips[s] = shift(strip, "tm", order, s)
+
+    before, strip = together(before, strip)
+    kap, even, tail, low = call(functools.partial(start_kernel, grid), [ext, sides, ext, ext], work, 4)(
         kappa, initial, before, after, left, right
     )
     odd = jnp.zeros(sides, jnp.float32)
-    for s in range(1, count // 2):
-        aways = sorted({s, count - s})
-        pairs = [x for a in aways for x in (tiles[a], strips[a])]
+
+    if steps == 1:
+        tiles, strips = {1: c_guess[0], -1: c_guess[0]}, {1: strip}
+    for s in range(1, steps):
+        given = [x for way in (1, -1) for x in (tiles[way], strips[way])]
+        strips = {way: shift(x, "tm", order, way) for way, x in strips.items() if s + 1 < steps or way == 1}
+        if s + 1 < steps:
+            tiles = {way: shift(x, "tm", order, way) for way, x in tiles.items()}
+        else:
+            second = shift(tiles[1][middle:], "tm", order, 1)
+            first = shift(tiles[-1][:middle], "tm", order, -1)
         even, odd, tail = call(
-            functools.partial(middle_kernel, grid, order, aways), [sides, sides, ext], work,
+            functools.partial(middle_kernel, grid, order, (s, count - s)), [sides, sides, ext], work, 1000,
             input_output_aliases={1: 0, 2: 1, 3: 2},
-        )(kap, even, odd, tail, *pairs)
+        )(kap, even, odd, tail, *given)
+    if steps == 1:
+        second, first = shift(tiles[1][middle:], "tm", order, 1), shift(tiles[-1][:middle], "tm", order, -1)
+        strips = {1: shift(strip, "tm", order, 1)}
     c_new, f_new, _, _ = call(
-        functools.partial(last_kernel, grid, order), [c_guess.shape] * 2 + [sides, ext], work,
+        functools.partial(last_kernel, grid, order), [c_guess.shape] * 2 + [sides, ext], work, 8,
         input_output_aliases={2: 2, 3: 3},
-    )(kap, even, odd, tail, low, first, second, strips[count // 2])
+    )(kap, even, odd, tail, low, first, second, strips[1])
     return c_new, f_new
 
 

time: 31 us -> 29.2 us (0.942)
  the two profiles are of different devices: /device:TPU:14 before, /device:TPU:12 now
where the time goes in v3:
time: 29.2 us; the launch traced here: 28.9 us
  starting transfers between devices  11 us (38%)
  waiting for transfers between devices  8.51 us (29%)
  Pallas kernels  5.57 us (19%)
  local copies, waits for them, and re-layouts  3.04 us (10%)
  between operations  0.81 us (3%)
    ppermute x9, starting transfers between devices, shift(): lax.ppermute(x, axis, [(order[i], order[(i + by) % size]) for i in range(...  7.4 us
    ppermute x9, waiting for transfers between devices, shift(): lax.ppermute(x, axis, [(order[i], order[(i + by) % size]) for i in range(...  5.5 us
    ppermute x2, starting transfers between devices, neighbours(): got.append(lax.ppermute(send, axis, sorted(pairs.items())))  3.56 us
    ppermute x2, waiting for transfers between devices, neighbours(): got.append(lax.ppermute(send, axis, sorted(pairs.items())))  3.01 us
    pallas_call x1, Pallas kernels, on_device(): call(functools.partial(last_kernel, grid, order), [c_guess.shape] * 2 + [...  2.55 us
    slice x2, local copies, waits for them, and re-layouts, on_device(): x[:, width - LANES:]  2.13 us
    pallas_call x1, Pallas kernels, on_device(): call(functools.partial(start_kernel, grid), [ext, sides, ext, ext], work, 4)  1.55 us
    pallas_call x1, Pallas kernels, on_device(): call(functools.partial(middle_kernel, grid, order, (s, count - s)), [side...  1.07 us
  transfers between devices with their start and end apart: 11, of which 5 were waited for; matrix products, arithmetic and copies ran while one was open for 11% of the time, Pallas kernels for 10%

profile of v3, /device:TPU:12, one launch (start us, length us, event | category | flops | bytes accessed | tf_op | source)
XLA Modules:
  0.0 28.9 jit_solution(392161163686090057)
XLA Ops:
  0.7 0.6 %collective-permute-start.4 = (f32[1,256,512]{2,1,0:T(8,128)}, f32[1,256,512]{2,1,0:T(8,128)S(1)}, u32[]{:S(2)}, u32[]{:S(2)}) collective-permute-start(f32[1,256,512]{2,1,0:T(8,128)} %param.5), channel_id=1, source_target_pairs={{0,8},{8,24},{24,16},{16,0},{1,9},{9,25},{25,17},{17,1},{2,10},{10... | collective-permute-start | bytes 1572872 | tf_op jit(solution)/shard_map/ppermute | solution.py:29
  1.2 1.5 %collective-permute-start.6 = (f32[1,256,512]{2,1,0:T(8,128)}, f32[1,256,512]{2,1,0:T(8,128)S(1)}, u32[]{:S(2)}, u32[]{:S(2)}) collective-permute-start(f32[1,256,512]{2,1,0:T(8,128)} %param.5), channel_id=1, source_target_pairs={{0,16},{8,0},{24,8},{16,24},{1,17},{9,1},{25,9},{17,25},{2,18},{10... | collective-permute-start | bytes 1572872 | tf_op jit(solution)/shard_map/ppermute | solution.py:29
  2.7 1.0 %fusion.2 = (f32[256,128]{1,0:T(8,128)S(1)}, f32[256,128]{1,0:T(8,128)S(1)}) fusion(f32[256,512]{1,0:T(8,128)} %bitcast.21), kind=kLoop, calls=%fused_computation.22 | loop fusion | bytes 524288 | tf_op jit(solution)/shard_map/slice | solution.py:339
  3.7 1.1 %fusion.3 = (f32[256,128]{1,0:T(8,128)S(1)}, f32[256,128]{1,0:T(8,128)S(1)}, f32[256,128]{1,0:T(8,128)S(1)}, f32[256,128]{1,0:T(8,128)S(1)}) fusion(f32[256,512]{1,0:T(8,128)} %initial.1, f32[256,512]{1,0:T(8,128)} %kappa.1), kind=kLoop, calls=%fused_computation.23 | loop fusion | bytes 1048576 | tf_op jit(solution)/shard_map/slice | solution.py:339
  4.9 0.3 shard_map.50
  5.2 3.5 %collective-permute-start = (f32[3,8,256]{2,1,0:T(8,128)S(1)}, f32[3,8,256]{2,1,0:T(8,128)S(1)}, u32[]{:S(2)}, u32[]{:S(2)}) collective-permute-start(f32[3,8,256]{2,1,0:T(8,128)S(1)} %get-tuple-element.45), channel_id=1, source_target_pairs={{0,0},{1,2},{2,1},{3,3},{4,4},{5,6},{6,5},{7,7},{8,8},{9,10},{10,9... | collective-permute-start | bytes 73736 | tf_op jit(solution)/shard_map/ppermute | solution.py:41
  8.7 0.1 collective-permute-start.1
  8.8 0.7 %slice_bitcast_fusion.2 = (f32[8,512]{1,0:T(8,128)S(1)}, f32[8,512]{1,0:T(8,128)S(1)}) fusion(f32[1,256,512]{2,1,0:T(8,128)} %param.5), kind=kLoop, calls=%fused_computation.9 | loop fusion | bytes 65536 | tf_op jit(solution)/shard_map/slice | solution.py:345
  9.5 1.4 %collective-permute-done = f32[3,8,256]{2,1,0:T(8,128)S(1)} collective-permute-done((f32[3,8,256]{2,1,0:T(8,128)S(1)}, f32[3,8,256]{2,1,0:T(8,128)S(1)}, u32[]{:S(2)}, u32[]{:S(2)}) %collective-permute-start) | collective-permute-done | bytes 24608 | tf_op jit(solution)/shard_map/ppermute | solution.py:41
  10.9 1.7 %collective-permute-done.1 = f32[3,8,256]{2,1,0:T(8,128)S(1)} collective-permute-done((f32[3,8,256]{2,1,0:T(8,128)S(1)}, f32[3,8,256]{2,1,0:T(8,128)S(1)}, u32[]{:S(2)}, u32[]{:S(2)}) %collective-permute-start.1) | collective-permute-done | bytes 24608 | tf_op jit(solution)/shard_map/ppermute | solution.py:41
  12.6 0.1 shard_map.51
  12.8 0.5 %collective-permute-start.3 = (f32[3,8,640]{2,1,0:T(8,128)S(1)}, f32[3,8,640]{2,1,0:T(8,128)S(1)}, u32[]{:S(2)}, u32[]{:S(2)}) collective-permute-start(f32[3,8,640]{2,1,0:T(8,128)S(1)} %get-tuple-element.19), channel_id=1, source_target_pairs={{0,4},{4,0},{1,5},{5,1},{2,6},{6,2},{3,7},{7,3},{8,12},{12,8},{9,1... | collective-permute-start | bytes 184328 | tf_op jit(solution)/shard_map/ppermute | solution.py:29
  13.3 0.7 %collective-permute-done.2.before = f32[3,8,640]{2,1,0:T(8,128)S(1)} collective-permute-done((f32[3,8,640]{2,1,0:T(8,128)S(1)}, f32[3,8,640]{2,1,0:T(8,128)S(1)}, u32[]{:S(2)}, u32[]{:S(2)}) %collective-permute-start.2) | collective-permute-done | bytes 61472 | tf_op jit(solution)/shard_map/ppermute | solution.py:29
  14.0 0.2 collective-permute-done.3.after
  14.2 0.6 %collective-permute-start.5 = (f32[16,512]{1,0:T(8,128)S(1)}, f32[16,512]{1,0:T(8,128)S(1)}, u32[]{:S(2)}, u32[]{:S(2)}) collective-permute-start(f32[16,512]{1,0:T(8,128)S(1)} %select_maximum_fusion), channel_id=1, source_target_pairs={{0,8},{8,24},{24,16},{16,0},{1,9},{9,25},{25,17},{17,1},{2,10},{10... | collective-permute-start | bytes 98312 | tf_op jit(solution)/shard_map/ppermute | solution.py:29
  14.8 1.5 %collective-permute-start.7 = (f32[16,512]{1,0:T(8,128)S(1)}, f32[16,512]{1,0:T(8,128)S(1)}, u32[]{:S(2)}, u32[]{:S(2)}) collective-permute-start(f32[16,512]{1,0:T(8,128)S(1)} %select_maximum_fusion), channel_id=1, source_target_pairs={{0,16},{8,0},{24,8},{16,24},{1,17},{9,1},{25,9},{17,25},{2,18},{10... | collective-permute-start | bytes 98312 | tf_op jit(solution)/shard_map/ppermute | solution.py:29
  16.3 1.6 %collective-permute-start.8 = (f32[128,512]{1,0:T(8,128)S(1)}, f32[128,512]{1,0:T(8,128)S(1)}, u32[]{:S(2)}, u32[]{:S(2)}) collective-permute-start(f32[128,512]{1,0:T(8,128)S(1)} %slice_bitcast_fusion.1), channel_id=1, source_target_pairs={{0,16},{8,0},{24,8},{16,24},{1,17},{9,1},{25,9},{17,25},{2,18},{10... | collective-permute-start | bytes 786440 | tf_op jit(solution)/shard_map/ppermute | solution.py:29
  17.9 0.6 %collective-permute-start.9 = (f32[128,512]{1,0:T(8,128)S(1)}, f32[128,512]{1,0:T(8,128)S(1)}, u32[]{:S(2)}, u32[]{:S(2)}) collective-permute-start(f32[128,512]{1,0:T(8,128)S(1)} %slice_bitcast_fusion), channel_id=1, source_target_pairs={{0,8},{8,24},{24,16},{16,0},{1,9},{9,25},{25,17},{17,1},{2,10},{10... | collective-permute-start | bytes 786440 | tf_op jit(solution)/shard_map/ppermute | solution.py:29
  18.5 1.6 %shard_map.52 = (f32[272,640]{1,0:T(8,128)S(1)}, f32[2,272,640]{2,1,0:T(8,128)S(1)}, f32[272,640]{1,0:T(8,128)S(1)}, f32[272,640]{1,0:T(8,128)S(1)}) custom-call(f32[256,512]{1,0:T(8,128)S(1)} %copy-done, f32[256,512]{1,0:T(8,128)S(1)} %copy-done.1, f32[3,8,640]{2,1,0:T(8,128)S(1)} %collective-permute-done.2.before, ...), custom_call_target="tpu_custom_call" | custom-call | flops 11141120 | bytes 16711680 | tf_op jit(solution)/shard_map/pallas_call | solution.py:364
  20.1 0.6 %collective-permute-start.10 = (f32[16,512]{1,0:T(8,128)S(1)}, f32[16,512]{1,0:T(8,128)S(1)}, u32[]{:S(2)}, u32[]{:S(2)}) collective-permute-start(f32[16,512]{1,0:T(8,128)S(1)} %collective-permute-done.5.refs_1_), channel_id=1, source_target_pairs={{0,8},{8,24},{24,16},{16,0},{1,9},{9,25},{25,17},{17,1},{2,10},{10... | collective-permute-start | bytes 98312 | tf_op jit(solution)/shard_map/ppermute | solution.py:29
  20.6 0.1 broadcast_in_dim.3.odd_in
  20.7 1.1 %shard_map.53 = (f32[2,272,640]{2,1,0:T(8,128)S(1)}, f32[2,272,640]{2,1,0:T(8,128)S(1)}, f32[272,640]{1,0:T(8,128)S(1)}) custom-call(f32[272,640]{1,0:T(8,128)S(1)} %get-tuple-element.21.kap, f32[2,272,640]{2,1,0:T(8,128)S(1)} %get-tuple-element.22.even_in, ...), custom_call_target="tpu_custom_call", output_to_operand_aliasing={{0}: (1, {}), {1}: (2, {}), {2}: (3, {})} | custom-call | flops 2785280000 | bytes 4177920000 | tf_op jit(solution)/shard_map/pallas_call | solution.py:379
  21.8 4.6 %collective-permute-done.10.strip = f32[16,512]{1,0:T(8,128)S(1)} collective-permute-done((f32[16,512]{1,0:T(8,128)S(1)}, f32[16,512]{1,0:T(8,128)S(1)}, u32[]{:S(2)}, u32[]{:S(2)}) %collective-permute-start.10) | collective-permute-done | bytes 32800 | tf_op jit(solution)/shard_map/ppermute | solution.py:29
  26.4 2.5 %shard_map.54 = (f32[1,256,512]{2,1,0:T(8,128)}, f32[1,256,512]{2,1,0:T(8,128)}, f32[2,272,640]{2,1,0:T(8,128)S(1)}, f32[272,640]{1,0:T(8,128)S(1)}) custom-call(f32[272,640]{1,0:T(8,128)S(1)} %get-tuple-element.21.kap, f32[2,272,640]{2,1,0:T(8,128)S(1)} %get-tuple-element.24.even, ...), custom_call_target="tpu_custom_call", output_to_operand_aliasing={{2}: (2, {}), {3}: (3, {})} | custom-call | flops 22282240 | bytes 33423360 | tf_op jit(solution)/shard_map/pallas_call | solution.py:386
  (25 shorter events, 0.2 us)
Async XLA Ops:
  0.6 8.1 %copy-start.1 = (f32[256,512]{1,0:T(8,128)S(1)}, f32[256,512]{1,0:T(8,128)}, u32[]{:S(2)}) copy-start(f32[256,512]{1,0:T(8,128)} %initial.1) | copy-start | bytes 1572868
  0.6 8.1 %copy-start = (f32[256,512]{1,0:T(8,128)S(1)}, f32[256,512]{1,0:T(8,128)}, u32[]{:S(2)}) copy-start(f32[256,512]{1,0:T(8,128)} %kappa.1) | copy-start | bytes 1572868
  0.7 17.3 %collective-permute-start.4 = (f32[1,256,512]{2,1,0:T(8,128)}, f32[1,256,512]{2,1,0:T(8,128)S(1)}, u32[]{:S(2)}, u32[]{:S(2)}) collective-permute-start(f32[1,256,512]{2,1,0:T(8,128)} %param.5), channel_id=1, source_target_pairs={{0,8},{8,24},{24,16},{16,0},{1,9},{9,25},{25,17},{17,1},{2,10},{10... | collective-permute-start | bytes 1572872 | tf_op jit(solution)/shard_map/ppermute | solution.py:29
  1.2 15.1 %collective-permute-start.6 = (f32[1,256,512]{2,1,0:T(8,128)}, f32[1,256,512]{2,1,0:T(8,128)S(1)}, u32[]{:S(2)}, u32[]{:S(2)}) collective-permute-start(f32[1,256,512]{2,1,0:T(8,128)} %param.5), channel_id=1, source_target_pairs={{0,16},{8,0},{24,8},{16,24},{1,17},{9,1},{25,9},{17,25},{2,18},{10... | collective-permute-start | bytes 1572872 | tf_op jit(solution)/shard_map/ppermute | solution.py:29
  5.2 5.7 %collective-permute-start = (f32[3,8,256]{2,1,0:T(8,128)S(1)}, f32[3,8,256]{2,1,0:T(8,128)S(1)}, u32[]{:S(2)}, u32[]{:S(2)}) collective-permute-start(f32[3,8,256]{2,1,0:T(8,128)S(1)} %get-tuple-element.45), channel_id=1, source_target_pairs={{0,0},{1,2},{2,1},{3,3},{4,4},{5,6},{6,5},{7,7},{8,8},{9,10},{10,9... | collective-permute-start | bytes 73736 | tf_op jit(solution)/shard_map/ppermute | solution.py:41
  8.7 3.9 %collective-permute-start.1 = (f32[3,8,256]{2,1,0:T(8,128)S(1)}, f32[3,8,256]{2,1,0:T(8,128)S(1)}, u32[]{:S(2)}, u32[]{:S(2)}) collective-permute-start(f32[3,8,256]{2,1,0:T(8,128)S(1)} %get-tuple-element.44), channel_id=1, source_target_pairs={{0,1},{1,0},{2,3},{3,2},{4,5},{5,4},{6,7},{7,6},{8,9},{9,8},{10,11... | collective-permute-start | bytes 73736 | tf_op jit(solution)/shard_map/ppermute | solution.py:41
  12.7 1.3 %collective-permute-start.2 = (f32[3,8,640]{2,1,0:T(8,128)S(1)}, f32[3,8,640]{2,1,0:T(8,128)S(1)}, u32[]{:S(2)}, u32[]{:S(2)}) collective-permute-start(f32[3,8,640]{2,1,0:T(8,128)S(1)} %get-tuple-element.18), channel_id=1, source_target_pairs={{0,4},{4,0},{1,5},{5,1},{2,6},{6,2},{3,7},{7,3},{8,12},{12,8},{9,1... | collective-permute-start | bytes 184328 | tf_op jit(solution)/shard_map/ppermute | solution.py:29
  12.8 1.4 %collective-permute-start.3 = (f32[3,8,640]{2,1,0:T(8,128)S(1)}, f32[3,8,640]{2,1,0:T(8,128)S(1)}, u32[]{:S(2)}, u32[]{:S(2)}) collective-permute-start(f32[3,8,640]{2,1,0:T(8,128)S(1)} %get-tuple-element.19), channel_id=1, source_target_pairs={{0,4},{4,0},{1,5},{5,1},{2,6},{6,2},{3,7},{7,3},{8,12},{12,8},{9,1... | collective-permute-start | bytes 184328 | tf_op jit(solution)/shard_map/ppermute | solution.py:29
  14.2 5.8 %collective-permute-start.5 = (f32[16,512]{1,0:T(8,128)S(1)}, f32[16,512]{1,0:T(8,128)S(1)}, u32[]{:S(2)}, u32[]{:S(2)}) collective-permute-start(f32[16,512]{1,0:T(8,128)S(1)} %select_maximum_fusion), channel_id=1, source_target_pairs={{0,8},{8,24},{24,16},{16,0},{1,9},{9,25},{25,17},{17,1},{2,10},{10... | collective-permute-start | bytes 98312 | tf_op jit(solution)/shard_map/ppermute | solution.py:29
  14.8 5.8 %collective-permute-start.7 = (f32[16,512]{1,0:T(8,128)S(1)}, f32[16,512]{1,0:T(8,128)S(1)}, u32[]{:S(2)}, u32[]{:S(2)}) collective-permute-start(f32[16,512]{1,0:T(8,128)S(1)} %select_maximum_fusion), channel_id=1, source_target_pairs={{0,16},{8,0},{24,8},{16,24},{1,17},{9,1},{25,9},{17,25},{2,18},{10... | collective-permute-start | bytes 98312 | tf_op jit(solution)/shard_map/ppermute | solution.py:29
  16.3 10.0 %collective-permute-start.8 = (f32[128,512]{1,0:T(8,128)S(1)}, f32[128,512]{1,0:T(8,128)S(1)}, u32[]{:S(2)}, u32[]{:S(2)}) collective-permute-start(f32[128,512]{1,0:T(8,128)S(1)} %slice_bitcast_fusion.1), channel_id=1, source_target_pairs={{0,16},{8,0},{24,8},{16,24},{1,17},{9,1},{25,9},{17,25},{2,18},{10... | collective-permute-start | bytes 786440 | tf_op jit(solution)/shard_map/ppermute | solution.py:29
  17.9 8.5 %collective-permute-start.9 = (f32[128,512]{1,0:T(8,128)S(1)}, f32[128,512]{1,0:T(8,128)S(1)}, u32[]{:S(2)}, u32[]{:S(2)}) collective-permute-start(f32[128,512]{1,0:T(8,128)S(1)} %slice_bitcast_fusion), channel_id=1, source_target_pairs={{0,8},{8,24},{24,16},{16,0},{1,9},{9,25},{25,17},{17,1},{2,10},{10... | collective-permute-start | bytes 786440 | tf_op jit(solution)/shard_map/ppermute | solution.py:29
  20.1 6.3 %collective-permute-start.10 = (f32[16,512]{1,0:T(8,128)S(1)}, f32[16,512]{1,0:T(8,128)S(1)}, u32[]{:S(2)}, u32[]{:S(2)}) collective-permute-start(f32[16,512]{1,0:T(8,128)S(1)} %collective-permute-done.5.refs_1_), channel_id=1, source_target_pairs={{0,8},{8,24},{24,16},{16,0},{1,9},{9,25},{25,17},{17,1},{2,10},{10... | collective-permute-start | bytes 98312 | tf_op jit(solution)/shard_map/ppermute | solution.py:29

commit v4 on v3

--- a/solution.py
+++ b/solution.py
@@ -10,23 +10,16 @@
 LANES = 128
 SUBLANES = 8
 BLOCK = 16
+SHARE = 7 / 16
+MIDDLE = 405
 
 
 def round_up(value, step):
     return -(-value // step) * step
 
 
-def ring(axis, gray=False):
-    size = lax.axis_size(axis)
-    order = list(range(size))
-    if gray and size & (size - 1) == 0:
-        order = [i ^ (i >> 1) for i in order]
-    return order
-
-
-def shift(x, axis, order, by):
-    size = len(order)
-    return lax.ppermute(x, axis, [(order[i], order[(i + by) % size]) for i in range(size)])
+def swap(x, axis, bits):
+    return lax.ppermute(x, axis, [(i, i ^ bits) for i in range(lax.axis_size(axis))])
 
 
 def neighbours(axis, to_next, to_previous):
@@ -38,7 +31,7 @@
         for i in range(start, size - 1, 2):
             pairs[i], pairs[i + 1] = i + 1, i
         send = jnp.where(even == (start == 0), to_next, to_previous)
-        got.append(lax.ppermute(send, axis, sorted(pairs.items())))
+        got.append(lax.ppermute(send, axis, sorted(pairs.items())) if size > start + 1 else send)
     from_next = jnp.where(even, got[0], got[1])
     from_previous = jnp.where(even, got[1], got[0])
     return from_previous, from_next
@@ -94,17 +87,28 @@
         self.ext = (self.total, self.wide)
         self.padded = (self.total + 2 * SUBLANES, self.wide)
 
-    def fill(self, dst, tile, before, after, left, right):
+    def fill(self, dst, tile, before, after, left, right, kap=None, flux=None):
         rows, halo, total, width = self.rows, self.halo, self.total, self.width
-        at = 0
-        for part in tile:
-            dst[at : at + part.shape[0], 0:width] = part[...]
-            at += part.shape[0]
         open_rows = 2 * halo - before.shape[0] - after.shape[0]
         gap = [jnp.zeros((open_rows, self.wide), jnp.float32)] if open_rows else []
         dst[rows:total, :] = jnp.concatenate([after, *gap, before], axis=0)
         gap = jnp.zeros((LANES - left.shape[0] - right.shape[0], rows), jnp.float32)
         dst[0:rows, width:] = jnp.concatenate([right, gap, left], axis=0).T
+        parts, start = [], 0
+        for part in tile:
+            parts.append((start, start + part.shape[0], part))
+            start += part.shape[0]
+
+        def body(at):
+            for first, stop, part in parts:
+                lo, hi = max(at.start, first), min(at.stop, stop)
+                if lo < hi:
+                    dst[lo:hi, 0:width] = part[lo - first : hi - first, :]
+            if flux is not None:
+                v = dst[at, :]
+                return kap[at, :] * v * v
+
+        self.over(body, flux)
 
     def over(self, body, dst=None):
         total = self.total
@@ -134,8 +138,7 @@
 
         self.over(body, dst)
 
-    def first_part(self, kap, w, mid, lap_w, fa, fb, out):
-        self.flux(kap, w, fa)
+    def first_part(self, kap, w, mid, lap_w, fa, fb, out, more=True, fc=None):
 
         def one(at):
             lw = self.lap(fa, at)
@@ -148,11 +151,12 @@
 
         def two(at):
             v = mid[at, :] + self.lap(fb, at)
-            mid[at, :] = v
-            out(at, (v - w[at, :]) - 2.0 * lap_w[at, :])
-            return kap[at, :] * v * v
-
-        self.over(two, fa)
+            if more:
+                mid[at, :] = v
+            value = out(at, (v - w[at, :]) - 2.0 * lap_w[at, :])
+            return kap[at, :] * v * v if more else value
+
+        self.over(two, fa if more else fc)
 
     def second_part(self, w, mid, lap_w, fa, out):
         def one(at):
@@ -162,9 +166,9 @@
         self.over(one)
 
 
-def absorb(grid, kap, point, here, load, even, odd, tail, work):
+def absorb(grid, kap, point, here, load, even, odd, tail, work, own_only=False):
     wk, mid, lap_w, fa, fb = work
-    load(wk)
+    load(wk, fa)
     step = lax.div(point, 2)
 
     @pl.when(lax.rem(point, 2) == 1)
@@ -172,14 +176,16 @@
         def out(at, g):
             odd[step, at, :] = g
 
-        grid.first_part(kap, wk, mid, lap_w, fa, fb, out)
+        grid.first_part(kap, wk, mid, lap_w, fa, fb, out, False)
 
     @pl.when(lax.rem(point, 2) == 0)
     def _():
         def out(at, g):
             tail[at, :] = g
 
-        grid.first_part(kap, wk, mid, lap_w, fa, fb, out)
+        grid.first_part(kap, wk, mid, lap_w, fa, fb, out, not own_only)
+        if own_only:
+            return
 
         @pl.when(point < here)
         def _():
@@ -197,7 +203,7 @@
         jnp.where(ix == 0, 0.0, before[0]), jnp.where(ix == last_ix, 0.0, after[0]),
         jnp.where(iy == 0, 0.0, left[0]), jnp.where(iy == last_iy, 0.0, right[0]),
     )
-    grid.fill(wk, [initial], before[1], after[1], left[1], right[1])
+    grid.fill(wk, [initial], before[1], after[1], left[1], right[1], kap, fa)
 
     def out(at, g):
         x, lx = wk[at, :], lap_w[at, :]
@@ -212,77 +218,104 @@
     grid.second_part(wk, mid, lap_w, fa, out_even)
 
 
-def arrival(grid, away, tile, strip, kap, order, even, odd, tail, work):
-    count = len(order)
-    here, point = lax.axis_index("tm"), jnp.int32(count)
-    for p in range(count):
-        point = jnp.where(here == order[p], order[(p - away) % count] + 1, point)
-
-    def load(wk):
+def loader(grid, kap, tile, strip):
+    def load(wk, flux):
         rows, width, deep, high = grid.rows, grid.width, grid.deep, grid.high
         edge = jnp.concatenate([strip[: 2 * deep, :width], strip[high : high + 2 * deep, rows : rows + LANES]], axis=1)
         cols = strip[high : high + 2 * deep, :rows]
-        grid.fill(wk, tile, edge[deep:], edge[:deep], cols[deep:], cols[:deep])
+        grid.fill(wk, tile, edge[deep:], edge[:deep], cols[deep:], cols[:deep], kap, flux)
+
+    return load
+
+
+def middle_kernel(grid, bits, kap, even_in, odd_in, tail_in, tile, strip, even, odd, tail, *work):
+    here = lax.axis_index("tm")
+    point = (here ^ bits) + 1
 
     @pl.when(point <= here)
     def _():
-        absorb(grid, kap, point, here, load, even, odd, tail, work)
-
-
-def middle_kernel(grid, order, aways, kap, even_in, odd_in, tail_in, *refs):
-    given, refs = refs[: 2 * len(aways)], refs[2 * len(aways) :]
-    even, odd, tail = refs[:3]
-    for i, away in enumerate(aways):
-        arrival(grid, away, [given[2 * i]], given[2 * i + 1], kap, order, even, odd, tail, refs[3:])
-
-
-def last_kernel(grid, order, kap, even, odd_in, tail_in, low, first, second, strip, c_out, f_out, odd, tail, *work):
-    wk, mid, lap_w, fa, fb = work
-    count = len(order)
+        absorb(grid, kap, point, here, loader(grid, kap, [tile], strip), even, odd, tail, work)
+
+
+def last_kernel(grid, count, kap, even, odd_in, tail_in, low, first, second, strip, c_out, f_out, odd, tail, *work):
+    wk, mid, lap_w, fa, fb, fc, c_rows, f_rows, sems = work
     here = lax.axis_index("tm")
+    point = (here ^ (count - 1)) + 1
     rows, width = grid.rows, grid.width
-    arrival(grid, count // 2, [first, second], strip, kap, order, even, odd, tail, work)
+    load = loader(grid, kap, [first, second], strip)
     state = wk
-
-    def put(dst, at, value):
+    chunk = round_up(-(-rows // sems.shape[1]), BLOCK)
+
+    def sent(which, i):
+        src, dst = ((c_rows, c_out), (f_rows, f_out))[which]
+        part = slice(i * chunk, min((i + 1) * chunk, rows))
+        return pltpu.make_async_copy(src.at[part], dst.at[0, part], sems.at[which, i])
+
+    def put(which, at, value):
         stop = min(at.stop, rows)
         if at.start < stop:
-            dst[0, at.start : stop, :] = value[: stop - at.start, :width]
+            (c_rows, f_rows)[which][at.start : stop, :] = value[: stop - at.start, :width]
+            if stop % chunk == 0 or stop == rows:
+                sent(which, (stop - 1) // chunk).start()
 
     @pl.when(here == 0)
     def _():
-        c_out[0] = tail[:rows, :width]
-        f_out[0] = low[:rows, :width]
+        def body(at):
+            put(0, at, tail[at, :])
+            put(1, at, low[at, :])
+
+        grid.over(body)
 
     @pl.when(here == 1)
     def _():
-        grid.flux(kap, tail, fa)
-
         def body(at):
-            put(c_out, at, even[0, at, :] + odd[0, at, :])
-            put(f_out, at, tail[at, :] + grid.lap(fa, at))
-
-        grid.over(body)
+            c = tail[at, :]
+            put(0, at, even[0, at, :] + odd[0, at, :])
+            return kap[at, :] * c * c
+
+        grid.over(body, fa)
+
+        def last(at):
+            put(1, at, tail[at, :] + grid.lap(fa, at))
+
+        grid.over(last)
 
     @pl.when(here >= 2)
     def _():
-        def begin(at):
-            x = even[0, at, :] + odd[0, at, :]
-            state[at, :] = x
-            return kap[at, :] * x * x
-
-        grid.over(begin, fb)
+        @pl.when(point == 1)
+        def _():
+            load(wk, fa)
+
+            def out(at, g):
+                x = even[0, at, :] + g
+                state[at, :] = x
+                return kap[at, :] * x * x
+
+            grid.first_part(kap, wk, mid, lap_w, fa, fb, out, False, fc)
+
+        @pl.when(point != 1)
+        def _():
+            @pl.when(point <= here)
+            def _():
+                absorb(grid, kap, point, here, load, even, odd, tail, work[:5], count == 4)
+
+            def begin(at):
+                x = even[0, at, :] + odd[0, at, :]
+                state[at, :] = x
+                return kap[at, :] * x * x
+
+            grid.over(begin, fc)
 
         if count > 4:
 
             def step(j, carry):
                 def body(at):
-                    x = state[at, :] + 4.0 * grid.lap(fb, at) + (even[j, at, :] + odd[j, at, :])
+                    x = state[at, :] + 4.0 * grid.lap(fc, at) + (even[j, at, :] + odd[j, at, :])
                     state[at, :] = x
                     return kap[at, :] * x * x
 
                 grid.over(body, fa)
-                fb[...] = fa[...]
+                fc[...] = fa[...]
                 return carry
 
             lax.fori_loop(1, lax.div(here, 2), step, 0)
@@ -290,9 +323,9 @@
         @pl.when(lax.rem(here, 2) == 0)
         def _():
             def body(at):
-                x, lx = state[at, :], grid.lap(fb, at)
-                put(c_out, at, x + 2.0 * lx + tail[at, :])
-                put(f_out, at, x + lx)
+                x, lx = state[at, :], grid.lap(fc, at)
+                put(0, at, x + 2.0 * lx + tail[at, :])
+                put(1, at, x + lx)
 
             grid.over(body)
 
@@ -301,18 +334,22 @@
             j = lax.div(here, 2)
 
             def body(at):
-                x, lx = state[at, :], grid.lap(fb, at)
+                x, lx = state[at, :], grid.lap(fc, at)
                 c = x + 2.0 * lx + tail[at, :]
                 mid[at, :] = c
-                put(c_out, at, x + 4.0 * lx + (even[j, at, :] + odd[j, at, :]))
+                put(0, at, x + 4.0 * lx + (even[j, at, :] + odd[j, at, :]))
                 return kap[at, :] * c * c
 
             grid.over(body, fa)
 
             def last(at):
-                put(f_out, at, mid[at, :] + grid.lap(fa, at))
+                put(1, at, mid[at, :] + grid.lap(fa, at))
 
             grid.over(last)
+
+    for which in (0, 1):
+        for i in range(-(-rows // chunk)):
+            sent(which, i).wait()
 
 
 def on_device(initial, kappa, c_guess):
@@ -321,17 +358,17 @@
     steps = count // 2
     halo, deep = round_up(steps + 3, SUBLANES), steps + 2
     grid = Grid(rows, width, halo, deep)
-    order = ring("tm", gray=True)
-    sx = ring("sx")
-    middle = rows // 2
+    share = round_up(int(rows * SHARE), BLOCK)
     ext, padded = grid.ext, grid.padded
     work = [ext] * 3 + [padded] * 2
     sides = (steps, *ext)
 
-    tiles, strips = {}, {}
-    if steps > 1:
-        for s in (1, -1):
-            tiles[s] = shift(c_guess, "tm", order, s)[0]
+    tiles, strips = {0: c_guess[0]}, {}
+    singles = [1 << i for i in range((count - 1).bit_length())]
+    several = sorted((d for d in range(1, count - 1) if d not in singles), key=lambda d: d.bit_count())
+    for bit in singles:
+        if bit < count - 1:
+            tiles[bit] = swap(c_guess, "tm", bit)[0]
 
     fields = (kappa, initial, c_guess[0])
     packed = (len(fields), halo, rows)
@@ -345,7 +382,7 @@
         jnp.concatenate([x[rows - halo :] for x in fields], axis=0),
         left, right,
     )
-    before, after = shift(last_rows, "sx", sx, 1), shift(first_rows, "sx", sx, -1)
+    before, after = neighbours("sx", last_rows, first_rows)
 
     def padded_to(x, shape):
         return jnp.pad(x, [(0, n - m) for m, n in zip(x.shape, shape)])
@@ -356,9 +393,10 @@
     strip = jnp.concatenate(
         [padded_to(edge[:, :width], part), padded_to(jnp.concatenate([cols, edge[:, width:]], axis=1), part)], axis=0
     )
-    if steps > 1:
-        for s in (1, -1):
-            strips[s] = shift(strip, "tm", order, s)
+    strips[0] = strip
+    for bit in singles:
+        if bit < count - 1:
+            strips[bit] = swap(strip, "tm", bit)
 
     before, strip = together(before, strip)
     kap, even, tail, low = call(functools.partial(start_kernel, grid), [ext, sides, ext, ext], work, 4)(
@@ -366,27 +404,23 @@
     )
     odd = jnp.zeros(sides, jnp.float32)
 
-    if steps == 1:
-        tiles, strips = {1: c_guess[0], -1: c_guess[0]}, {1: strip}
-    for s in range(1, steps):
-        given = [x for way in (1, -1) for x in (tiles[way], strips[way])]
-        strips = {way: shift(x, "tm", order, way) for way, x in strips.items() if s + 1 < steps or way == 1}
-        if s + 1 < steps:
-            tiles = {way: shift(x, "tm", order, way) for way, x in tiles.items()}
-        else:
-            second = shift(tiles[1][middle:], "tm", order, 1)
-            first = shift(tiles[-1][:middle], "tm", order, -1)
-        even, odd, tail = call(
-            functools.partial(middle_kernel, grid, order, (s, count - s)), [sides, sides, ext], work, 1000,
-            input_output_aliases={1: 0, 2: 1, 3: 2},
-        )(kap, even, odd, tail, *given)
-    if steps == 1:
-        second, first = shift(tiles[1][middle:], "tm", order, 1), shift(tiles[-1][:middle], "tm", order, -1)
-        strips = {1: shift(strip, "tm", order, 1)}
+    for d in several:
+        bit = d & -d
+        tiles[d], strips[d] = swap(tiles[d ^ bit], "tm", bit), swap(strips[d ^ bit], "tm", bit)
+    near, far, last = singles[0], singles[-1], count - 1
+    first, second = swap(tiles[last ^ near][:share], "tm", near), swap(tiles[last ^ far][share:], "tm", far)
+    strips[last] = swap(strips[last ^ near], "tm", near)
+    for d in (*singles, *several):
+        if d != last:
+            even, odd, tail = call(
+                functools.partial(middle_kernel, grid, d), [sides, sides, ext], work, MIDDLE,
+                input_output_aliases={1: 0, 2: 1, 3: 2},
+            )(kap, even, odd, tail, tiles[d], strips[d])
     c_new, f_new, _, _ = call(
-        functools.partial(last_kernel, grid, order), [c_guess.shape] * 2 + [sides, ext], work, 8,
-        input_output_aliases={2: 2, 3: 3},
-    )(kap, even, odd, tail, low, first, second, strips[1])
+        functools.partial(last_kernel, grid, count), [c_guess.shape] * 2 + [sides, ext],
+        work + [padded] + [(rows, width)] * 2, 8, semaphores=(2, 4), input_output_aliases={2: 2, 3: 3},
+        out_specs=[pl.BlockSpec(memory_space=space) for space in (pl.ANY, pl.ANY, pltpu.VMEM, pltpu.VMEM)],
+    )(kap, even, odd, tail, low, first, second, strips[last])
     return c_new, f_new
 
 

time: 29.2 us -> 27.9 us (0.955)
  the two profiles are of different devices: /device:TPU:12 before, /device:TPU:14 now
where the time goes in v4:
time: 27.9 us; the launch traced here: 27.6 us
  starting transfers between devices  10.5 us (38%)
  Pallas kernels  7.02 us (25%)
  waiting for transfers between devices  6.04 us (22%)
  local copies, waits for them, and re-layouts  3.04 us (11%)
  between operations  0.86 us (3%)
    ppermute x7, starting transfers between devices, swap(): lax.ppermute(x, axis, [(i, i ^ bits) for i in range(lax.axis_size(axis))])  6.91 us
    ppermute x3, waiting for transfers between devices, neighbours(): lax.ppermute(send, axis, sorted(pairs.items()))  4.22 us
    ppermute x3, starting transfers between devices, neighbours(): lax.ppermute(send, axis, sorted(pairs.items()))  3.63 us
    pallas_call x1, Pallas kernels, on_device(): call(functools.partial(last_kernel, grid, count), [c_guess.shape] * 2 + [...  2.62 us
    pallas_call x2, Pallas kernels, on_device(): call(functools.partial(middle_kernel, grid, d), [sides, sides, ext], work...  2.45 us
    slice x2, local copies, waits for them, and re-layouts, on_device(): x[:, width - LANES:]  2.13 us
    ppermute x7, waiting for transfers between devices, swap(): lax.ppermute(x, axis, [(i, i ^ bits) for i in range(lax.axis_size(axis))])  1.81 us
    pallas_call x1, Pallas kernels, on_device(): call(functools.partial(start_kernel, grid), [ext, sides, ext, ext], work, 4)  1.55 us
  transfers between devices with their start and end apart: 10, of which 5 were waited for; matrix products, arithmetic and copies ran while one was open for 11% of the time, Pallas kernels for 16%

profile of v4, /device:TPU:14, one launch (start us, length us, event | category | flops | bytes accessed | tf_op | source)
XLA Modules:
  0.0 27.6 jit_solution(18165906379678882773)
XLA Ops:
  0.7 0.6 %collective-permute-start.3 = (f32[1,256,512]{2,1,0:T(8,128)}, f32[1,256,512]{2,1,0:T(8,128)S(1)}, u32[]{:S(2)}, u32[]{:S(2)}) collective-permute-start(f32[1,256,512]{2,1,0:T(8,128)} %param.5), channel_id=1, source_target_pairs={{0,8},{8,0},{16,24},{24,16},{1,9},{9,1},{17,25},{25,17},{2,10},{10... | collective-permute-start | bytes 1572872 | tf_op jit(solution)/shard_map/ppermute | solution.py:22
  1.3 0.5 %collective-permute-start.5 = (f32[1,256,512]{2,1,0:T(8,128)}, f32[1,256,512]{2,1,0:T(8,128)S(1)}, u32[]{:S(2)}, u32[]{:S(2)}) collective-permute-start(f32[1,256,512]{2,1,0:T(8,128)} %param.5), channel_id=1, source_target_pairs={{0,16},{8,24},{16,0},{24,8},{1,17},{9,25},{17,1},{25,9},{2,18},{10... | collective-permute-start | bytes 1572872 | tf_op jit(solution)/shard_map/ppermute | solution.py:22
  1.8 1.0 %fusion.2 = (f32[256,128]{1,0:T(8,128)S(1)}, f32[256,128]{1,0:T(8,128)S(1)}) fusion(f32[256,512]{1,0:T(8,128)} %bitcast.21), kind=kLoop, calls=%fused_computation.26 | loop fusion | bytes 524288 | tf_op jit(solution)/shard_map/slice | solution.py:376
  2.8 1.1 %fusion.3 = (f32[256,128]{1,0:T(8,128)S(1)}, f32[256,128]{1,0:T(8,128)S(1)}, f32[256,128]{1,0:T(8,128)S(1)}, f32[256,128]{1,0:T(8,128)S(1)}) fusion(f32[256,512]{1,0:T(8,128)} %initial.1, f32[256,512]{1,0:T(8,128)} %kappa.1), kind=kLoop, calls=%fused_computation.27 | loop fusion | bytes 1048576 | tf_op jit(solution)/shard_map/slice | solution.py:376
  3.9 0.3 shard_map.50
  4.2 3.5 %collective-permute-start = (f32[3,8,256]{2,1,0:T(8,128)S(1)}, f32[3,8,256]{2,1,0:T(8,128)S(1)}, u32[]{:S(2)}, u32[]{:S(2)}) collective-permute-start(f32[3,8,256]{2,1,0:T(8,128)S(1)} %get-tuple-element.53), channel_id=1, source_target_pairs={{0,0},{1,2},{2,1},{3,3},{4,4},{5,6},{6,5},{7,7},{8,8},{9,10},{10,9... | collective-permute-start | bytes 73736 | tf_op jit(solution)/shard_map/ppermute | solution.py:34
  7.8 0.7 %slice_bitcast_fusion.2 = (f32[8,512]{1,0:T(8,128)S(1)}, f32[8,512]{1,0:T(8,128)S(1)}) fusion(f32[1,256,512]{2,1,0:T(8,128)} %param.5), kind=kLoop, calls=%fused_computation.13 | loop fusion | bytes 65536 | tf_op jit(solution)/shard_map/slice | solution.py:382
  8.6 1.3 %collective-permute-done = f32[3,8,256]{2,1,0:T(8,128)S(1)} collective-permute-done((f32[3,8,256]{2,1,0:T(8,128)S(1)}, f32[3,8,256]{2,1,0:T(8,128)S(1)}, u32[]{:S(2)}, u32[]{:S(2)}) %collective-permute-start) | collective-permute-done | bytes 24608 | tf_op jit(solution)/shard_map/ppermute | solution.py:34
  9.9 1.7 %collective-permute-done.1 = f32[3,8,256]{2,1,0:T(8,128)S(1)} collective-permute-done((f32[3,8,256]{2,1,0:T(8,128)S(1)}, f32[3,8,256]{2,1,0:T(8,128)S(1)}, u32[]{:S(2)}, u32[]{:S(2)}) %collective-permute-start.1) | collective-permute-done | bytes 24608 | tf_op jit(solution)/shard_map/ppermute | solution.py:34
  11.6 0.1 shard_map.51
  11.8 0.1 collective-permute-start.2
  11.9 1.2 %collective-permute-done.2 = f32[3,8,640]{2,1,0:T(8,128)S(1)} collective-permute-done((f32[3,8,640]{2,1,0:T(8,128)S(1)}, f32[3,8,640]{2,1,0:T(8,128)S(1)}, u32[]{:S(2)}, u32[]{:S(2)}) %collective-permute-start.2) | collective-permute-done | bytes 61472 | tf_op jit(solution)/shard_map/ppermute | solution.py:34
  13.2 1.6 %collective-permute-start.4 = (f32[16,512]{1,0:T(8,128)S(1)}, f32[16,512]{1,0:T(8,128)S(1)}, u32[]{:S(2)}, u32[]{:S(2)}) collective-permute-start(f32[16,512]{1,0:T(8,128)S(1)} %select_maximum_fusion), channel_id=1, source_target_pairs={{0,8},{8,0},{16,24},{24,16},{1,9},{9,1},{17,25},{25,17},{2,10},{10... | collective-permute-start | bytes 98312 | tf_op jit(solution)/shard_map/ppermute | solution.py:22
  14.7 1.5 %collective-permute-start.6 = (f32[16,512]{1,0:T(8,128)S(1)}, f32[16,512]{1,0:T(8,128)S(1)}, u32[]{:S(2)}, u32[]{:S(2)}) collective-permute-start(f32[16,512]{1,0:T(8,128)S(1)} %select_maximum_fusion), channel_id=1, source_target_pairs={{0,16},{8,24},{16,0},{24,8},{1,17},{9,25},{17,1},{25,9},{2,18},{10... | collective-permute-start | bytes 98312 | tf_op jit(solution)/shard_map/ppermute | solution.py:22
  16.3 0.6 %collective-permute-start.8 = (f32[144,512]{1,0:T(8,128)S(1)}, f32[144,512]{1,0:T(8,128)S(1)}, u32[]{:S(2)}, u32[]{:S(2)}) collective-permute-start(f32[144,512]{1,0:T(8,128)S(1)} %slice_bitcast_fusion), channel_id=1, source_target_pairs={{0,16},{8,24},{16,0},{24,8},{1,17},{9,25},{17,1},{25,9},{2,18},{10... | collective-permute-start | bytes 884744 | tf_op jit(solution)/shard_map/ppermute | solution.py:22
  16.9 0.6 %collective-permute-start.7 = (f32[112,512]{1,0:T(8,128)S(1)}, f32[112,512]{1,0:T(8,128)S(1)}, u32[]{:S(2)}, u32[]{:S(2)}) collective-permute-start(f32[112,512]{1,0:T(8,128)S(1)} %slice_bitcast_fusion.1), channel_id=1, source_target_pairs={{0,8},{8,0},{16,24},{24,16},{1,9},{9,1},{17,25},{25,17},{2,10},{10... | collective-permute-start | bytes 688136 | tf_op jit(solution)/shard_map/ppermute | solution.py:22
  17.5 1.5 %shard_map.52 = (f32[272,640]{1,0:T(8,128)S(1)}, f32[2,272,640]{2,1,0:T(8,128)S(1)}, f32[272,640]{1,0:T(8,128)S(1)}, f32[272,640]{1,0:T(8,128)S(1)}) custom-call(f32[256,512]{1,0:T(8,128)S(1)} %copy-done, f32[256,512]{1,0:T(8,128)S(1)} %copy-done.1, f32[3,8,640]{2,1,0:T(8,128)S(1)} %get-tuple-element.23.before, f32[3,8,640]{2,1,0:T(8,128)S(1)} %get-tuple-element.48.after, ...), custom_call_target="tpu_custom_call" | custom-call | flops 11141120 | bytes 16711680 | tf_op jit(solution)/shard_map/pallas_call | solution.py:402
  19.1 1.6 %collective-permute-start.9 = (f32[16,512]{1,0:T(8,128)S(1)}, f32[16,512]{1,0:T(8,128)S(1)}, u32[]{:S(2)}, u32[]{:S(2)}) collective-permute-start(f32[16,512]{1,0:T(8,128)S(1)} %collective-permute-done.6.strip), channel_id=1, source_target_pairs={{0,8},{8,0},{16,24},{24,16},{1,9},{9,1},{17,25},{25,17},{2,10},{10... | collective-permute-start | bytes 98312 | tf_op jit(solution)/shard_map/ppermute | solution.py:22
  20.6 0.1 broadcast_in_dim.3.odd_in
  20.7 1.0 %shard_map.53 = (f32[2,272,640]{2,1,0:T(8,128)S(1)}, f32[2,272,640]{2,1,0:T(8,128)S(1)}, f32[272,640]{1,0:T(8,128)S(1)}) custom-call(f32[272,640]{1,0:T(8,128)S(1)} %get-tuple-element.24.kap, f32[2,272,640]{2,1,0:T(8,128)S(1)} %get-tuple-element.25.even_in, ...), custom_call_target="tpu_custom_call", output_to_operand_aliasing={{0}: (1, {}), {1}: (2, {}), {2}: (3, {})} | custom-call | flops 1128038400 | bytes 1692057600 | tf_op jit(solution)/shard_map/pallas_call | solution.py:415
  21.7 1.5 %shard_map.54 = (f32[2,272,640]{2,1,0:T(8,128)S(1)}, f32[2,272,640]{2,1,0:T(8,128)S(1)}, f32[272,640]{1,0:T(8,128)S(1)}) custom-call(f32[272,640]{1,0:T(8,128)S(1)} %get-tuple-element.24.kap, f32[2,272,640]{2,1,0:T(8,128)S(1)} %get-tuple-element.27.even_in, ...), custom_call_target="tpu_custom_call", output_to_operand_aliasing={{0}: (1, {}), {1}: (2, {}), {2}: (3, {})} | custom-call | flops 1128038400 | bytes 1692057600 | tf_op jit(solution)/shard_map/pallas_call | solution.py:415
  23.2 1.3 %collective-permute-done.9.strip = f32[16,512]{1,0:T(8,128)S(1)} collective-permute-done((f32[16,512]{1,0:T(8,128)S(1)}, f32[16,512]{1,0:T(8,128)S(1)}, u32[]{:S(2)}, u32[]{:S(2)}) %collective-permute-start.9) | collective-permute-done | bytes 32800 | tf_op jit(solution)/shard_map/ppermute | solution.py:22
  24.5 0.5 %collective-permute-done.8.second = f32[144,512]{1,0:T(8,128)S(1)} collective-permute-done((f32[144,512]{1,0:T(8,128)S(1)}, f32[144,512]{1,0:T(8,128)S(1)}, u32[]{:S(2)}, u32[]{:S(2)}) %collective-permute-start.8) | collective-permute-done | bytes 294944 | tf_op jit(solution)/shard_map/ppermute | solution.py:22
  25.0 2.6 %shard_map.55 = (f32[1,256,512]{2,1,0:T(8,128)}, f32[1,256,512]{2,1,0:T(8,128)}, f32[2,272,640]{2,1,0:T(8,128)S(1)}, f32[272,640]{1,0:T(8,128)S(1)}) custom-call(f32[272,640]{1,0:T(8,128)S(1)} %get-tuple-element.24.kap, f32[2,272,640]{2,1,0:T(8,128)S(1)} %get-tuple-element.30.even, ...), custom_call_target="tpu_custom_call", output_to_operand_aliasing={{2}: (2, {}), {3}: (3, {})} | custom-call | flops 22282240 | bytes 33423360 | tf_op jit(solution)/shard_map/pallas_call | solution.py:419
  (26 shorter events, 0.3 us)
Async XLA Ops:
  0.6 7.2 %copy-start.1 = (f32[256,512]{1,0:T(8,128)S(1)}, f32[256,512]{1,0:T(8,128)}, u32[]{:S(2)}) copy-start(f32[256,512]{1,0:T(8,128)} %initial.1) | copy-start | bytes 1572868
  0.6 7.1 %copy-start = (f32[256,512]{1,0:T(8,128)S(1)}, f32[256,512]{1,0:T(8,128)}, u32[]{:S(2)}) copy-start(f32[256,512]{1,0:T(8,128)} %kappa.1) | copy-start | bytes 1572868
  0.7 15.6 %collective-permute-start.3 = (f32[1,256,512]{2,1,0:T(8,128)}, f32[1,256,512]{2,1,0:T(8,128)S(1)}, u32[]{:S(2)}, u32[]{:S(2)}) collective-permute-start(f32[1,256,512]{2,1,0:T(8,128)} %param.5), channel_id=1, source_target_pairs={{0,8},{8,0},{16,24},{24,16},{1,9},{9,1},{17,25},{25,17},{2,10},{10... | collective-permute-start | bytes 1572872 | tf_op jit(solution)/shard_map/ppermute | solution.py:22
  1.3 15.6 %collective-permute-start.5 = (f32[1,256,512]{2,1,0:T(8,128)}, f32[1,256,512]{2,1,0:T(8,128)S(1)}, u32[]{:S(2)}, u32[]{:S(2)}) collective-permute-start(f32[1,256,512]{2,1,0:T(8,128)} %param.5), channel_id=1, source_target_pairs={{0,16},{8,24},{16,0},{24,8},{1,17},{9,25},{17,1},{25,9},{2,18},{10... | collective-permute-start | bytes 1572872 | tf_op jit(solution)/shard_map/ppermute | solution.py:22
  4.2 5.7 %collective-permute-start = (f32[3,8,256]{2,1,0:T(8,128)S(1)}, f32[3,8,256]{2,1,0:T(8,128)S(1)}, u32[]{:S(2)}, u32[]{:S(2)}) collective-permute-start(f32[3,8,256]{2,1,0:T(8,128)S(1)} %get-tuple-element.53), channel_id=1, source_target_pairs={{0,0},{1,2},{2,1},{3,3},{4,4},{5,6},{6,5},{7,7},{8,8},{9,10},{10,9... | collective-permute-start | bytes 73736 | tf_op jit(solution)/shard_map/ppermute | solution.py:34
  7.7 3.9 %collective-permute-start.1 = (f32[3,8,256]{2,1,0:T(8,128)S(1)}, f32[3,8,256]{2,1,0:T(8,128)S(1)}, u32[]{:S(2)}, u32[]{:S(2)}) collective-permute-start(f32[3,8,256]{2,1,0:T(8,128)S(1)} %get-tuple-element.52), channel_id=1, source_target_pairs={{0,1},{1,0},{2,3},{3,2},{4,5},{5,4},{6,7},{7,6},{8,9},{9,8},{10,11... | collective-permute-start | bytes 73736 | tf_op jit(solution)/shard_map/ppermute | solution.py:34
  11.8 1.3 %collective-permute-start.2 = (f32[3,8,640]{2,1,0:T(8,128)S(1)}, f32[3,8,640]{2,1,0:T(8,128)S(1)}, u32[]{:S(2)}, u32[]{:S(2)}) collective-permute-start(f32[3,8,640]{2,1,0:T(8,128)S(1)} %broadcast_select_fusion.3), channel_id=1, source_target_pairs={{0,4},{4,0},{1,5},{5,1},{2,6},{6,2},{3,7},{7,3},{8,12},{12,8},{9,1... | collective-permute-start | bytes 184328 | tf_op jit(solution)/shard_map/ppermute | solution.py:34
  13.2 7.4 %collective-permute-start.4 = (f32[16,512]{1,0:T(8,128)S(1)}, f32[16,512]{1,0:T(8,128)S(1)}, u32[]{:S(2)}, u32[]{:S(2)}) collective-permute-start(f32[16,512]{1,0:T(8,128)S(1)} %select_maximum_fusion), channel_id=1, source_target_pairs={{0,8},{8,0},{16,24},{24,16},{1,9},{9,1},{17,25},{25,17},{2,10},{10... | collective-permute-start | bytes 98312 | tf_op jit(solution)/shard_map/ppermute | solution.py:22
  14.7 4.3 %collective-permute-start.6 = (f32[16,512]{1,0:T(8,128)S(1)}, f32[16,512]{1,0:T(8,128)S(1)}, u32[]{:S(2)}, u32[]{:S(2)}) collective-permute-start(f32[16,512]{1,0:T(8,128)S(1)} %select_maximum_fusion), channel_id=1, source_target_pairs={{0,16},{8,24},{16,0},{24,8},{1,17},{9,25},{17,1},{25,9},{2,18},{10... | collective-permute-start | bytes 98312 | tf_op jit(solution)/shard_map/ppermute | solution.py:22
  16.3 8.7 %collective-permute-start.8 = (f32[144,512]{1,0:T(8,128)S(1)}, f32[144,512]{1,0:T(8,128)S(1)}, u32[]{:S(2)}, u32[]{:S(2)}) collective-permute-start(f32[144,512]{1,0:T(8,128)S(1)} %slice_bitcast_fusion), channel_id=1, source_target_pairs={{0,16},{8,24},{16,0},{24,8},{1,17},{9,25},{17,1},{25,9},{2,18},{10... | collective-permute-start | bytes 884744 | tf_op jit(solution)/shard_map/ppermute | solution.py:22
  16.9 7.6 %collective-permute-start.7 = (f32[112,512]{1,0:T(8,128)S(1)}, f32[112,512]{1,0:T(8,128)S(1)}, u32[]{:S(2)}, u32[]{:S(2)}) collective-permute-start(f32[112,512]{1,0:T(8,128)S(1)} %slice_bitcast_fusion.1), channel_id=1, source_target_pairs={{0,8},{8,0},{16,24},{24,16},{1,9},{9,1},{17,25},{25,17},{2,10},{10... | collective-permute-start | bytes 688136 | tf_op jit(solution)/shard_map/ppermute | solution.py:22
  19.1 5.4 %collective-permute-start.9 = (f32[16,512]{1,0:T(8,128)S(1)}, f32[16,512]{1,0:T(8,128)S(1)}, u32[]{:S(2)}, u32[]{:S(2)}) collective-permute-start(f32[16,512]{1,0:T(8,128)S(1)} %collective-permute-done.6.strip), channel_id=1, source_target_pairs={{0,8},{8,0},{16,24},{24,16},{1,9},{9,1},{17,25},{25,17},{2,10},{10... | collective-permute-start | bytes 98312 | tf_op jit(solution)/shard_map/ppermute | solution.py:22

commit v5 on v4

--- a/solution.py
+++ b/solution.py
@@ -55,12 +55,11 @@
 
 
 def cols_kernel(halo, *refs):
-    fields = len(refs) // 2 - 1
-    firsts, lasts = refs[:fields], refs[fields : 2 * fields]
-    first_out, last_out = refs[2 * fields :]
-    for k in range(fields):
-        first_out[k] = firsts[k][...].T[:halo]
-        last_out[k] = lasts[k][...].T[LANES - halo :]
+    *fields, first_out, last_out = refs
+    for k, field in enumerate(fields):
+        width = field.shape[1]
+        first_out[k] = field[:, :LANES].T[:halo]
+        last_out[k] = field[:, width - LANES :].T[LANES - halo :]
 
 
 def rows_kernel(halo, first_rows, last_rows, left, right, first_out, last_out):
@@ -373,7 +372,7 @@
     fields = (kappa, initial, c_guess[0])
     packed = (len(fields), halo, rows)
     first_cols, last_cols = call(functools.partial(cols_kernel, halo), [packed] * 2)(
-        *[x[:, :LANES] for x in fields], *[x[:, width - LANES :] for x in fields]
+        kappa, initial, jnp.concatenate([c_guess[0, :, :LANES], c_guess[0, :, width - LANES :]], axis=1)
     )
     left, right = neighbours("sy", last_cols, first_cols)
     packed = (len(fields), halo, grid.wide)

time: 27.9 us -> 26.8 us (0.961)
  local copies, waits for them, and re-layouts: 3.04 us -> 1.9 us
    slice x2 -> x0, local copies, waits for them, and re-layouts: 2.13 us -> none  [on_device(): x[:, width - LANES:]]
    squeeze x0 -> x1, local copies, waits for them, and re-layouts: none -> 0.99 us  [on_device(): c_guess[0, :, :LANES]]
  transfers between devices with their start and end apart: 10 -> 10, of which waited for: 5 -> 5; matrix products, arithmetic and copies ran while one was open for 11% -> 8% of each run, Pallas kernels for 16% -> 17%
where the time goes in v5:
time: 26.8 us; the launch traced here: 26.5 us
  starting transfers between devices  10.5 us (39%)
  Pallas kernels  7.03 us (26%)
  waiting for transfers between devices  6.05 us (23%)
  local copies, waits for them, and re-layouts  1.9 us (7%)
  between operations  0.87 us (3%)
    ppermute x7, starting transfers between devices, swap(): lax.ppermute(x, axis, [(i, i ^ bits) for i in range(lax.axis_size(axis))])  6.91 us
    ppermute x3, waiting for transfers between devices, neighbours(): lax.ppermute(send, axis, sorted(pairs.items()))  4.24 us
    ppermute x3, starting transfers between devices, neighbours(): lax.ppermute(send, axis, sorted(pairs.items()))  3.63 us
    pallas_call x1, Pallas kernels, on_device(): call(functools.partial(last_kernel, grid, count), [c_guess.shape] * 2 + [...  2.62 us
    pallas_call x2, Pallas kernels, on_device(): call(functools.partial(middle_kernel, grid, d), [sides, sides, ext], work...  2.45 us
    ppermute x7, waiting for transfers between devices, swap(): lax.ppermute(x, axis, [(i, i ^ bits) for i in range(lax.axis_size(axis))])  1.81 us
    pallas_call x1, Pallas kernels, on_device(): call(functools.partial(start_kernel, grid), [ext, sides, ext, ext], work, 4)  1.55 us
    squeeze x1, local copies, waits for them, and re-layouts, on_device(): c_guess[0, :, :LANES]  0.99 us
  transfers between devices with their start and end apart: 10, of which 5 were waited for; matrix products, arithmetic and copies ran while one was open for 8% of the time, Pallas kernels for 17%

profile of v5, /device:TPU:14, one launch (start us, length us, event | category | flops | bytes accessed | tf_op | source)
XLA Modules:
  0.0 26.5 jit_solution(1644530001635680153)
XLA Ops:
  0.6 0.6 %collective-permute-start.3 = (f32[1,256,512]{2,1,0:T(8,128)}, f32[1,256,512]{2,1,0:T(8,128)S(1)}, u32[]{:S(2)}, u32[]{:S(2)}) collective-permute-start(f32[1,256,512]{2,1,0:T(8,128)} %param.5), channel_id=1, source_target_pairs={{0,8},{8,0},{16,24},{24,16},{1,9},{9,1},{17,25},{25,17},{2,10},{10... | collective-permute-start | bytes 1572872 | tf_op jit(solution)/shard_map/ppermute | solution.py:22
  1.2 0.5 %collective-permute-start.5 = (f32[1,256,512]{2,1,0:T(8,128)}, f32[1,256,512]{2,1,0:T(8,128)S(1)}, u32[]{:S(2)}, u32[]{:S(2)}) collective-permute-start(f32[1,256,512]{2,1,0:T(8,128)} %param.5), channel_id=1, source_target_pairs={{0,16},{8,24},{16,0},{24,8},{1,17},{9,25},{17,1},{25,9},{2,18},{10... | collective-permute-start | bytes 1572872 | tf_op jit(solution)/shard_map/ppermute | solution.py:22
  1.8 1.0 %slice_bitcast_fusion.3 = (f32[256,128]{1,0:T(8,128)S(1)}, f32[256,128]{1,0:T(8,128)S(1)}) fusion(f32[1,256,512]{2,1,0:T(8,128)} %param.5), kind=kLoop, calls=%fused_computation.4 | loop fusion | bytes 524288 | tf_op jit(solution)/shard_map/squeeze | solution.py:375
  2.8 0.3 shard_map.50
  3.1 3.5 %collective-permute-start = (f32[3,8,256]{2,1,0:T(8,128)S(1)}, f32[3,8,256]{2,1,0:T(8,128)S(1)}, u32[]{:S(2)}, u32[]{:S(2)}) collective-permute-start(f32[3,8,256]{2,1,0:T(8,128)S(1)} %get-tuple-element.49), channel_id=1, source_target_pairs={{0,0},{1,2},{2,1},{3,3},{4,4},{5,6},{6,5},{7,7},{8,8},{9,10},{10,9... | collective-permute-start | bytes 73736 | tf_op jit(solution)/shard_map/ppermute | solution.py:34
  6.6 0.1 collective-permute-start.1
  6.7 0.7 %slice_bitcast_fusion.4 = (f32[8,512]{1,0:T(8,128)S(1)}, f32[8,512]{1,0:T(8,128)S(1)}) fusion(f32[1,256,512]{2,1,0:T(8,128)} %param.5), kind=kLoop, calls=%fused_computation.16 | loop fusion | bytes 65536 | tf_op jit(solution)/shard_map/slice | solution.py:381
  7.5 1.4 %collective-permute-done = f32[3,8,256]{2,1,0:T(8,128)S(1)} collective-permute-done((f32[3,8,256]{2,1,0:T(8,128)S(1)}, f32[3,8,256]{2,1,0:T(8,128)S(1)}, u32[]{:S(2)}, u32[]{:S(2)}) %collective-permute-start) | collective-permute-done | bytes 24608 | tf_op jit(solution)/shard_map/ppermute | solution.py:34
  8.8 1.7 %collective-permute-done.1 = f32[3,8,256]{2,1,0:T(8,128)S(1)} collective-permute-done((f32[3,8,256]{2,1,0:T(8,128)S(1)}, f32[3,8,256]{2,1,0:T(8,128)S(1)}, u32[]{:S(2)}, u32[]{:S(2)}) %collective-permute-start.1) | collective-permute-done | bytes 24608 | tf_op jit(solution)/shard_map/ppermute | solution.py:34
  10.5 0.2 shard_map.51
  10.7 0.1 collective-permute-start.2
  10.8 1.2 %collective-permute-done.2 = f32[3,8,640]{2,1,0:T(8,128)S(1)} collective-permute-done((f32[3,8,640]{2,1,0:T(8,128)S(1)}, f32[3,8,640]{2,1,0:T(8,128)S(1)}, u32[]{:S(2)}, u32[]{:S(2)}) %collective-permute-start.2) | collective-permute-done | bytes 61472 | tf_op jit(solution)/shard_map/ppermute | solution.py:34
  12.1 1.6 %collective-permute-start.4 = (f32[16,512]{1,0:T(8,128)S(1)}, f32[16,512]{1,0:T(8,128)S(1)}, u32[]{:S(2)}, u32[]{:S(2)}) collective-permute-start(f32[16,512]{1,0:T(8,128)S(1)} %select_maximum_fusion), channel_id=1, source_target_pairs={{0,8},{8,0},{16,24},{24,16},{1,9},{9,1},{17,25},{25,17},{2,10},{10... | collective-permute-start | bytes 98312 | tf_op jit(solution)/shard_map/ppermute | solution.py:22
  13.6 1.5 %collective-permute-start.6 = (f32[16,512]{1,0:T(8,128)S(1)}, f32[16,512]{1,0:T(8,128)S(1)}, u32[]{:S(2)}, u32[]{:S(2)}) collective-permute-start(f32[16,512]{1,0:T(8,128)S(1)} %select_maximum_fusion), channel_id=1, source_target_pairs={{0,16},{8,24},{16,0},{24,8},{1,17},{9,25},{17,1},{25,9},{2,18},{10... | collective-permute-start | bytes 98312 | tf_op jit(solution)/shard_map/ppermute | solution.py:22
  15.2 0.6 %collective-permute-start.8 = (f32[144,512]{1,0:T(8,128)S(1)}, f32[144,512]{1,0:T(8,128)S(1)}, u32[]{:S(2)}, u32[]{:S(2)}) collective-permute-start(f32[144,512]{1,0:T(8,128)S(1)} %slice_bitcast_fusion), channel_id=1, source_target_pairs={{0,16},{8,24},{16,0},{24,8},{1,17},{9,25},{17,1},{25,9},{2,18},{10... | collective-permute-start | bytes 884744 | tf_op jit(solution)/shard_map/ppermute | solution.py:22
  15.8 0.6 %collective-permute-start.7 = (f32[112,512]{1,0:T(8,128)S(1)}, f32[112,512]{1,0:T(8,128)S(1)}, u32[]{:S(2)}, u32[]{:S(2)}) collective-permute-start(f32[112,512]{1,0:T(8,128)S(1)} %slice_bitcast_fusion.1), channel_id=1, source_target_pairs={{0,8},{8,0},{16,24},{24,16},{1,9},{9,1},{17,25},{25,17},{2,10},{10... | collective-permute-start | bytes 688136 | tf_op jit(solution)/shard_map/ppermute | solution.py:22
  16.4 1.5 %shard_map.52 = (f32[272,640]{1,0:T(8,128)S(1)}, f32[2,272,640]{2,1,0:T(8,128)S(1)}, f32[272,640]{1,0:T(8,128)S(1)}, f32[272,640]{1,0:T(8,128)S(1)}) custom-call(f32[256,512]{1,0:T(8,128)S(1)} %copy-done, f32[256,512]{1,0:T(8,128)S(1)} %copy-done.1, f32[3,8,640]{2,1,0:T(8,128)S(1)} %get-tuple-element.23.before, f32[3,8,640]{2,1,0:T(8,128)S(1)} %get-tuple-element.44.after, ...), custom_call_target="tpu_custom_call" | custom-call | flops 11141120 | bytes 16711680 | tf_op jit(solution)/shard_map/pallas_call | solution.py:401
  18.0 1.5 %collective-permute-start.9 = (f32[16,512]{1,0:T(8,128)S(1)}, f32[16,512]{1,0:T(8,128)S(1)}, u32[]{:S(2)}, u32[]{:S(2)}) collective-permute-start(f32[16,512]{1,0:T(8,128)S(1)} %collective-permute-done.6.strip), channel_id=1, source_target_pairs={{0,8},{8,0},{16,24},{24,16},{1,9},{9,1},{17,25},{25,17},{2,10},{10... | collective-permute-start | bytes 98312 | tf_op jit(solution)/shard_map/ppermute | solution.py:22
  19.5 0.1 broadcast_in_dim.3.odd_in
  19.6 1.0 %shard_map.53 = (f32[2,272,640]{2,1,0:T(8,128)S(1)}, f32[2,272,640]{2,1,0:T(8,128)S(1)}, f32[272,640]{1,0:T(8,128)S(1)}) custom-call(f32[272,640]{1,0:T(8,128)S(1)} %get-tuple-element.24.kap, f32[2,272,640]{2,1,0:T(8,128)S(1)} %get-tuple-element.25.even_in, ...), custom_call_target="tpu_custom_call", output_to_operand_aliasing={{0}: (1, {}), {1}: (2, {}), {2}: (3, {})} | custom-call | flops 1128038400 | bytes 1692057600 | tf_op jit(solution)/shard_map/pallas_call | solution.py:414
  20.6 1.5 %shard_map.54 = (f32[2,272,640]{2,1,0:T(8,128)S(1)}, f32[2,272,640]{2,1,0:T(8,128)S(1)}, f32[272,640]{1,0:T(8,128)S(1)}) custom-call(f32[272,640]{1,0:T(8,128)S(1)} %get-tuple-element.24.kap, f32[2,272,640]{2,1,0:T(8,128)S(1)} %get-tuple-element.27.even_in, ...), custom_call_target="tpu_custom_call", output_to_operand_aliasing={{0}: (1, {}), {1}: (2, {}), {2}: (3, {})} | custom-call | flops 1128038400 | bytes 1692057600 | tf_op jit(solution)/shard_map/pallas_call | solution.py:414
  22.1 1.3 %collective-permute-done.9.strip = f32[16,512]{1,0:T(8,128)S(1)} collective-permute-done((f32[16,512]{1,0:T(8,128)S(1)}, f32[16,512]{1,0:T(8,128)S(1)}, u32[]{:S(2)}, u32[]{:S(2)}) %collective-permute-start.9) | collective-permute-done | bytes 32800 | tf_op jit(solution)/shard_map/ppermute | solution.py:22
  23.4 0.5 %collective-permute-done.8.second = f32[144,512]{1,0:T(8,128)S(1)} collective-permute-done((f32[144,512]{1,0:T(8,128)S(1)}, f32[144,512]{1,0:T(8,128)S(1)}, u32[]{:S(2)}, u32[]{:S(2)}) %collective-permute-start.8) | collective-permute-done | bytes 294944 | tf_op jit(solution)/shard_map/ppermute | solution.py:22
  23.9 2.6 %shard_map.55 = (f32[1,256,512]{2,1,0:T(8,128)}, f32[1,256,512]{2,1,0:T(8,128)}, f32[2,272,640]{2,1,0:T(8,128)S(1)}, f32[272,640]{1,0:T(8,128)S(1)}) custom-call(f32[272,640]{1,0:T(8,128)S(1)} %get-tuple-element.24.kap, f32[2,272,640]{2,1,0:T(8,128)S(1)} %get-tuple-element.30.even, ...), custom_call_target="tpu_custom_call", output_to_operand_aliasing={{2}: (2, {}), {3}: (3, {})} | custom-call | flops 22282240 | bytes 33423360 | tf_op jit(solution)/shard_map/pallas_call | solution.py:418
  (25 shorter events, 0.2 us)
Async XLA Ops:
  0.6 2.2 %copy-start.1 = (f32[256,512]{1,0:T(8,128)S(1)}, f32[256,512]{1,0:T(8,128)}, u32[]{:S(2)}) copy-start(f32[256,512]{1,0:T(8,128)} %initial.1) | copy-start | bytes 1572868
  0.6 2.2 %copy-start = (f32[256,512]{1,0:T(8,128)S(1)}, f32[256,512]{1,0:T(8,128)}, u32[]{:S(2)}) copy-start(f32[256,512]{1,0:T(8,128)} %kappa.1) | copy-start | bytes 1572868
  0.6 14.5 %collective-permute-start.3 = (f32[1,256,512]{2,1,0:T(8,128)}, f32[1,256,512]{2,1,0:T(8,128)S(1)}, u32[]{:S(2)}, u32[]{:S(2)}) collective-permute-start(f32[1,256,512]{2,1,0:T(8,128)} %param.5), channel_id=1, source_target_pairs={{0,8},{8,0},{16,24},{24,16},{1,9},{9,1},{17,25},{25,17},{2,10},{10... | collective-permute-start | bytes 1572872 | tf_op jit(solution)/shard_map/ppermute | solution.py:22
  1.2 14.5 %collective-permute-start.5 = (f32[1,256,512]{2,1,0:T(8,128)}, f32[1,256,512]{2,1,0:T(8,128)S(1)}, u32[]{:S(2)}, u32[]{:S(2)}) collective-permute-start(f32[1,256,512]{2,1,0:T(8,128)} %param.5), channel_id=1, source_target_pairs={{0,16},{8,24},{16,0},{24,8},{1,17},{9,25},{17,1},{25,9},{2,18},{10... | collective-permute-start | bytes 1572872 | tf_op jit(solution)/shard_map/ppermute | solution.py:22
  3.1 5.7 %collective-permute-start = (f32[3,8,256]{2,1,0:T(8,128)S(1)}, f32[3,8,256]{2,1,0:T(8,128)S(1)}, u32[]{:S(2)}, u32[]{:S(2)}) collective-permute-start(f32[3,8,256]{2,1,0:T(8,128)S(1)} %get-tuple-element.49), channel_id=1, source_target_pairs={{0,0},{1,2},{2,1},{3,3},{4,4},{5,6},{6,5},{7,7},{8,8},{9,10},{10,9... | collective-permute-start | bytes 73736 | tf_op jit(solution)/shard_map/ppermute | solution.py:34
  6.6 3.9 %collective-permute-start.1 = (f32[3,8,256]{2,1,0:T(8,128)S(1)}, f32[3,8,256]{2,1,0:T(8,128)S(1)}, u32[]{:S(2)}, u32[]{:S(2)}) collective-permute-start(f32[3,8,256]{2,1,0:T(8,128)S(1)} %get-tuple-element.48), channel_id=1, source_target_pairs={{0,1},{1,0},{2,3},{3,2},{4,5},{5,4},{6,7},{7,6},{8,9},{9,8},{10,11... | collective-permute-start | bytes 73736 | tf_op jit(solution)/shard_map/ppermute | solution.py:34
  10.7 1.3 %collective-permute-start.2 = (f32[3,8,640]{2,1,0:T(8,128)S(1)}, f32[3,8,640]{2,1,0:T(8,128)S(1)}, u32[]{:S(2)}, u32[]{:S(2)}) collective-permute-start(f32[3,8,640]{2,1,0:T(8,128)S(1)} %broadcast_select_fusion.3), channel_id=1, source_target_pairs={{0,4},{4,0},{1,5},{5,1},{2,6},{6,2},{3,7},{7,3},{8,12},{12,8},{9,1... | collective-permute-start | bytes 184328 | tf_op jit(solution)/shard_map/ppermute | solution.py:34
  12.1 7.4 %collective-permute-start.4 = (f32[16,512]{1,0:T(8,128)S(1)}, f32[16,512]{1,0:T(8,128)S(1)}, u32[]{:S(2)}, u32[]{:S(2)}) collective-permute-start(f32[16,512]{1,0:T(8,128)S(1)} %select_maximum_fusion), channel_id=1, source_target_pairs={{0,8},{8,0},{16,24},{24,16},{1,9},{9,1},{17,25},{25,17},{2,10},{10... | collective-permute-start | bytes 98312 | tf_op jit(solution)/shard_map/ppermute | solution.py:22
  13.6 4.3 %collective-permute-start.6 = (f32[16,512]{1,0:T(8,128)S(1)}, f32[16,512]{1,0:T(8,128)S(1)}, u32[]{:S(2)}, u32[]{:S(2)}) collective-permute-start(f32[16,512]{1,0:T(8,128)S(1)} %select_maximum_fusion), channel_id=1, source_target_pairs={{0,16},{8,24},{16,0},{24,8},{1,17},{9,25},{17,1},{25,9},{2,18},{10... | collective-permute-start | bytes 98312 | tf_op jit(solution)/shard_map/ppermute | solution.py:22
  15.2 8.7 %collective-permute-start.8 = (f32[144,512]{1,0:T(8,128)S(1)}, f32[144,512]{1,0:T(8,128)S(1)}, u32[]{:S(2)}, u32[]{:S(2)}) collective-permute-start(f32[144,512]{1,0:T(8,128)S(1)} %slice_bitcast_fusion), channel_id=1, source_target_pairs={{0,16},{8,24},{16,0},{24,8},{1,17},{9,25},{17,1},{25,9},{2,18},{10... | collective-permute-start | bytes 884744 | tf_op jit(solution)/shard_map/ppermute | solution.py:22
  15.8 7.6 %collective-permute-start.7 = (f32[112,512]{1,0:T(8,128)S(1)}, f32[112,512]{1,0:T(8,128)S(1)}, u32[]{:S(2)}, u32[]{:S(2)}) collective-permute-start(f32[112,512]{1,0:T(8,128)S(1)} %slice_bitcast_fusion.1), channel_id=1, source_target_pairs={{0,8},{8,0},{16,24},{24,16},{1,9},{9,1},{17,25},{25,17},{2,10},{10... | collective-permute-start | bytes 688136 | tf_op jit(solution)/shard_map/ppermute | solution.py:22
  18.0 5.4 %collective-permute-start.9 = (f32[16,512]{1,0:T(8,128)S(1)}, f32[16,512]{1,0:T(8,128)S(1)}, u32[]{:S(2)}, u32[]{:S(2)}) collective-permute-start(f32[16,512]{1,0:T(8,128)S(1)} %collective-permute-done.6.strip), channel_id=1, source_target_pairs={{0,8},{8,0},{16,24},{24,16},{1,9},{9,1},{17,25},{25,17},{2,10},{10... | collective-permute-start | bytes 98312 | tf_op jit(solution)/shard_map/ppermute | solution.py:22

commit v6 on v5

--- a/solution.py
+++ b/solution.py
@@ -10,8 +10,9 @@
 LANES = 128
 SUBLANES = 8
 BLOCK = 16
-SHARE = 7 / 16
-MIDDLE = 405
+CHUNKS = 8
+SHARE = 15 / 32
+MIDDLE = 430
 
 
 def round_up(value, step):
@@ -138,29 +139,28 @@
         self.over(body, dst)
 
     def first_part(self, kap, w, mid, lap_w, fa, fb, out, more=True, fc=None):
-
         def one(at):
             lw = self.lap(fa, at)
             lap_w[at, :] = lw
             f = w[at, :] + lw
-            mid[at, :] = f
             return kap[at, :] * f * f
 
         self.over(one, fb)
 
         def two(at):
-            v = mid[at, :] + self.lap(fb, at)
-            if more:
-                mid[at, :] = v
-            value = out(at, (v - w[at, :]) - 2.0 * lap_w[at, :])
-            return kap[at, :] * v * v if more else value
+            lw, lf = lap_w[at, :], self.lap(fb, at)
+            value = out(at, lf - lw)
+            if not more:
+                return value
+            mid[at, :] = lf - 3.0 * lw
+            v = w[at, :] + lw + lf
+            return kap[at, :] * v * v
 
         self.over(two, fa if more else fc)
 
-    def second_part(self, w, mid, lap_w, fa, out):
+    def second_part(self, mid, fa, out):
         def one(at):
-            q = w[at, :] + 4.0 * lap_w[at, :]
-            out(at, mid[at, :] + 2.0 * self.lap(fa, at) - q)
+            out(at, mid[at, :] + 2.0 * self.lap(fa, at))
 
         self.over(one)
 
@@ -191,10 +191,13 @@
             def out(at, h):
                 even[step, at, :] = h
 
-            grid.second_part(wk, mid, lap_w, fa, out)
-
-
-def start_kernel(grid, kappa, initial, before, after, left, right, kap, even, tail, low, wk, mid, lap_w, fa, fb):
+            grid.second_part(mid, fa, out)
+
+
+def start_kernel(
+    grid, kappa, initial, before, after, left, right, kap, even, tail, c_out, f_out, wk, low, fa, fb, sems
+):
+    rows, width = grid.rows, grid.width
     ix, last_ix = lax.axis_index("sx"), lax.axis_size("sx") - 1
     iy, last_iy = lax.axis_index("sy"), lax.axis_size("sy") - 1
     grid.fill(
@@ -204,17 +207,39 @@
     )
     grid.fill(wk, [initial], before[1], after[1], left[1], right[1], kap, fa)
 
-    def out(at, g):
-        x, lx = wk[at, :], lap_w[at, :]
-        tail[at, :] = x + 2.0 * lx + g
-        low[at, :] = x + lx
-
-    grid.first_part(kap, wk, mid, lap_w, fa, fb, out)
-
-    def out_even(at, h):
-        even[0, at, :] = (wk[at, :] + 4.0 * lap_w[at, :]) + h
-
-    grid.second_part(wk, mid, lap_w, fa, out_even)
+    def one(at):
+        f = wk[at, :] + grid.lap(fa, at)
+        low[at, :] = f
+        return kap[at, :] * f * f
+
+    grid.over(one, fb)
+
+    def two(at):
+        v = low[at, :] + grid.lap(fb, at)
+        tail[at, :] = v
+        return kap[at, :] * v * v
+
+    grid.over(two, fa)
+    here = lax.axis_index("tm")
+    tile = (slice(0, rows), slice(0, width))
+    copies = [
+        pltpu.make_async_copy(src.at[tile], dst.at[0], sems.at[i])
+        for i, (src, dst) in enumerate(((tail, c_out), (low, f_out)))
+    ]
+
+    @pl.when(here == 0)
+    def _():
+        for copy in copies:
+            copy.start()
+        for copy in copies:
+            copy.wait()
+
+    @pl.when(here > 0)
+    def _():
+        def three(at):
+            even[0, at, :] = tail[at, :] + 2.0 * grid.lap(fa, at)
+
+        grid.over(three)
 
 
 def loader(grid, kap, tile, strip):
@@ -236,7 +261,9 @@
         absorb(grid, kap, point, here, loader(grid, kap, [tile], strip), even, odd, tail, work)
 
 
-def last_kernel(grid, count, kap, even, odd_in, tail_in, low, first, second, strip, c_out, f_out, odd, tail, *work):
+def last_kernel(
+    grid, count, kap, even, odd_in, tail_in, first, second, strip, c_in, f_in, c_out, f_out, odd, tail, *work
+):
     wk, mid, lap_w, fa, fb, fc, c_rows, f_rows, sems = work
     here = lax.axis_index("tm")
     point = (here ^ (count - 1)) + 1
@@ -257,14 +284,6 @@
             if stop % chunk == 0 or stop == rows:
                 sent(which, (stop - 1) // chunk).start()
 
-    @pl.when(here == 0)
-    def _():
-        def body(at):
-            put(0, at, tail[at, :])
-            put(1, at, low[at, :])
-
-        grid.over(body)
-
     @pl.when(here == 1)
     def _():
         def body(at):
@@ -346,9 +365,11 @@
 
             grid.over(last)
 
-    for which in (0, 1):
-        for i in range(-(-rows // chunk)):
-            sent(which, i).wait()
+    @pl.when(here > 0)
+    def _():
+        for which in (0, 1):
+            for i in range(-(-rows // chunk)):
+                sent(which, i).wait()
 
 
 def on_device(initial, kappa, c_guess):
@@ -357,7 +378,7 @@
     steps = count // 2
     halo, deep = round_up(steps + 3, SUBLANES), steps + 2
     grid = Grid(rows, width, halo, deep)
-    share = round_up(int(rows * SHARE), BLOCK)
+    share = round_up(int(rows * SHARE), SUBLANES)
     ext, padded = grid.ext, grid.padded
     work = [ext] * 3 + [padded] * 2
     sides = (steps, *ext)
@@ -398,9 +419,11 @@
             strips[bit] = swap(strip, "tm", bit)
 
     before, strip = together(before, strip)
-    kap, even, tail, low = call(functools.partial(start_kernel, grid), [ext, sides, ext, ext], work, 4)(
-        kappa, initial, before, after, left, right
-    )
+    outside, inside = pl.BlockSpec(memory_space=pltpu.HBM), pl.BlockSpec(memory_space=pltpu.VMEM)
+    kap, even, tail, c_new, f_new = call(
+        functools.partial(start_kernel, grid), [ext, sides, ext] + [c_guess.shape] * 2, [ext] * 2 + [padded] * 2, 4,
+        semaphores=(2,), out_specs=[inside] * 3 + [outside] * 2,
+    )(kappa, initial, before, after, left, right)
     odd = jnp.zeros(sides, jnp.float32)
 
     for d in several:
@@ -417,9 +440,9 @@
             )(kap, even, odd, tail, tiles[d], strips[d])
     c_new, f_new, _, _ = call(
         functools.partial(last_kernel, grid, count), [c_guess.shape] * 2 + [sides, ext],
-        work + [padded] + [(rows, width)] * 2, 8, semaphores=(2, 4), input_output_aliases={2: 2, 3: 3},
-        out_specs=[pl.BlockSpec(memory_space=space) for space in (pl.ANY, pl.ANY, pltpu.VMEM, pltpu.VMEM)],
-    )(kap, even, odd, tail, low, first, second, strips[last])
+        work + [padded] + [(rows, width)] * 2, 8, semaphores=(2, CHUNKS), input_output_aliases={2: 2, 3: 3, 7: 0, 8: 1},
+        in_specs=[inside] * 7 + [outside] * 2, out_specs=[outside] * 2 + [inside] * 2,
+    )(kap, even, odd, tail, first, second, strips[last], c_new, f_new)
     return c_new, f_new
 
 

time: 26.8 us -> 26.6 us (level)
  transfers between devices with their start and end apart: 10 -> 10, of which waited for: 5 -> 4; matrix products, arithmetic and copies ran while one was open for 8% -> 8% of each run, Pallas kernels for 17% -> 16%
where the time goes in v6:
time: 26.6 us; the launch traced here: 26.3 us
  starting transfers between devices  10.5 us (39%)
  Pallas kernels  6.83 us (26%)
  waiting for transfers between devices  6.05 us (23%)
  local copies, waits for them, and re-layouts  1.9 us (7%)
  between operations  0.87 us (3%)
    ppermute x7, starting transfers between devices, swap(): lax.ppermute(x, axis, [(i, i ^ bits) for i in range(lax.axis_size(axis))])  6.91 us
    ppermute x3, waiting for transfers between devices, neighbours(): lax.ppermute(send, axis, sorted(pairs.items()))  4.24 us
    ppermute x3, starting transfers between devices, neighbours(): lax.ppermute(send, axis, sorted(pairs.items()))  3.63 us
    pallas_call x1, Pallas kernels, on_device(): call(functools.partial(last_kernel, grid, count), [c_guess.shape] * 2 + [...  2.55 us
    pallas_call x2, Pallas kernels, on_device(): call(functools.partial(middle_kernel, grid, d), [sides, sides, ext], work...  2.43 us
    ppermute x7, waiting for transfers between devices, swap(): lax.ppermute(x, axis, [(i, i ^ bits) for i in range(lax.axis_size(axis))])  1.81 us
    pallas_call x1, Pallas kernels, on_device(): call(functools.partial(start_kernel, grid), [ext, sides, ext] + [c_guess....  1.43 us
    squeeze x1, local copies, waits for them, and re-layouts, on_device(): c_guess[0, :, :LANES]  0.99 us
  transfers between devices with their start and end apart: 10, of which 4 were waited for; matrix products, arithmetic and copies ran while one was open for 8% of the time, Pallas kernels for 16%

profile of v6, /device:TPU:14, one launch (start us, length us, event | category | flops | bytes accessed | tf_op | source)
XLA Modules:
  0.0 26.3 jit_solution(12866889841376047913)
XLA Ops:
  0.6 0.6 %collective-permute-start.3 = (f32[1,256,512]{2,1,0:T(8,128)}, f32[1,256,512]{2,1,0:T(8,128)S(1)}, u32[]{:S(2)}, u32[]{:S(2)}) collective-permute-start(f32[1,256,512]{2,1,0:T(8,128)} %param.5), channel_id=1, source_target_pairs={{0,8},{8,0},{16,24},{24,16},{1,9},{9,1},{17,25},{25,17},{2,10},{10... | collective-permute-start | bytes 1572872 | tf_op jit(solution)/shard_map/ppermute | solution.py:23
  1.2 0.5 %collective-permute-start.5 = (f32[1,256,512]{2,1,0:T(8,128)}, f32[1,256,512]{2,1,0:T(8,128)S(1)}, u32[]{:S(2)}, u32[]{:S(2)}) collective-permute-start(f32[1,256,512]{2,1,0:T(8,128)} %param.5), channel_id=1, source_target_pairs={{0,16},{8,24},{16,0},{24,8},{1,17},{9,25},{17,1},{25,9},{2,18},{10... | collective-permute-start | bytes 1572872 | tf_op jit(solution)/shard_map/ppermute | solution.py:23
  1.8 1.0 %slice_bitcast_fusion.3 = (f32[256,128]{1,0:T(8,128)S(1)}, f32[256,128]{1,0:T(8,128)S(1)}) fusion(f32[1,256,512]{2,1,0:T(8,128)} %param.5), kind=kLoop, calls=%fused_computation.4 | loop fusion | bytes 524288 | tf_op jit(solution)/shard_map/squeeze | solution.py:396
  2.8 0.3 shard_map.50
  3.1 3.5 %collective-permute-start = (f32[3,8,256]{2,1,0:T(8,128)S(1)}, f32[3,8,256]{2,1,0:T(8,128)S(1)}, u32[]{:S(2)}, u32[]{:S(2)}) collective-permute-start(f32[3,8,256]{2,1,0:T(8,128)S(1)} %get-tuple-element.51), channel_id=1, source_target_pairs={{0,0},{1,2},{2,1},{3,3},{4,4},{5,6},{6,5},{7,7},{8,8},{9,10},{10,9... | collective-permute-start | bytes 73736 | tf_op jit(solution)/shard_map/ppermute | solution.py:35
  6.6 0.1 collective-permute-start.1
  6.7 0.7 %slice_bitcast_fusion.4 = (f32[8,512]{1,0:T(8,128)S(1)}, f32[8,512]{1,0:T(8,128)S(1)}) fusion(f32[1,256,512]{2,1,0:T(8,128)} %param.5), kind=kLoop, calls=%fused_computation.16 | loop fusion | bytes 65536 | tf_op jit(solution)/shard_map/slice | solution.py:402
  7.5 1.4 %collective-permute-done = f32[3,8,256]{2,1,0:T(8,128)S(1)} collective-permute-done((f32[3,8,256]{2,1,0:T(8,128)S(1)}, f32[3,8,256]{2,1,0:T(8,128)S(1)}, u32[]{:S(2)}, u32[]{:S(2)}) %collective-permute-start) | collective-permute-done | bytes 24608 | tf_op jit(solution)/shard_map/ppermute | solution.py:35
  8.8 1.7 %collective-permute-done.1 = f32[3,8,256]{2,1,0:T(8,128)S(1)} collective-permute-done((f32[3,8,256]{2,1,0:T(8,128)S(1)}, f32[3,8,256]{2,1,0:T(8,128)S(1)}, u32[]{:S(2)}, u32[]{:S(2)}) %collective-permute-start.1) | collective-permute-done | bytes 24608 | tf_op jit(solution)/shard_map/ppermute | solution.py:35
  10.5 0.2 shard_map.51
  10.7 0.1 collective-permute-start.2
  10.8 1.2 %collective-permute-done.2 = f32[3,8,640]{2,1,0:T(8,128)S(1)} collective-permute-done((f32[3,8,640]{2,1,0:T(8,128)S(1)}, f32[3,8,640]{2,1,0:T(8,128)S(1)}, u32[]{:S(2)}, u32[]{:S(2)}) %collective-permute-start.2) | collective-permute-done | bytes 61472 | tf_op jit(solution)/shard_map/ppermute | solution.py:35
  12.1 1.6 %collective-permute-start.4 = (f32[16,512]{1,0:T(8,128)S(1)}, f32[16,512]{1,0:T(8,128)S(1)}, u32[]{:S(2)}, u32[]{:S(2)}) collective-permute-start(f32[16,512]{1,0:T(8,128)S(1)} %select_maximum_fusion), channel_id=1, source_target_pairs={{0,8},{8,0},{16,24},{24,16},{1,9},{9,1},{17,25},{25,17},{2,10},{10... | collective-permute-start | bytes 98312 | tf_op jit(solution)/shard_map/ppermute | solution.py:23
  13.6 1.5 %collective-permute-start.6 = (f32[16,512]{1,0:T(8,128)S(1)}, f32[16,512]{1,0:T(8,128)S(1)}, u32[]{:S(2)}, u32[]{:S(2)}) collective-permute-start(f32[16,512]{1,0:T(8,128)S(1)} %select_maximum_fusion), channel_id=1, source_target_pairs={{0,16},{8,24},{16,0},{24,8},{1,17},{9,25},{17,1},{25,9},{2,18},{10... | collective-permute-start | bytes 98312 | tf_op jit(solution)/shard_map/ppermute | solution.py:23
  15.2 0.6 %collective-permute-start.8 = (f32[136,512]{1,0:T(8,128)S(1)}, f32[136,512]{1,0:T(8,128)S(1)}, u32[]{:S(2)}, u32[]{:S(2)}) collective-permute-start(f32[136,512]{1,0:T(8,128)S(1)} %slice_bitcast_fusion), channel_id=1, source_target_pairs={{0,16},{8,24},{16,0},{24,8},{1,17},{9,25},{17,1},{25,9},{2,18},{10... | collective-permute-start | bytes 835592 | tf_op jit(solution)/shard_map/ppermute | solution.py:23
  15.8 0.6 %collective-permute-start.7 = (f32[120,512]{1,0:T(8,128)S(1)}, f32[120,512]{1,0:T(8,128)S(1)}, u32[]{:S(2)}, u32[]{:S(2)}) collective-permute-start(f32[120,512]{1,0:T(8,128)S(1)} %slice_bitcast_fusion.1), channel_id=1, source_target_pairs={{0,8},{8,0},{16,24},{24,16},{1,9},{9,1},{17,25},{25,17},{2,10},{10... | collective-permute-start | bytes 737288 | tf_op jit(solution)/shard_map/ppermute | solution.py:23
  16.4 1.4 %shard_map.52 = (f32[272,640]{1,0:T(8,128)S(1)}, f32[2,272,640]{2,1,0:T(8,128)S(1)}, f32[272,640]{1,0:T(8,128)S(1)}, f32[1,256,512]{2,1,0:T(8,128)}, f32[1,256,512]{2,1,0:T(8,128)}) custom-call(f32[256,512]{1,0:T(8,128)S(1)} %copy-done, f32[256,512]{1,0:T(8,128)S(1)} %copy-done.1, f32[3,8,640]{2,1,0:T(8,128)S(1)} %get-tuple-element.24.before, ...), custom_call_target="tpu_custom_call" | custom-call | flops 11141120 | bytes 16711680 | tf_op jit(solution)/shard_map/pallas_call | solution.py:423
  17.9 0.0 collective-permute-done.6.strip
  17.9 1.5 %collective-permute-start.9 = (f32[16,512]{1,0:T(8,128)S(1)}, f32[16,512]{1,0:T(8,128)S(1)}, u32[]{:S(2)}, u32[]{:S(2)}) collective-permute-start(f32[16,512]{1,0:T(8,128)S(1)} %collective-permute-done.6.strip), channel_id=1, source_target_pairs={{0,8},{8,0},{16,24},{24,16},{1,9},{9,1},{17,25},{25,17},{2,10},{10... | collective-permute-start | bytes 98312 | tf_op jit(solution)/shard_map/ppermute | solution.py:23
  19.4 0.1 broadcast_in_dim.3.odd_in
  19.5 0.9 %shard_map.53 = (f32[2,272,640]{2,1,0:T(8,128)S(1)}, f32[2,272,640]{2,1,0:T(8,128)S(1)}, f32[272,640]{1,0:T(8,128)S(1)}) custom-call(f32[272,640]{1,0:T(8,128)S(1)} %get-tuple-element.25.kap, f32[2,272,640]{2,1,0:T(8,128)S(1)} %get-tuple-element.26.even_in, ...), custom_call_target="tpu_custom_call", output_to_operand_aliasing={{0}: (1, {}), {1}: (2, {}), {2}: (3, {})} | custom-call | flops 1197670400 | bytes 1796505600 | tf_op jit(solution)/shard_map/pallas_call | solution.py:437
  20.4 1.5 %shard_map.54 = (f32[2,272,640]{2,1,0:T(8,128)S(1)}, f32[2,272,640]{2,1,0:T(8,128)S(1)}, f32[272,640]{1,0:T(8,128)S(1)}) custom-call(f32[272,640]{1,0:T(8,128)S(1)} %get-tuple-element.25.kap, f32[2,272,640]{2,1,0:T(8,128)S(1)} %get-tuple-element.28.even_in, ...), custom_call_target="tpu_custom_call", output_to_operand_aliasing={{0}: (1, {}), {1}: (2, {}), {2}: (3, {})} | custom-call | flops 1197670400 | bytes 1796505600 | tf_op jit(solution)/shard_map/pallas_call | solution.py:437
  21.9 1.8 %collective-permute-done.9.strip = f32[16,512]{1,0:T(8,128)S(1)} collective-permute-done((f32[16,512]{1,0:T(8,128)S(1)}, f32[16,512]{1,0:T(8,128)S(1)}, u32[]{:S(2)}, u32[]{:S(2)}) %collective-permute-start.9) | collective-permute-done | bytes 32800 | tf_op jit(solution)/shard_map/ppermute | solution.py:23
  23.7 2.6 %shard_map.55 = (f32[1,256,512]{2,1,0:T(8,128)}, f32[1,256,512]{2,1,0:T(8,128)}, f32[2,272,640]{2,1,0:T(8,128)S(1)}, f32[272,640]{1,0:T(8,128)S(1)}) custom-call(f32[272,640]{1,0:T(8,128)S(1)} %get-tuple-element.25.kap, f32[2,272,640]{2,1,0:T(8,128)S(1)} %get-tuple-element.31.even, ...), custom_call_target="tpu_custom_call", output_to_operand_aliasing={{2}: (2, {}), {3}: (3, {}), {0}: (7, {}), {1}: (8, {})} | custom-call | flops 22282240 | bytes 33423360 | tf_op jit(solution)/shard_map/pallas_call | solution.py:441
  (25 shorter events, 0.2 us)
Async XLA Ops:
  0.6 2.2 %copy-start.1 = (f32[256,512]{1,0:T(8,128)S(1)}, f32[256,512]{1,0:T(8,128)}, u32[]{:S(2)}) copy-start(f32[256,512]{1,0:T(8,128)} %initial.1) | copy-start | bytes 1572868
  0.6 2.2 %copy-start = (f32[256,512]{1,0:T(8,128)S(1)}, f32[256,512]{1,0:T(8,128)}, u32[]{:S(2)}) copy-start(f32[256,512]{1,0:T(8,128)} %kappa.1) | copy-start | bytes 1572868
  0.6 14.5 %collective-permute-start.3 = (f32[1,256,512]{2,1,0:T(8,128)}, f32[1,256,512]{2,1,0:T(8,128)S(1)}, u32[]{:S(2)}, u32[]{:S(2)}) collective-permute-start(f32[1,256,512]{2,1,0:T(8,128)} %param.5), channel_id=1, source_target_pairs={{0,8},{8,0},{16,24},{24,16},{1,9},{9,1},{17,25},{25,17},{2,10},{10... | collective-permute-start | bytes 1572872 | tf_op jit(solution)/shard_map/ppermute | solution.py:23
  1.2 14.5 %collective-permute-start.5 = (f32[1,256,512]{2,1,0:T(8,128)}, f32[1,256,512]{2,1,0:T(8,128)S(1)}, u32[]{:S(2)}, u32[]{:S(2)}) collective-permute-start(f32[1,256,512]{2,1,0:T(8,128)} %param.5), channel_id=1, source_target_pairs={{0,16},{8,24},{16,0},{24,8},{1,17},{9,25},{17,1},{25,9},{2,18},{10... | collective-permute-start | bytes 1572872 | tf_op jit(solution)/shard_map/ppermute | solution.py:23
  3.1 5.7 %collective-permute-start = (f32[3,8,256]{2,1,0:T(8,128)S(1)}, f32[3,8,256]{2,1,0:T(8,128)S(1)}, u32[]{:S(2)}, u32[]{:S(2)}) collective-permute-start(f32[3,8,256]{2,1,0:T(8,128)S(1)} %get-tuple-element.51), channel_id=1, source_target_pairs={{0,0},{1,2},{2,1},{3,3},{4,4},{5,6},{6,5},{7,7},{8,8},{9,10},{10,9... | collective-permute-start | bytes 73736 | tf_op jit(solution)/shard_map/ppermute | solution.py:35
  6.6 3.9 %collective-permute-start.1 = (f32[3,8,256]{2,1,0:T(8,128)S(1)}, f32[3,8,256]{2,1,0:T(8,128)S(1)}, u32[]{:S(2)}, u32[]{:S(2)}) collective-permute-start(f32[3,8,256]{2,1,0:T(8,128)S(1)} %get-tuple-element.50), channel_id=1, source_target_pairs={{0,1},{1,0},{2,3},{3,2},{4,5},{5,4},{6,7},{7,6},{8,9},{9,8},{10,11... | collective-permute-start | bytes 73736 | tf_op jit(solution)/shard_map/ppermute | solution.py:35
  10.7 1.3 %collective-permute-start.2 = (f32[3,8,640]{2,1,0:T(8,128)S(1)}, f32[3,8,640]{2,1,0:T(8,128)S(1)}, u32[]{:S(2)}, u32[]{:S(2)}) collective-permute-start(f32[3,8,640]{2,1,0:T(8,128)S(1)} %broadcast_select_fusion.3), channel_id=1, source_target_pairs={{0,4},{4,0},{1,5},{5,1},{2,6},{6,2},{3,7},{7,3},{8,12},{12,8},{9,1... | collective-permute-start | bytes 184328 | tf_op jit(solution)/shard_map/ppermute | solution.py:35
  12.1 7.3 %collective-permute-start.4 = (f32[16,512]{1,0:T(8,128)S(1)}, f32[16,512]{1,0:T(8,128)S(1)}, u32[]{:S(2)}, u32[]{:S(2)}) collective-permute-start(f32[16,512]{1,0:T(8,128)S(1)} %select_maximum_fusion), channel_id=1, source_target_pairs={{0,8},{8,0},{16,24},{24,16},{1,9},{9,1},{17,25},{25,17},{2,10},{10... | collective-permute-start | bytes 98312 | tf_op jit(solution)/shard_map/ppermute | solution.py:23
  13.6 4.2 %collective-permute-start.6 = (f32[16,512]{1,0:T(8,128)S(1)}, f32[16,512]{1,0:T(8,128)S(1)}, u32[]{:S(2)}, u32[]{:S(2)}) collective-permute-start(f32[16,512]{1,0:T(8,128)S(1)} %select_maximum_fusion), channel_id=1, source_target_pairs={{0,16},{8,24},{16,0},{24,8},{1,17},{9,25},{17,1},{25,9},{2,18},{10... | collective-permute-start | bytes 98312 | tf_op jit(solution)/shard_map/ppermute | solution.py:23
  15.2 8.5 %collective-permute-start.8 = (f32[136,512]{1,0:T(8,128)S(1)}, f32[136,512]{1,0:T(8,128)S(1)}, u32[]{:S(2)}, u32[]{:S(2)}) collective-permute-start(f32[136,512]{1,0:T(8,128)S(1)} %slice_bitcast_fusion), channel_id=1, source_target_pairs={{0,16},{8,24},{16,0},{24,8},{1,17},{9,25},{17,1},{25,9},{2,18},{10... | collective-permute-start | bytes 835592 | tf_op jit(solution)/shard_map/ppermute | solution.py:23
  15.8 7.9 %collective-permute-start.7 = (f32[120,512]{1,0:T(8,128)S(1)}, f32[120,512]{1,0:T(8,128)S(1)}, u32[]{:S(2)}, u32[]{:S(2)}) collective-permute-start(f32[120,512]{1,0:T(8,128)S(1)} %slice_bitcast_fusion.1), channel_id=1, source_target_pairs={{0,8},{8,0},{16,24},{24,16},{1,9},{9,1},{17,25},{25,17},{2,10},{10... | collective-permute-start | bytes 737288 | tf_op jit(solution)/shard_map/ppermute | solution.py:23
  17.9 5.9 %collective-permute-start.9 = (f32[16,512]{1,0:T(8,128)S(1)}, f32[16,512]{1,0:T(8,128)S(1)}, u32[]{:S(2)}, u32[]{:S(2)}) collective-permute-start(f32[16,512]{1,0:T(8,128)S(1)} %collective-permute-done.6.strip), channel_id=1, source_target_pairs={{0,8},{8,0},{16,24},{24,16},{1,9},{9,1},{17,25},{25,17},{2,10},{10... | collective-permute-start | bytes 98312 | tf_op jit(solution)/shard_map/ppermute | solution.py:23

commit v7 on v6

--- a/solution.py
+++ b/solution.py
@@ -10,7 +10,7 @@
 LANES = 128
 SUBLANES = 8
 BLOCK = 16
-CHUNKS = 8
+CHUNKS = 4
 SHARE = 15 / 32
 MIDDLE = 430
 
@@ -180,7 +180,7 @@
     @pl.when(lax.rem(point, 2) == 0)
     def _():
         def out(at, g):
-            tail[at, :] = g
+            tail[at, :] = g if lax.axis_size("tm") <= 4 else jnp.where(step == lax.div(here, 2), g, tail[at, :])
 
         grid.first_part(kap, wk, mid, lap_w, fa, fb, out, not own_only)
         if own_only:
@@ -255,21 +255,30 @@
 def middle_kernel(grid, bits, kap, even_in, odd_in, tail_in, tile, strip, even, odd, tail, *work):
     here = lax.axis_index("tm")
     point = (here ^ bits) + 1
+    even[...], odd[...], tail[...] = even_in[...], odd_in[...], tail_in[...]
 
     @pl.when(point <= here)
     def _():
         absorb(grid, kap, point, here, loader(grid, kap, [tile], strip), even, odd, tail, work)
 
 
-def last_kernel(
-    grid, count, kap, even, odd_in, tail_in, first, second, strip, c_in, f_in, c_out, f_out, odd, tail, *work
-):
-    wk, mid, lap_w, fa, fb, fc, c_rows, f_rows, sems = work
+def last_kernel(grid, count, kap, even, odd, tail, first, second, strip, c_in, f_in, c_out, f_out, *work):
+    wk, mid, lap_w, fa, fb, fc, c_rows, f_rows, even_own, odd_own, tail_own, sems = work
     here = lax.axis_index("tm")
     point = (here ^ (count - 1)) + 1
     rows, width = grid.rows, grid.width
     load = loader(grid, kap, [first, second], strip)
     state = wk
+    tail_even = tail_own
+    if count != 4:
+        even_own[...], odd_own[...], tail_own[...] = even[...], odd[...], tail[...]
+        even, odd, tail = even_own, odd_own, tail_own
+    if count == 2:
+
+        @pl.when(here == 1)
+        def _():
+            absorb(grid, kap, point, here, load, even, odd, tail, work[:5])
+
     chunk = round_up(-(-rows // sems.shape[1]), BLOCK)
 
     def sent(which, i):
@@ -315,7 +324,7 @@
         def _():
             @pl.when(point <= here)
             def _():
-                absorb(grid, kap, point, here, load, even, odd, tail, work[:5], count == 4)
+                absorb(grid, kap, point, here, load, even, odd_own, tail_own, work[:5], count == 4)
 
             def begin(at):
                 x = even[0, at, :] + odd[0, at, :]
@@ -342,7 +351,7 @@
         def _():
             def body(at):
                 x, lx = state[at, :], grid.lap(fc, at)
-                put(0, at, x + 2.0 * lx + tail[at, :])
+                put(0, at, x + 2.0 * lx + tail_even[at, :])
                 put(1, at, x + lx)
 
             grid.over(body)
@@ -438,10 +447,11 @@
                 functools.partial(middle_kernel, grid, d), [sides, sides, ext], work, MIDDLE,
                 input_output_aliases={1: 0, 2: 1, 3: 2},
             )(kap, even, odd, tail, tiles[d], strips[d])
-    c_new, f_new, _, _ = call(
-        functools.partial(last_kernel, grid, count), [c_guess.shape] * 2 + [sides, ext],
-        work + [padded] + [(rows, width)] * 2, 8, semaphores=(2, CHUNKS), input_output_aliases={2: 2, 3: 3, 7: 0, 8: 1},
-        in_specs=[inside] * 7 + [outside] * 2, out_specs=[outside] * 2 + [inside] * 2,
+    own = [sides, sides, ext] if count != 4 else [(1, *grid.ext), (1, *grid.ext), ext]
+    c_new, f_new = call(
+        functools.partial(last_kernel, grid, count), [c_guess.shape] * 2, work + [padded] + [(rows, width)] * 2 + own, 8,
+        semaphores=(2, CHUNKS), input_output_aliases={7: 0, 8: 1},
+        in_specs=[inside] * 7 + [outside] * 2, out_specs=[outside] * 2,
     )(kap, even, odd, tail, first, second, strips[last], c_new, f_new)
     return c_new, f_new
 

time: 26.6 us -> 26.5 us (level)
  waiting for transfers between devices: 6.05 us -> 5.17 us
  Pallas kernels: 6.83 us -> 7.66 us
    ppermute x7, waiting for transfers between devices: 1.81 us -> 0.93 us  [swap(): lax.ppermute(x, axis, [(i, i ^ bits) for i in range(lax.axis_size(axis))])]
    pallas_call x2, Pallas kernels: 2.43 us -> 3.31 us  [on_device(): call(functools.partial(middle_kernel, grid, d), [sides, sides, ext], work...]
  transfers between devices with their start and end apart: 10 -> 10, of which waited for: 4 -> 4; matrix products, arithmetic and copies ran while one was open for 8% -> 8% of each run, Pallas kernels for 16% -> 20%
where the time goes in v7:
time: 26.5 us; the launch traced here: 26.2 us
  starting transfers between devices  10.5 us (40%)
  Pallas kernels  7.66 us (29%)
  waiting for transfers between devices  5.17 us (20%)
  local copies, waits for them, and re-layouts  1.9 us (7%)
  between operations  0.87 us (3%)
    ppermute x7, starting transfers between devices, swap(): lax.ppermute(x, axis, [(i, i ^ bits) for i in range(lax.axis_size(axis))])  6.91 us
    ppermute x3, waiting for transfers between devices, neighbours(): lax.ppermute(send, axis, sorted(pairs.items()))  4.24 us
    ppermute x3, starting transfers between devices, neighbours(): lax.ppermute(send, axis, sorted(pairs.items()))  3.63 us
    pallas_call x2, Pallas kernels, on_device(): call(functools.partial(middle_kernel, grid, d), [sides, sides, ext], work...  3.31 us
    pallas_call x1, Pallas kernels, on_device(): call(functools.partial(last_kernel, grid, count), [c_guess.shape] * 2, wo...  2.5 us
    pallas_call x1, Pallas kernels, on_device(): call(functools.partial(start_kernel, grid), [ext, sides, ext] + [c_guess....  1.43 us
    squeeze x1, local copies, waits for them, and re-layouts, on_device(): c_guess[0, :, :LANES]  0.99 us
    ppermute x7, waiting for transfers between devices, swap(): lax.ppermute(x, axis, [(i, i ^ bits) for i in range(lax.axis_size(axis))])  0.93 us
  transfers between devices with their start and end apart: 10, of which 4 were waited for; matrix products, arithmetic and copies ran while one was open for 8% of the time, Pallas kernels for 20%

profile of v7, /device:TPU:14, one launch (start us, length us, event | category | flops | bytes accessed | tf_op | source)
XLA Modules:
  0.0 26.2 jit_solution(8066885993118344706)
XLA Ops:
  0.6 0.6 %collective-permute-start.3 = (f32[1,256,512]{2,1,0:T(8,128)}, f32[1,256,512]{2,1,0:T(8,128)S(1)}, u32[]{:S(2)}, u32[]{:S(2)}) collective-permute-start(f32[1,256,512]{2,1,0:T(8,128)} %param.5), channel_id=1, source_target_pairs={{0,8},{8,0},{16,24},{24,16},{1,9},{9,1},{17,25},{25,17},{2,10},{10... | collective-permute-start | bytes 1572872 | tf_op jit(solution)/shard_map/ppermute | solution.py:23
  1.2 0.5 %collective-permute-start.5 = (f32[1,256,512]{2,1,0:T(8,128)}, f32[1,256,512]{2,1,0:T(8,128)S(1)}, u32[]{:S(2)}, u32[]{:S(2)}) collective-permute-start(f32[1,256,512]{2,1,0:T(8,128)} %param.5), channel_id=1, source_target_pairs={{0,16},{8,24},{16,0},{24,8},{1,17},{9,25},{17,1},{25,9},{2,18},{10... | collective-permute-start | bytes 1572872 | tf_op jit(solution)/shard_map/ppermute | solution.py:23
  1.8 1.0 %slice_bitcast_fusion.3 = (f32[256,128]{1,0:T(8,128)S(1)}, f32[256,128]{1,0:T(8,128)S(1)}) fusion(f32[1,256,512]{2,1,0:T(8,128)} %param.5), kind=kLoop, calls=%fused_computation.4 | loop fusion | bytes 524288 | tf_op jit(solution)/shard_map/squeeze | solution.py:405
  2.8 0.3 shard_map.50
  3.1 3.5 %collective-permute-start = (f32[3,8,256]{2,1,0:T(8,128)S(1)}, f32[3,8,256]{2,1,0:T(8,128)S(1)}, u32[]{:S(2)}, u32[]{:S(2)}) collective-permute-start(f32[3,8,256]{2,1,0:T(8,128)S(1)} %get-tuple-element.47), channel_id=1, source_target_pairs={{0,0},{1,2},{2,1},{3,3},{4,4},{5,6},{6,5},{7,7},{8,8},{9,10},{10,9... | collective-permute-start | bytes 73736 | tf_op jit(solution)/shard_map/ppermute | solution.py:35
  6.6 0.1 collective-permute-start.1
  6.7 0.7 %slice_bitcast_fusion.4 = (f32[8,512]{1,0:T(8,128)S(1)}, f32[8,512]{1,0:T(8,128)S(1)}) fusion(f32[1,256,512]{2,1,0:T(8,128)} %param.5), kind=kLoop, calls=%fused_computation.16 | loop fusion | bytes 65536 | tf_op jit(solution)/shard_map/slice | solution.py:411
  7.5 1.4 %collective-permute-done = f32[3,8,256]{2,1,0:T(8,128)S(1)} collective-permute-done((f32[3,8,256]{2,1,0:T(8,128)S(1)}, f32[3,8,256]{2,1,0:T(8,128)S(1)}, u32[]{:S(2)}, u32[]{:S(2)}) %collective-permute-start) | collective-permute-done | bytes 24608 | tf_op jit(solution)/shard_map/ppermute | solution.py:35
  8.8 1.7 %collective-permute-done.1 = f32[3,8,256]{2,1,0:T(8,128)S(1)} collective-permute-done((f32[3,8,256]{2,1,0:T(8,128)S(1)}, f32[3,8,256]{2,1,0:T(8,128)S(1)}, u32[]{:S(2)}, u32[]{:S(2)}) %collective-permute-start.1) | collective-permute-done | bytes 24608 | tf_op jit(solution)/shard_map/ppermute | solution.py:35
  10.5 0.2 shard_map.51
  10.7 0.1 collective-permute-start.2
  10.8 1.2 %collective-permute-done.2 = f32[3,8,640]{2,1,0:T(8,128)S(1)} collective-permute-done((f32[3,8,640]{2,1,0:T(8,128)S(1)}, f32[3,8,640]{2,1,0:T(8,128)S(1)}, u32[]{:S(2)}, u32[]{:S(2)}) %collective-permute-start.2) | collective-permute-done | bytes 61472 | tf_op jit(solution)/shard_map/ppermute | solution.py:35
  12.1 1.6 %collective-permute-start.4 = (f32[16,512]{1,0:T(8,128)S(1)}, f32[16,512]{1,0:T(8,128)S(1)}, u32[]{:S(2)}, u32[]{:S(2)}) collective-permute-start(f32[16,512]{1,0:T(8,128)S(1)} %select_maximum_fusion), channel_id=1, source_target_pairs={{0,8},{8,0},{16,24},{24,16},{1,9},{9,1},{17,25},{25,17},{2,10},{10... | collective-permute-start | bytes 98312 | tf_op jit(solution)/shard_map/ppermute | solution.py:23
  13.6 1.5 %collective-permute-start.6 = (f32[16,512]{1,0:T(8,128)S(1)}, f32[16,512]{1,0:T(8,128)S(1)}, u32[]{:S(2)}, u32[]{:S(2)}) collective-permute-start(f32[16,512]{1,0:T(8,128)S(1)} %select_maximum_fusion), channel_id=1, source_target_pairs={{0,16},{8,24},{16,0},{24,8},{1,17},{9,25},{17,1},{25,9},{2,18},{10... | collective-permute-start | bytes 98312 | tf_op jit(solution)/shard_map/ppermute | solution.py:23
  15.2 0.6 %collective-permute-start.8 = (f32[136,512]{1,0:T(8,128)S(1)}, f32[136,512]{1,0:T(8,128)S(1)}, u32[]{:S(2)}, u32[]{:S(2)}) collective-permute-start(f32[136,512]{1,0:T(8,128)S(1)} %slice_bitcast_fusion), channel_id=1, source_target_pairs={{0,16},{8,24},{16,0},{24,8},{1,17},{9,25},{17,1},{25,9},{2,18},{10... | collective-permute-start | bytes 835592 | tf_op jit(solution)/shard_map/ppermute | solution.py:23
  15.8 0.6 %collective-permute-start.7 = (f32[120,512]{1,0:T(8,128)S(1)}, f32[120,512]{1,0:T(8,128)S(1)}, u32[]{:S(2)}, u32[]{:S(2)}) collective-permute-start(f32[120,512]{1,0:T(8,128)S(1)} %slice_bitcast_fusion.1), channel_id=1, source_target_pairs={{0,8},{8,0},{16,24},{24,16},{1,9},{9,1},{17,25},{25,17},{2,10},{10... | collective-permute-start | bytes 737288 | tf_op jit(solution)/shard_map/ppermute | solution.py:23
  16.4 1.4 %shard_map.52 = (f32[272,640]{1,0:T(8,128)S(1)}, f32[2,272,640]{2,1,0:T(8,128)S(1)}, f32[272,640]{1,0:T(8,128)S(1)}, f32[1,256,512]{2,1,0:T(8,128)}, f32[1,256,512]{2,1,0:T(8,128)}) custom-call(f32[256,512]{1,0:T(8,128)S(1)} %copy-done, f32[256,512]{1,0:T(8,128)S(1)} %copy-done.1, f32[3,8,640]{2,1,0:T(8,128)S(1)} %get-tuple-element.22.before, ...), custom_call_target="tpu_custom_call" | custom-call | flops 11141120 | bytes 16711680 | tf_op jit(solution)/shard_map/pallas_call | solution.py:432
  17.9 0.0 collective-permute-done.6.strip
  17.9 1.5 %collective-permute-start.9 = (f32[16,512]{1,0:T(8,128)S(1)}, f32[16,512]{1,0:T(8,128)S(1)}, u32[]{:S(2)}, u32[]{:S(2)}) collective-permute-start(f32[16,512]{1,0:T(8,128)S(1)} %collective-permute-done.6.strip), channel_id=1, source_target_pairs={{0,8},{8,0},{16,24},{24,16},{1,9},{9,1},{17,25},{25,17},{2,10},{10... | collective-permute-start | bytes 98312 | tf_op jit(solution)/shard_map/ppermute | solution.py:23
  19.4 0.1 broadcast_in_dim.3.odd_in
  19.5 1.4 %shard_map.53 = (f32[2,272,640]{2,1,0:T(8,128)S(1)}, f32[2,272,640]{2,1,0:T(8,128)S(1)}, f32[272,640]{1,0:T(8,128)S(1)}) custom-call(f32[272,640]{1,0:T(8,128)S(1)} %get-tuple-element.23.kap, f32[2,272,640]{2,1,0:T(8,128)S(1)} %get-tuple-element.24.even_in, ...), custom_call_target="tpu_custom_call", output_to_operand_aliasing={{0}: (1, {}), {1}: (2, {}), {2}: (3, {})} | custom-call | flops 1197670400 | bytes 1796505600 | tf_op jit(solution)/shard_map/pallas_call | solution.py:446
  20.9 1.9 %shard_map.54 = (f32[2,272,640]{2,1,0:T(8,128)S(1)}, f32[2,272,640]{2,1,0:T(8,128)S(1)}, f32[272,640]{1,0:T(8,128)S(1)}) custom-call(f32[272,640]{1,0:T(8,128)S(1)} %get-tuple-element.23.kap, f32[2,272,640]{2,1,0:T(8,128)S(1)} %get-tuple-element.26.even_in, ...), custom_call_target="tpu_custom_call", output_to_operand_aliasing={{0}: (1, {}), {1}: (2, {}), {2}: (3, {})} | custom-call | flops 1197670400 | bytes 1796505600 | tf_op jit(solution)/shard_map/pallas_call | solution.py:446
  22.8 0.9 %collective-permute-done.9.strip = f32[16,512]{1,0:T(8,128)S(1)} collective-permute-done((f32[16,512]{1,0:T(8,128)S(1)}, f32[16,512]{1,0:T(8,128)S(1)}, u32[]{:S(2)}, u32[]{:S(2)}) %collective-permute-start.9) | collective-permute-done | bytes 32800 | tf_op jit(solution)/shard_map/ppermute | solution.py:23
  23.7 2.5 %shard_map.55 = (f32[1,256,512]{2,1,0:T(8,128)}, f32[1,256,512]{2,1,0:T(8,128)}) custom-call(f32[272,640]{1,0:T(8,128)S(1)} %get-tuple-element.23.kap, f32[2,272,640]{2,1,0:T(8,128)S(1)} %get-tuple-element.29.even, f32[2,272,640]{2,1,0:T(8,128)S(1)} %get-tuple-element.30.odd, ...), custom_call_target="tpu_custom_call", output_to_operand_aliasing={{0}: (7, {}), {1}: (8, {})} | custom-call | flops 22282240 | bytes 33423360 | tf_op jit(solution)/shard_map/pallas_call | solution.py:451
  (25 shorter events, 0.2 us)
Async XLA Ops:
  0.6 2.2 %copy-start.1 = (f32[256,512]{1,0:T(8,128)S(1)}, f32[256,512]{1,0:T(8,128)}, u32[]{:S(2)}) copy-start(f32[256,512]{1,0:T(8,128)} %initial.1) | copy-start | bytes 1572868
  0.6 2.2 %copy-start = (f32[256,512]{1,0:T(8,128)S(1)}, f32[256,512]{1,0:T(8,128)}, u32[]{:S(2)}) copy-start(f32[256,512]{1,0:T(8,128)} %kappa.1) | copy-start | bytes 1572868
  0.6 14.5 %collective-permute-start.3 = (f32[1,256,512]{2,1,0:T(8,128)}, f32[1,256,512]{2,1,0:T(8,128)S(1)}, u32[]{:S(2)}, u32[]{:S(2)}) collective-permute-start(f32[1,256,512]{2,1,0:T(8,128)} %param.5), channel_id=1, source_target_pairs={{0,8},{8,0},{16,24},{24,16},{1,9},{9,1},{17,25},{25,17},{2,10},{10... | collective-permute-start | bytes 1572872 | tf_op jit(solution)/shard_map/ppermute | solution.py:23
  1.2 14.5 %collective-permute-start.5 = (f32[1,256,512]{2,1,0:T(8,128)}, f32[1,256,512]{2,1,0:T(8,128)S(1)}, u32[]{:S(2)}, u32[]{:S(2)}) collective-permute-start(f32[1,256,512]{2,1,0:T(8,128)} %param.5), channel_id=1, source_target_pairs={{0,16},{8,24},{16,0},{24,8},{1,17},{9,25},{17,1},{25,9},{2,18},{10... | collective-permute-start | bytes 1572872 | tf_op jit(solution)/shard_map/ppermute | solution.py:23
  3.1 5.7 %collective-permute-start = (f32[3,8,256]{2,1,0:T(8,128)S(1)}, f32[3,8,256]{2,1,0:T(8,128)S(1)}, u32[]{:S(2)}, u32[]{:S(2)}) collective-permute-start(f32[3,8,256]{2,1,0:T(8,128)S(1)} %get-tuple-element.47), channel_id=1, source_target_pairs={{0,0},{1,2},{2,1},{3,3},{4,4},{5,6},{6,5},{7,7},{8,8},{9,10},{10,9... | collective-permute-start | bytes 73736 | tf_op jit(solution)/shard_map/ppermute | solution.py:35
  6.6 3.9 %collective-permute-start.1 = (f32[3,8,256]{2,1,0:T(8,128)S(1)}, f32[3,8,256]{2,1,0:T(8,128)S(1)}, u32[]{:S(2)}, u32[]{:S(2)}) collective-permute-start(f32[3,8,256]{2,1,0:T(8,128)S(1)} %get-tuple-element.46), channel_id=1, source_target_pairs={{0,1},{1,0},{2,3},{3,2},{4,5},{5,4},{6,7},{7,6},{8,9},{9,8},{10,11... | collective-permute-start | bytes 73736 | tf_op jit(solution)/shard_map/ppermute | solution.py:35
  10.7 1.3 %collective-permute-start.2 = (f32[3,8,640]{2,1,0:T(8,128)S(1)}, f32[3,8,640]{2,1,0:T(8,128)S(1)}, u32[]{:S(2)}, u32[]{:S(2)}) collective-permute-start(f32[3,8,640]{2,1,0:T(8,128)S(1)} %broadcast_select_fusion.3), channel_id=1, source_target_pairs={{0,4},{4,0},{1,5},{5,1},{2,6},{6,2},{3,7},{7,3},{8,12},{12,8},{9,1... | collective-permute-start | bytes 184328 | tf_op jit(solution)/shard_map/ppermute | solution.py:35
  12.1 7.3 %collective-permute-start.4 = (f32[16,512]{1,0:T(8,128)S(1)}, f32[16,512]{1,0:T(8,128)S(1)}, u32[]{:S(2)}, u32[]{:S(2)}) collective-permute-start(f32[16,512]{1,0:T(8,128)S(1)} %select_maximum_fusion), channel_id=1, source_target_pairs={{0,8},{8,0},{16,24},{24,16},{1,9},{9,1},{17,25},{25,17},{2,10},{10... | collective-permute-start | bytes 98312 | tf_op jit(solution)/shard_map/ppermute | solution.py:23
  13.6 4.2 %collective-permute-start.6 = (f32[16,512]{1,0:T(8,128)S(1)}, f32[16,512]{1,0:T(8,128)S(1)}, u32[]{:S(2)}, u32[]{:S(2)}) collective-permute-start(f32[16,512]{1,0:T(8,128)S(1)} %select_maximum_fusion), channel_id=1, source_target_pairs={{0,16},{8,24},{16,0},{24,8},{1,17},{9,25},{17,1},{25,9},{2,18},{10... | collective-permute-start | bytes 98312 | tf_op jit(solution)/shard_map/ppermute | solution.py:23
  15.2 8.5 %collective-permute-start.8 = (f32[136,512]{1,0:T(8,128)S(1)}, f32[136,512]{1,0:T(8,128)S(1)}, u32[]{:S(2)}, u32[]{:S(2)}) collective-permute-start(f32[136,512]{1,0:T(8,128)S(1)} %slice_bitcast_fusion), channel_id=1, source_target_pairs={{0,16},{8,24},{16,0},{24,8},{1,17},{9,25},{17,1},{25,9},{2,18},{10... | collective-permute-start | bytes 835592 | tf_op jit(solution)/shard_map/ppermute | solution.py:23
  15.8 7.9 %collective-permute-start.7 = (f32[120,512]{1,0:T(8,128)S(1)}, f32[120,512]{1,0:T(8,128)S(1)}, u32[]{:S(2)}, u32[]{:S(2)}) collective-permute-start(f32[120,512]{1,0:T(8,128)S(1)} %slice_bitcast_fusion.1), channel_id=1, source_target_pairs={{0,8},{8,0},{16,24},{24,16},{1,9},{9,1},{17,25},{25,17},{2,10},{10... | collective-permute-start | bytes 737288 | tf_op jit(solution)/shard_map/ppermute | solution.py:23
  17.9 5.9 %collective-permute-start.9 = (f32[16,512]{1,0:T(8,128)S(1)}, f32[16,512]{1,0:T(8,128)S(1)}, u32[]{:S(2)}, u32[]{:S(2)}) collective-permute-start(f32[16,512]{1,0:T(8,128)S(1)} %collective-permute-done.6.strip), channel_id=1, source_target_pairs={{0,8},{8,0},{16,24},{24,16},{1,9},{9,1},{17,25},{25,17},{2,10},{10... | collective-permute-start | bytes 98312 | tf_op jit(solution)/shard_map/ppermute | solution.py:23

commit v8 on v7

--- a/solution.py
+++ b/solution.py
@@ -10,7 +10,7 @@
 LANES = 128
 SUBLANES = 8
 BLOCK = 16
-CHUNKS = 4
+CHUNKS = (1 / 2, 7 / 8, 1)
 SHARE = 15 / 32
 MIDDLE = 430
 
@@ -279,19 +279,19 @@
         def _():
             absorb(grid, kap, point, here, load, even, odd, tail, work[:5])
 
-    chunk = round_up(-(-rows // sems.shape[1]), BLOCK)
+    stops = sorted({min(rows, round_up(int(rows * part), BLOCK)) for part in CHUNKS})
 
     def sent(which, i):
         src, dst = ((c_rows, c_out), (f_rows, f_out))[which]
-        part = slice(i * chunk, min((i + 1) * chunk, rows))
+        part = slice(stops[i - 1] if i else 0, stops[i])
         return pltpu.make_async_copy(src.at[part], dst.at[0, part], sems.at[which, i])
 
     def put(which, at, value):
         stop = min(at.stop, rows)
         if at.start < stop:
             (c_rows, f_rows)[which][at.start : stop, :] = value[: stop - at.start, :width]
-            if stop % chunk == 0 or stop == rows:
-                sent(which, (stop - 1) // chunk).start()
+            if stop in stops:
+                sent(which, stops.index(stop)).start()
 
     @pl.when(here == 1)
     def _():
@@ -377,7 +377,7 @@
     @pl.when(here > 0)
     def _():
         for which in (0, 1):
-            for i in range(-(-rows // chunk)):
+            for i in range(len(stops)):
                 sent(which, i).wait()
 
 
@@ -450,7 +450,7 @@
     own = [sides, sides, ext] if count != 4 else [(1, *grid.ext), (1, *grid.ext), ext]
     c_new, f_new = call(
         functools.partial(last_kernel, grid, count), [c_guess.shape] * 2, work + [padded] + [(rows, width)] * 2 + own, 8,
-        semaphores=(2, CHUNKS), input_output_aliases={7: 0, 8: 1},
+        semaphores=(2, len(CHUNKS)), input_output_aliases={7: 0, 8: 1},
         in_specs=[inside] * 7 + [outside] * 2, out_specs=[outside] * 2,
     )(kap, even, odd, tail, first, second, strips[last], c_new, f_new)
     return c_new, f_new

time: 26.5 us -> 26.5 us (level)
  no operation moved by 1% of the time
where the time goes in v8:
time: 26.5 us; the launch traced here: 26.2 us
  starting transfers between devices  10.5 us (40%)
  Pallas kernels  7.64 us (29%)
  waiting for transfers between devices  5.17 us (20%)
  local copies, waits for them, and re-layouts  1.9 us (7%)
  between operations  0.87 us (3%)
    ppermute x7, starting transfers between devices, swap(): lax.ppermute(x, axis, [(i, i ^ bits) for i in range(lax.axis_size(axis))])  6.91 us
    ppermute x3, waiting for transfers between devices, neighbours(): lax.ppermute(send, axis, sorted(pairs.items()))  4.24 us
    ppermute x3, starting transfers between devices, neighbours(): lax.ppermute(send, axis, sorted(pairs.items()))  3.63 us
    pallas_call x2, Pallas kernels, on_device(): call(functools.partial(middle_kernel, grid, d), [sides, sides, ext], work...  3.31 us
    pallas_call x1, Pallas kernels, on_device(): call(functools.partial(last_kernel, grid, count), [c_guess.shape] * 2, wo...  2.48 us
    pallas_call x1, Pallas kernels, on_device(): call(functools.partial(start_kernel, grid), [ext, sides, ext] + [c_guess....  1.43 us
    squeeze x1, local copies, waits for them, and re-layouts, on_device(): c_guess[0, :, :LANES]  0.99 us
    ppermute x7, waiting for transfers between devices, swap(): lax.ppermute(x, axis, [(i, i ^ bits) for i in range(lax.axis_size(axis))])  0.93 us
  transfers between devices with their start and end apart: 10, of which 4 were waited for; matrix products, arithmetic and copies ran while one was open for 8% of the time, Pallas kernels for 20%

profile of v8, /device:TPU:14, one launch (start us, length us, event | category | flops | bytes accessed | tf_op | source)
XLA Modules:
  0.0 26.2 jit_solution(16179479742731644424)
XLA Ops:
  0.6 0.6 %collective-permute-start.3 = (f32[1,256,512]{2,1,0:T(8,128)}, f32[1,256,512]{2,1,0:T(8,128)S(1)}, u32[]{:S(2)}, u32[]{:S(2)}) collective-permute-start(f32[1,256,512]{2,1,0:T(8,128)} %param.5), channel_id=1, source_target_pairs={{0,8},{8,0},{16,24},{24,16},{1,9},{9,1},{17,25},{25,17},{2,10},{10... | collective-permute-start | bytes 1572872 | tf_op jit(solution)/shard_map/ppermute | solution.py:23
  1.2 0.5 %collective-permute-start.5 = (f32[1,256,512]{2,1,0:T(8,128)}, f32[1,256,512]{2,1,0:T(8,128)S(1)}, u32[]{:S(2)}, u32[]{:S(2)}) collective-permute-start(f32[1,256,512]{2,1,0:T(8,128)} %param.5), channel_id=1, source_target_pairs={{0,16},{8,24},{16,0},{24,8},{1,17},{9,25},{17,1},{25,9},{2,18},{10... | collective-permute-start | bytes 1572872 | tf_op jit(solution)/shard_map/ppermute | solution.py:23
  1.8 1.0 %slice_bitcast_fusion.3 = (f32[256,128]{1,0:T(8,128)S(1)}, f32[256,128]{1,0:T(8,128)S(1)}) fusion(f32[1,256,512]{2,1,0:T(8,128)} %param.5), kind=kLoop, calls=%fused_computation.4 | loop fusion | bytes 524288 | tf_op jit(solution)/shard_map/squeeze | solution.py:405
  2.8 0.3 shard_map.50
  3.1 3.5 %collective-permute-start = (f32[3,8,256]{2,1,0:T(8,128)S(1)}, f32[3,8,256]{2,1,0:T(8,128)S(1)}, u32[]{:S(2)}, u32[]{:S(2)}) collective-permute-start(f32[3,8,256]{2,1,0:T(8,128)S(1)} %get-tuple-element.47), channel_id=1, source_target_pairs={{0,0},{1,2},{2,1},{3,3},{4,4},{5,6},{6,5},{7,7},{8,8},{9,10},{10,9... | collective-permute-start | bytes 73736 | tf_op jit(solution)/shard_map/ppermute | solution.py:35
  6.6 0.1 collective-permute-start.1
  6.7 0.7 %slice_bitcast_fusion.4 = (f32[8,512]{1,0:T(8,128)S(1)}, f32[8,512]{1,0:T(8,128)S(1)}) fusion(f32[1,256,512]{2,1,0:T(8,128)} %param.5), kind=kLoop, calls=%fused_computation.16 | loop fusion | bytes 65536 | tf_op jit(solution)/shard_map/slice | solution.py:411
  7.5 1.4 %collective-permute-done = f32[3,8,256]{2,1,0:T(8,128)S(1)} collective-permute-done((f32[3,8,256]{2,1,0:T(8,128)S(1)}, f32[3,8,256]{2,1,0:T(8,128)S(1)}, u32[]{:S(2)}, u32[]{:S(2)}) %collective-permute-start) | collective-permute-done | bytes 24608 | tf_op jit(solution)/shard_map/ppermute | solution.py:35
  8.8 1.7 %collective-permute-done.1 = f32[3,8,256]{2,1,0:T(8,128)S(1)} collective-permute-done((f32[3,8,256]{2,1,0:T(8,128)S(1)}, f32[3,8,256]{2,1,0:T(8,128)S(1)}, u32[]{:S(2)}, u32[]{:S(2)}) %collective-permute-start.1) | collective-permute-done | bytes 24608 | tf_op jit(solution)/shard_map/ppermute | solution.py:35
  10.5 0.2 shard_map.51
  10.7 0.1 collective-permute-start.2
  10.8 1.2 %collective-permute-done.2 = f32[3,8,640]{2,1,0:T(8,128)S(1)} collective-permute-done((f32[3,8,640]{2,1,0:T(8,128)S(1)}, f32[3,8,640]{2,1,0:T(8,128)S(1)}, u32[]{:S(2)}, u32[]{:S(2)}) %collective-permute-start.2) | collective-permute-done | bytes 61472 | tf_op jit(solution)/shard_map/ppermute | solution.py:35
  12.1 1.6 %collective-permute-start.4 = (f32[16,512]{1,0:T(8,128)S(1)}, f32[16,512]{1,0:T(8,128)S(1)}, u32[]{:S(2)}, u32[]{:S(2)}) collective-permute-start(f32[16,512]{1,0:T(8,128)S(1)} %select_maximum_fusion), channel_id=1, source_target_pairs={{0,8},{8,0},{16,24},{24,16},{1,9},{9,1},{17,25},{25,17},{2,10},{10... | collective-permute-start | bytes 98312 | tf_op jit(solution)/shard_map/ppermute | solution.py:23
  13.6 1.5 %collective-permute-start.6 = (f32[16,512]{1,0:T(8,128)S(1)}, f32[16,512]{1,0:T(8,128)S(1)}, u32[]{:S(2)}, u32[]{:S(2)}) collective-permute-start(f32[16,512]{1,0:T(8,128)S(1)} %select_maximum_fusion), channel_id=1, source_target_pairs={{0,16},{8,24},{16,0},{24,8},{1,17},{9,25},{17,1},{25,9},{2,18},{10... | collective-permute-start | bytes 98312 | tf_op jit(solution)/shard_map/ppermute | solution.py:23
  15.2 0.6 %collective-permute-start.8 = (f32[136,512]{1,0:T(8,128)S(1)}, f32[136,512]{1,0:T(8,128)S(1)}, u32[]{:S(2)}, u32[]{:S(2)}) collective-permute-start(f32[136,512]{1,0:T(8,128)S(1)} %slice_bitcast_fusion), channel_id=1, source_target_pairs={{0,16},{8,24},{16,0},{24,8},{1,17},{9,25},{17,1},{25,9},{2,18},{10... | collective-permute-start | bytes 835592 | tf_op jit(solution)/shard_map/ppermute | solution.py:23
  15.8 0.6 %collective-permute-start.7 = (f32[120,512]{1,0:T(8,128)S(1)}, f32[120,512]{1,0:T(8,128)S(1)}, u32[]{:S(2)}, u32[]{:S(2)}) collective-permute-start(f32[120,512]{1,0:T(8,128)S(1)} %slice_bitcast_fusion.1), channel_id=1, source_target_pairs={{0,8},{8,0},{16,24},{24,16},{1,9},{9,1},{17,25},{25,17},{2,10},{10... | collective-permute-start | bytes 737288 | tf_op jit(solution)/shard_map/ppermute | solution.py:23
  16.4 1.4 %shard_map.52 = (f32[272,640]{1,0:T(8,128)S(1)}, f32[2,272,640]{2,1,0:T(8,128)S(1)}, f32[272,640]{1,0:T(8,128)S(1)}, f32[1,256,512]{2,1,0:T(8,128)}, f32[1,256,512]{2,1,0:T(8,128)}) custom-call(f32[256,512]{1,0:T(8,128)S(1)} %copy-done, f32[256,512]{1,0:T(8,128)S(1)} %copy-done.1, f32[3,8,640]{2,1,0:T(8,128)S(1)} %get-tuple-element.22.before, ...), custom_call_target="tpu_custom_call" | custom-call | flops 11141120 | bytes 16711680 | tf_op jit(solution)/shard_map/pallas_call | solution.py:432
  17.9 0.0 collective-permute-done.6.strip
  17.9 1.5 %collective-permute-start.9 = (f32[16,512]{1,0:T(8,128)S(1)}, f32[16,512]{1,0:T(8,128)S(1)}, u32[]{:S(2)}, u32[]{:S(2)}) collective-permute-start(f32[16,512]{1,0:T(8,128)S(1)} %collective-permute-done.6.strip), channel_id=1, source_target_pairs={{0,8},{8,0},{16,24},{24,16},{1,9},{9,1},{17,25},{25,17},{2,10},{10... | collective-permute-start | bytes 98312 | tf_op jit(solution)/shard_map/ppermute | solution.py:23
  19.4 0.1 broadcast_in_dim.3.odd_in
  19.5 1.4 %shard_map.53 = (f32[2,272,640]{2,1,0:T(8,128)S(1)}, f32[2,272,640]{2,1,0:T(8,128)S(1)}, f32[272,640]{1,0:T(8,128)S(1)}) custom-call(f32[272,640]{1,0:T(8,128)S(1)} %get-tuple-element.23.kap, f32[2,272,640]{2,1,0:T(8,128)S(1)} %get-tuple-element.24.even_in, ...), custom_call_target="tpu_custom_call", output_to_operand_aliasing={{0}: (1, {}), {1}: (2, {}), {2}: (3, {})} | custom-call | flops 1197670400 | bytes 1796505600 | tf_op jit(solution)/shard_map/pallas_call | solution.py:446
  20.9 1.9 %shard_map.54 = (f32[2,272,640]{2,1,0:T(8,128)S(1)}, f32[2,272,640]{2,1,0:T(8,128)S(1)}, f32[272,640]{1,0:T(8,128)S(1)}) custom-call(f32[272,640]{1,0:T(8,128)S(1)} %get-tuple-element.23.kap, f32[2,272,640]{2,1,0:T(8,128)S(1)} %get-tuple-element.26.even_in, ...), custom_call_target="tpu_custom_call", output_to_operand_aliasing={{0}: (1, {}), {1}: (2, {}), {2}: (3, {})} | custom-call | flops 1197670400 | bytes 1796505600 | tf_op jit(solution)/shard_map/pallas_call | solution.py:446
  22.8 0.9 %collective-permute-done.9.strip = f32[16,512]{1,0:T(8,128)S(1)} collective-permute-done((f32[16,512]{1,0:T(8,128)S(1)}, f32[16,512]{1,0:T(8,128)S(1)}, u32[]{:S(2)}, u32[]{:S(2)}) %collective-permute-start.9) | collective-permute-done | bytes 32800 | tf_op jit(solution)/shard_map/ppermute | solution.py:23
  23.7 2.5 %shard_map.55 = (f32[1,256,512]{2,1,0:T(8,128)}, f32[1,256,512]{2,1,0:T(8,128)}) custom-call(f32[272,640]{1,0:T(8,128)S(1)} %get-tuple-element.23.kap, f32[2,272,640]{2,1,0:T(8,128)S(1)} %get-tuple-element.29.even, f32[2,272,640]{2,1,0:T(8,128)S(1)} %get-tuple-element.30.odd, ...), custom_call_target="tpu_custom_call", output_to_operand_aliasing={{0}: (7, {}), {1}: (8, {})} | custom-call | flops 22282240 | bytes 33423360 | tf_op jit(solution)/shard_map/pallas_call | solution.py:451
  (25 shorter events, 0.2 us)
Async XLA Ops:
  0.6 2.2 %copy-start.1 = (f32[256,512]{1,0:T(8,128)S(1)}, f32[256,512]{1,0:T(8,128)}, u32[]{:S(2)}) copy-start(f32[256,512]{1,0:T(8,128)} %initial.1) | copy-start | bytes 1572868
  0.6 2.2 %copy-start = (f32[256,512]{1,0:T(8,128)S(1)}, f32[256,512]{1,0:T(8,128)}, u32[]{:S(2)}) copy-start(f32[256,512]{1,0:T(8,128)} %kappa.1) | copy-start | bytes 1572868
  0.6 14.5 %collective-permute-start.3 = (f32[1,256,512]{2,1,0:T(8,128)}, f32[1,256,512]{2,1,0:T(8,128)S(1)}, u32[]{:S(2)}, u32[]{:S(2)}) collective-permute-start(f32[1,256,512]{2,1,0:T(8,128)} %param.5), channel_id=1, source_target_pairs={{0,8},{8,0},{16,24},{24,16},{1,9},{9,1},{17,25},{25,17},{2,10},{10... | collective-permute-start | bytes 1572872 | tf_op jit(solution)/shard_map/ppermute | solution.py:23
  1.2 14.5 %collective-permute-start.5 = (f32[1,256,512]{2,1,0:T(8,128)}, f32[1,256,512]{2,1,0:T(8,128)S(1)}, u32[]{:S(2)}, u32[]{:S(2)}) collective-permute-start(f32[1,256,512]{2,1,0:T(8,128)} %param.5), channel_id=1, source_target_pairs={{0,16},{8,24},{16,0},{24,8},{1,17},{9,25},{17,1},{25,9},{2,18},{10... | collective-permute-start | bytes 1572872 | tf_op jit(solution)/shard_map/ppermute | solution.py:23
  3.1 5.7 %collective-permute-start = (f32[3,8,256]{2,1,0:T(8,128)S(1)}, f32[3,8,256]{2,1,0:T(8,128)S(1)}, u32[]{:S(2)}, u32[]{:S(2)}) collective-permute-start(f32[3,8,256]{2,1,0:T(8,128)S(1)} %get-tuple-element.47), channel_id=1, source_target_pairs={{0,0},{1,2},{2,1},{3,3},{4,4},{5,6},{6,5},{7,7},{8,8},{9,10},{10,9... | collective-permute-start | bytes 73736 | tf_op jit(solution)/shard_map/ppermute | solution.py:35
  6.6 3.9 %collective-permute-start.1 = (f32[3,8,256]{2,1,0:T(8,128)S(1)}, f32[3,8,256]{2,1,0:T(8,128)S(1)}, u32[]{:S(2)}, u32[]{:S(2)}) collective-permute-start(f32[3,8,256]{2,1,0:T(8,128)S(1)} %get-tuple-element.46), channel_id=1, source_target_pairs={{0,1},{1,0},{2,3},{3,2},{4,5},{5,4},{6,7},{7,6},{8,9},{9,8},{10,11... | collective-permute-start | bytes 73736 | tf_op jit(solution)/shard_map/ppermute | solution.py:35
  10.7 1.3 %collective-permute-start.2 = (f32[3,8,640]{2,1,0:T(8,128)S(1)}, f32[3,8,640]{2,1,0:T(8,128)S(1)}, u32[]{:S(2)}, u32[]{:S(2)}) collective-permute-start(f32[3,8,640]{2,1,0:T(8,128)S(1)} %broadcast_select_fusion.3), channel_id=1, source_target_pairs={{0,4},{4,0},{1,5},{5,1},{2,6},{6,2},{3,7},{7,3},{8,12},{12,8},{9,1... | collective-permute-start | bytes 184328 | tf_op jit(solution)/shard_map/ppermute | solution.py:35
  12.1 7.3 %collective-permute-start.4 = (f32[16,512]{1,0:T(8,128)S(1)}, f32[16,512]{1,0:T(8,128)S(1)}, u32[]{:S(2)}, u32[]{:S(2)}) collective-permute-start(f32[16,512]{1,0:T(8,128)S(1)} %select_maximum_fusion), channel_id=1, source_target_pairs={{0,8},{8,0},{16,24},{24,16},{1,9},{9,1},{17,25},{25,17},{2,10},{10... | collective-permute-start | bytes 98312 | tf_op jit(solution)/shard_map/ppermute | solution.py:23
  13.6 4.2 %collective-permute-start.6 = (f32[16,512]{1,0:T(8,128)S(1)}, f32[16,512]{1,0:T(8,128)S(1)}, u32[]{:S(2)}, u32[]{:S(2)}) collective-permute-start(f32[16,512]{1,0:T(8,128)S(1)} %select_maximum_fusion), channel_id=1, source_target_pairs={{0,16},{8,24},{16,0},{24,8},{1,17},{9,25},{17,1},{25,9},{2,18},{10... | collective-permute-start | bytes 98312 | tf_op jit(solution)/shard_map/ppermute | solution.py:23
  15.2 8.5 %collective-permute-start.8 = (f32[136,512]{1,0:T(8,128)S(1)}, f32[136,512]{1,0:T(8,128)S(1)}, u32[]{:S(2)}, u32[]{:S(2)}) collective-permute-start(f32[136,512]{1,0:T(8,128)S(1)} %slice_bitcast_fusion), channel_id=1, source_target_pairs={{0,16},{8,24},{16,0},{24,8},{1,17},{9,25},{17,1},{25,9},{2,18},{10... | collective-permute-start | bytes 835592 | tf_op jit(solution)/shard_map/ppermute | solution.py:23
  15.8 7.9 %collective-permute-start.7 = (f32[120,512]{1,0:T(8,128)S(1)}, f32[120,512]{1,0:T(8,128)S(1)}, u32[]{:S(2)}, u32[]{:S(2)}) collective-permute-start(f32[120,512]{1,0:T(8,128)S(1)} %slice_bitcast_fusion.1), channel_id=1, source_target_pairs={{0,8},{8,0},{16,24},{24,16},{1,9},{9,1},{17,25},{25,17},{2,10},{10... | collective-permute-start | bytes 737288 | tf_op jit(solution)/shard_map/ppermute | solution.py:23
  17.9 5.9 %collective-permute-start.9 = (f32[16,512]{1,0:T(8,128)S(1)}, f32[16,512]{1,0:T(8,128)S(1)}, u32[]{:S(2)}, u32[]{:S(2)}) collective-permute-start(f32[16,512]{1,0:T(8,128)S(1)} %collective-permute-done.6.strip), channel_id=1, source_target_pairs={{0,8},{8,0},{16,24},{24,16},{1,9},{9,1},{17,25},{25,17},{2,10},{10... | collective-permute-start | bytes 98312 | tf_op jit(solution)/shard_map/ppermute | solution.py:23
